TPU v7x, 32 devices: a whole 2x2x4 slice. The times are simulated.
32 devices in a mesh: pipe: 2 (over y), patch: 8 (over z, x), hour: 2 (over core).
Axes of the slice: x: 2, y: 2, z: 4, core: 2. Of those that a mesh axis runs over, the one named last changes fastest.
Arguments:
- inputs: bfloat16 [2, 128, 32, 512], P(None, 'patch', 'hour'), may hold values from -6 to 6
- visibility: int32 [2, 2], replicated, may hold values from 0 to 1, all different within a row
- norm_gains: float32 [2, 3, 512], P('pipe'), may hold values from 0.1 to 1.9
- scales: float32 [2, 2, 8], P('pipe'), may hold values from 2 to 12
- mixer_in: bfloat16 [2, 2, 512, 1536], P('pipe'), may hold values from -0.25 to 0.25
- mixer_out: bfloat16 [2, 2, 512, 512], P('pipe'), may hold values from -0.25 to 0.25
- expand_weight: bfloat16 [2, 512, 2048], P('pipe'), may hold values from -0.25 to 0.25
- reduce_weight: bfloat16 [2, 2048, 512], P('pipe'), may hold values from -0.125 to 0.125
Outputs:
- outputs: bfloat16 [2, 128, 32, 512], P(None, 'patch', 'hour')
Inputs may be any that keep to these rules, and one draw needn't show every extreme that they name: `visibility`: row b lists 2 different key blocks of 64 patches for query block b; every block is listed in some row.
All inputs are finite; a program needn't handle non-finite values.
Results may differ from a plain program's by a relative error of at most 0.023.
Values may be sent and summed in bfloat16 or wider, within the bound.
No kernel may reach another device: no remote copies, remote signals or barrier semaphores. Data moves between devices by JAX's collectives and lax.ppermute only.
A program may use at most 64 MiB of HBM per device.

v0:
```python
import functools

import jax
import jax.numpy as jnp
from jax import lax
from jax.experimental import pallas as pl
from jax.experimental.pallas import tpu as pltpu
from jax.sharding import PartitionSpec as P

HEADS = 8
HEAD_DIM = 64
PB = 64
LOG2E = 1.4426950408889634


def row_norm(x, gain):
    factor = lax.rsqrt(jnp.mean(x * x, axis=-1, keepdims=True) + 1e-05)
    return (x * factor * gain).astype(jnp.bfloat16)


def matmul(a, b):
    return jnp.dot(a, b, preferred_element_type=jnp.float32)


def same_head():
    rows = lax.broadcasted_iota(jnp.int32, (256, 256), 0) // HEAD_DIM
    cols = lax.broadcasted_iota(jnp.int32, (256, 256), 1) // HEAD_DIM
    return jnp.where(rows == cols, 1.0, 0.0).astype(jnp.bfloat16)


def head_factor(values, group):
    squares = (values * values).astype(jnp.bfloat16)
    halves = [
        matmul(squares[:, start : start + 256], group) for start in range(0, values.shape[1], 256)
    ]
    sums = jnp.concatenate(halves, axis=1)
    return lax.rsqrt(sums * (1.0 / HEAD_DIM) + 1e-06)


def regrouped(x, groups, inner):
    outer = x.shape[0] // (groups * inner)
    starts = [(o * groups + g) * inner for g in range(groups) for o in range(outer)]
    return jnp.concatenate([x[start : start + inner] for start in starts], axis=0)


def attention_update(xs, groups, gain, scale_of, w_in, w_out, mask):
    rows, width = xs[0].shape
    normed = row_norm(xs[0], gain)
    seen = jnp.concatenate([normed] + [row_norm(t, gain) for t in xs[1:]], axis=0)
    same = same_head()
    head = lax.broadcasted_iota(jnp.int32, (1, width), 1) // HEAD_DIM
    scale = jnp.zeros((1, width), jnp.float32)
    for n in range(HEADS):
        scale = jnp.where(head == n, scale_of(n) * (LOG2E / HEAD_DIM), scale)
    q = matmul(normed, w_in[:, :width])
    k = matmul(seen, w_in[:, width : 2 * width])
    v = matmul(seen, w_in[:, 2 * width :]).astype(jnp.bfloat16)
    q = (q * head_factor(q, same) * scale).astype(jnp.bfloat16)
    k = (k * head_factor(k, same)).astype(jnp.bfloat16)
    pair = 2 * HEAD_DIM
    size = rows // groups
    first = lax.broadcasted_iota(jnp.int32, (1, pair), 1) < HEAD_DIM
    low = jnp.where(first, 1.0, 0.0).astype(jnp.bfloat16)
    high = jnp.where(first, 0.0, 1.0).astype(jnp.bfloat16)
    keys = size * len(xs)
    low_all = jnp.broadcast_to(low, (keys, pair))
    high_all = jnp.broadcast_to(high, (keys, pair))
    done = []
    for g in range(groups):
        q_g = q[g * size : (g + 1) * size]
        spans = [slice(i * rows + g * size, i * rows + (g + 1) * size) for i in range(len(xs))]
        k_g = jnp.concatenate([k[span] for span in spans], axis=0)
        v_g = jnp.concatenate([v[span] for span in spans], axis=0)
        parts = []
        for start in range(0, width, pair):
            q2, k2, v2 = (t[:, start : start + pair] for t in (q_g, k_g, v_g))
            powers = []
            for side in (low, high):
                scores = lax.dot_general(
                    q2 * side, k2, (((1,), (1,)), ((), ())), preferred_element_type=jnp.float32
                )
                powers.append(jnp.exp2(scores).astype(jnp.bfloat16) * mask)
            powers = jnp.concatenate(powers, axis=1)
            upper = jnp.concatenate([v2 * low, low_all], axis=1)
            lower = jnp.concatenate([v2 * high, high_all], axis=1)
            sums = matmul(powers, jnp.concatenate([upper, lower], axis=0))
            parts.append((sums[:, :pair] / sums[:, pair:]).astype(jnp.bfloat16))
        done.append(jnp.concatenate(parts, axis=1))
    return matmul(jnp.concatenate(done, axis=0), w_out[...])


def rounded(x):
    return x.astype(jnp.bfloat16).astype(jnp.float32)


def digits(shape, dimension, *bases):
    index = lax.broadcasted_iota(jnp.int32, shape, dimension)
    out = []
    for base in bases:
        out.append(index % base)
        index = index // base
    return out + [index]


def far_first(slow):
    return sorted(range(slow), key=lambda k: (k < slow // 2, k))


def pieces_of(sequence):
    half = len(sequence) // 2
    return [sequence[:half], sequence[half:]]


def row_sets(refs, slow, pieces):
    sets = []
    for start in range(0, len(refs), len(pieces)):
        found = {}
        for ref, piece in zip(refs[start : start + len(pieces)], pieces):
            size = ref.shape[0] // len(piece)
            for place, k in enumerate(piece):
                found[k] = ref[place * size : (place + 1) * size, :]
        sets.append([found[k] for k in range(slow)])
    return sets


def at_work(place_ref, step, micro):
    number = step - place_ref[0]
    return jnp.logical_and(number >= 0, number < micro)


def order_kernel(sizes, place_ref, order_ref):
    slow, _, patches, hl = sizes
    shape = order_ref.shape
    patch, late, offset = digits(shape, 0, patches, hl)
    source = lax.broadcasted_iota(jnp.int32, shape, 1)
    wanted = (patch * slow + (offset ^ place_ref[1])) * hl + late
    order_ref[...] = jnp.where(wanted == source, 1.0, 0.0).astype(jnp.bfloat16)


def time_kernel(sizes, step, micro, place_ref, *refs):
    shards, peers, patches, hl = sizes
    given = peers if step < micro else 0
    order_refs, refs = refs[: min(given, 1)], refs[min(given, 1) :]
    pieces = pieces_of(far_first(shards))
    came = peers * len(pieces) if step > 0 else 0
    input_refs, refs = refs[:given], refs[given:]
    came_refs, refs = refs[:came], refs[came:]
    (gain_ref, scale_ref, w_in_ref, w_out_ref), refs = refs[:4], refs[4:]
    y_refs, refs = refs[:shards], refs[shards:]
    x_ref = refs[0]
    rows = x_ref.shape[0] // peers

    @pl.when(at_work(place_ref, step, micro))
    def _():
        if given:

            @pl.when(place_ref[0] == 0)
            def _():
                order = order_refs[0][...]
                for j, ref in enumerate(input_refs):
                    moved = matmul(order, ref[step]).astype(jnp.bfloat16)
                    x_ref[j * rows : (j + 1) * rows, :] = moved

        if came:

            @pl.when(place_ref[0] != 0)
            def _():
                for j, blocks in enumerate(row_sets(came_refs, shards, pieces)):
                    x_ref[j * rows : (j + 1) * rows, :] = jnp.concatenate(blocks, axis=0)

        inner = min(patches, 8)
        groups = patches // inner
        xs = [
            regrouped(x_ref[j * rows : (j + 1) * rows, :].astype(jnp.float32), groups, inner)
            for j in range(peers)
        ]
        shape = (rows // groups, rows // groups * peers)
        mine = digits(shape, 0, inner)[0]
        theirs = digits(shape, 1, inner)[0]
        mask = jnp.where(mine == theirs, 1.0, 0.0).astype(jnp.bfloat16)
        update = attention_update(
            xs,
            groups,
            gain_ref[0, 0:1, :],
            lambda n: scale_ref[0, 0, n],
            w_in_ref.at[0, 0],
            w_out_ref.at[0, 0],
            mask,
        )
        y = regrouped(xs[0] + update, rows // (groups * inner), inner).astype(jnp.bfloat16)
        size = rows // shards
        for k in range(shards):
            y_refs[k][...] = y[k * size : (k + 1) * size]


def patch_kernel(sizes, step, micro, outs, place_ref, seen_ref, *refs):
    slow, _, patches, hl = sizes
    count = len(refs) - 6 - outs
    pieces = pieces_of([0] + [k for k in far_first(slow) if k])
    fast = count // len(pieces)
    x_refs, (gain_ref, scale_ref, w_in_ref, w_out_ref, up_ref, down_ref), y_refs = (
        refs[:count],
        refs[count : count + 6],
        refs[count + 6 :],
    )

    @pl.when(at_work(place_ref, step, micro))
    def _():
        xs = [
            jnp.concatenate(blocks, axis=0).astype(jnp.float32)
            for blocks in row_sets(x_refs, slow, pieces)
        ]
        rows = xs[0].shape[0]
        groups = 2 if hl % 2 == 0 else 1
        inner = hl // groups * patches
        xs = [regrouped(x, groups, inner) for x in xs]
        x = xs[0]
        shape = (rows // groups, rows // groups * fast)

        def block_and_hour(dimension):
            patch, late, offset, other = digits(shape, dimension, patches, hl // groups, slow)
            shard = (offset ^ place_ref[1]) * fast + (other ^ place_ref[2])
            return (shard * patches + patch) // PB, late

        query_block, query_hour = block_and_hour(0)
        key_block, key_hour = block_and_hour(1)
        seen = None
        for kv in range(seen_ref.shape[1]):
            chosen = jnp.full(shape, seen_ref[0, kv], jnp.int32)
            for b in range(1, seen_ref.shape[0]):
                chosen = jnp.where(query_block == b, seen_ref[b, kv], chosen)
            hit = jnp.where(chosen == key_block, 1.0, 0.0)
            seen = hit if seen is None else jnp.maximum(seen, hit)
        mask = jnp.where(query_hour == key_hour, seen, 0.0).astype(jnp.bfloat16)
        update = attention_update(
            xs,
            groups,
            gain_ref[0, 1:2, :],
            lambda n: scale_ref[0, 1, n],
            w_in_ref.at[0, 1],
            w_out_ref.at[0, 1],
            mask,
        )
        x = rounded(x + update)
        normed = row_norm(x, gain_ref[0, 2:3, :])
        total = x
        chunk = 512
        for start in range(0, up_ref.shape[2], chunk):
            u = matmul(normed, up_ref[0, :, start : start + chunk])
            bent = jnp.tanh(u * (0.7978845608028654 + 0.035677408136300125 * (u * u)))
            hidden = (0.5 * u * (1.0 + bent)).astype(jnp.bfloat16)
            total = total + matmul(hidden, down_ref[0, start : start + chunk, :])
        y = regrouped(total, slow, inner).astype(jnp.bfloat16)
        size = rows // outs
        for k in range(outs):
            y_refs[k][...] = y[k * size : (k + 1) * size]


def pick_kernel(slow, last, place_ref, *refs):
    x_refs, y_refs = refs[:-slow], refs[-slow:]
    size = x_refs[0].shape[0] // slow
    for hops, x_ref in enumerate(x_refs):

        @pl.when(place_ref[0] == (last + hops) % len(x_refs))
        def _():
            for k, y_ref in enumerate(y_refs):
                y_ref[...] = x_ref[k * size : (k + 1) * size, :]


def write_rows(sizes, place_ref, x, y_ref):
    slow, _, patches, hl = sizes
    rows = slow * patches * hl
    late, shard, patch = digits((rows, rows), 0, hl, slow)
    source = lax.broadcasted_iota(jnp.int32, (rows, rows), 1)
    wanted = ((shard ^ place_ref[1]) * hl + late) * patches + patch
    order = jnp.where(wanted == source, 1.0, 0.0).astype(jnp.bfloat16)
    y_ref[...] = matmul(order, x).astype(jnp.bfloat16)


def early_kernel(sizes, pipes, place_ref, *refs):
    x_refs, y_ref = refs[:pipes], refs[-1]
    for stage, x_ref in enumerate(x_refs):

        @pl.when(place_ref[0] == stage)
        def _():
            write_rows(sizes, place_ref, x_ref[...], y_ref)


def final_kernel(sizes, place_ref, *refs):
    x_refs, y_ref = refs[: sizes[0]], refs[-1]
    write_rows(sizes, place_ref, jnp.concatenate([ref[...] for ref in x_refs], axis=0), y_ref)


VMEM = pl.BlockSpec(memory_space=pltpu.VMEM)
SMEM = pl.BlockSpec(memory_space=pltpu.SMEM)
PARAMS = pltpu.CompilerParams(vmem_limit_bytes=32 << 20)
COST = pl.CostEstimate(flops=5 << 30, bytes_accessed=1 << 20, transcendentals=1 << 20)


def blocks_of(count, rows, width):
    return [jax.ShapeDtypeStruct((rows // count, width), jnp.bfloat16)] * count


def call_order(sizes, place, rows):
    return pl.pallas_call(
        functools.partial(order_kernel, sizes),
        out_shape=jax.ShapeDtypeStruct((rows, rows), jnp.bfloat16),
        in_specs=[SMEM],
        out_specs=VMEM,
        compiler_params=PARAMS,
        cost_estimate=COST,
        name="input_order",
    )(place)


def call_time(sizes, step, micro, shape, place, order, given, came, gains, scales, w_in, w_out):
    rows, width = shape
    xs = ([order] if given else []) + list(given) + list(came)
    return pl.pallas_call(
        functools.partial(time_kernel, sizes, step, micro),
        out_shape=blocks_of(sizes[0], rows, width),
        in_specs=[SMEM] + [VMEM] * len(xs) + [VMEM, SMEM, VMEM, VMEM],
        out_specs=[VMEM] * sizes[0],
        scratch_shapes=[pltpu.VMEM((rows * sizes[1], width), jnp.bfloat16)],
        compiler_params=PARAMS,
        cost_estimate=COST,
        name="time_attention",
    )(place, *xs, gains, scales, w_in, w_out)


def call_patch(sizes, step, micro, shape, outs, place, seen, xs, gains, scales, w_in, w_out, w_up, w_down):
    rows, width = shape
    return pl.pallas_call(
        functools.partial(patch_kernel, sizes, step, micro, outs),
        out_shape=blocks_of(outs, rows, width),
        in_specs=[SMEM, SMEM] + [VMEM] * len(xs) + [VMEM, SMEM] + [VMEM] * 4,
        out_specs=[VMEM] * outs,
        compiler_params=PARAMS,
        cost_estimate=COST,
        name="patch_attention_and_ffn",
    )(place, seen, *xs, gains, scales, w_in, w_out, w_up, w_down)


def call_pick(slow, last, place, xs):
    rows, width = xs[0].shape
    return pl.pallas_call(
        functools.partial(pick_kernel, slow, last),
        out_shape=blocks_of(slow, rows, width),
        in_specs=[SMEM] + [VMEM] * len(xs),
        out_specs=[VMEM] * slow,
        compiler_params=PARAMS,
        name="pick",
    )(place, *xs)


def call_write(kernel, sizes, place, shape, number, xs, out):
    given = [] if out is None else [out]
    return pl.pallas_call(
        kernel,
        out_shape=jax.ShapeDtypeStruct(shape, jnp.bfloat16),
        grid=(1,),
        in_specs=[SMEM] + [VMEM] * len(xs) + [pl.BlockSpec(memory_space=pl.ANY)] * len(given),
        out_specs=pl.BlockSpec((None,) + shape[1:], lambda i: (number, 0, 0)),
        input_output_aliases={1 + len(xs): 0} if given else {},
        compiler_params=PARAMS,
        name="final_order",
    )(place, *xs, *given)


def flipped(x, axis, k):
    return lax.ppermute(x, axis, [(s, s ^ k) for s in range(lax.axis_size(axis))])


def handed_on(x, k):
    pipes, shards = lax.axis_size("pipe"), lax.axis_size("patch")
    pairs = [
        (stage * shards + s, (stage + 1) % pipes * shards + (s ^ k))
        for stage in range(pipes)
        for s in range(shards)
    ]
    return lax.ppermute(x, ("pipe", "patch"), pairs)


def local(inputs, seen, gains, scales, w_in, w_out, w_up, w_down):
    shards = lax.axis_size("patch")
    peers = lax.axis_size("hour")
    pipes = lax.axis_size("pipe")
    micro, patches, hours, width = inputs.shape
    rows = patches * hours
    fast = 2
    slow = shards // fast
    sizes = (slow, peers, patches, hours // slow)
    last = pipes - 1
    shard = lax.axis_index("patch")
    place = jnp.stack([lax.axis_index("pipe"), lax.div(shard, fast), lax.rem(shard, fast)])
    far = far_first(slow)
    order = call_order(sizes, place, rows)

    def gathered(blocks, axis, count, sequence):
        own = [jnp.concatenate([blocks[k] for k in piece]) for piece in pieces_of(sequence)]
        out = list(own)
        for j in range(1, count):
            out += [flipped(piece, axis, j) for piece in own]
        return out

    def along_slow(blocks, send, first):
        got = {k: send(blocks[k], k * fast) for k in far if k >= first}
        return [got.get(k, blocks[k]) for k in range(slow)]

    def in_stage(x, k):
        return flipped(x, "patch", k)

    def onward(x):
        return lax.ppermute(x, "pipe", [(s, (s + 1) % pipes) for s in range(pipes)])

    x = inputs.reshape(micro, rows, width)
    given = [x] + [flipped(x, "hour", j) for j in range(1, peers)]
    came = []
    out = None
    back = []
    for step in range(micro + pipes - 1):
        now = given if step < micro else []
        mixed = call_time(sizes, step, micro, x.shape[1:], place, order, now, came, gains, scales, w_in, w_out)
        own = along_slow(mixed, in_stage, 1)
        spread = gathered(own, "patch", fast, [0] + [k for k in far if k])
        if back:
            spread, back = lax.optimization_barrier((spread, back))
            write = functools.partial(early_kernel, sizes, pipes)
            out = call_write(write, sizes, place, x.shape, step - pipes, back, out)
        at_end = step == micro + pipes - 2
        outs = 1 if at_end else slow
        done = call_patch(
            sizes,
            step,
            micro,
            x.shape[1:],
            outs,
            place,
            seen,
            spread,
            gains,
            scales,
            w_in,
            w_out,
            w_up,
            w_down,
        )
        if not at_end:
            arrived = along_slow(done, handed_on, 0)
            came = gathered(arrived, "hour", peers, far)
            if step >= last:
                back = [jnp.concatenate(arrived)]
                for _ in range(1, pipes):
                    back.append(onward(back[-1]))
    done = list(done)
    for _ in range(1, pipes):
        done.append(onward(done[-1]))
    blocks = along_slow(call_pick(slow, last, place, done), in_stage, 1)
    write = functools.partial(final_kernel, sizes)
    out = call_write(write, sizes, place, x.shape, micro - 1, blocks, out)
    return out.reshape(inputs.shape)


def solution(mesh):
    placed = (
        P(None, "patch", "hour", None),
        P(),
        P("pipe", None, None),
        P("pipe", None, None),
        P("pipe", None, None, None),
        P("pipe", None, None, None),
        P("pipe", None, None),
        P("pipe", None, None),
    )
    return jax.shard_map(
        local, mesh=mesh, in_specs=placed, out_specs=P(None, "patch", "hour", None), check_vma=False
    )
```

profile of v0, /device:TPU:0, one launch (start us, length us, event | category | flops | bytes accessed | tf_op | source)
XLA Modules:
  0.0 121.4 jit_solution(11367991420002988040)
XLA Ops:
  3.5 2.9 %time_attention.3 = (bf16[64,512]{1,0:T(8,128)(2,1)S(1)}, bf16[64,512]{1,0:T(8,128)(2,1)S(1)}, bf16[64,512]{1,0:T(8,128)(2,1)S(1)}, bf16[64,512]{1,0:T(8,128)(2,1)S(1)}) custom-call(s32[3]{0:T(128)S(1)} %pad_add_fusion.place_ref, bf16[256,256]{1,0:T(8,128)(2,1)S(1)} %input_order.1.refs_0_, bf16[2,256,512]{2,1,0:T(8,128)(2,1)S(1)} %bitcast.6, ...), custom_call_target="tpu_custom_call" | custom-call | flops 5368709120 | bytes 1048576 | tf_op jit(solution)/shard_map/time_attention/pallas_call | solution.py:319
  6.4 3.6 %collective-permute-start.1 = (bf16[64,512]{1,0:T(8,128)(2,1)S(1)}, bf16[64,512]{1,0:T(8,128)(2,1)S(1)}, u32[]{:S(2)}, u32[]{:S(2)}) collective-permute-start(bf16[64,512]{1,0:T(8,128)(2,1)S(1)} %get-tuple-element.36), channel_id=1, source_target_pairs={{0,8},{2,10},{4,12},{6,14},{8,0},{10,2},{12,4},{14,6},{1,9},{3,11}... | collective-permute-start | bytes 196616 | tf_op jit(solution)/shard_map/ppermute | solution.py:371
  11.6 5.1 %collective-permute-done.2 = bf16[64,512]{1,0:T(8,128)(2,1)S(1)} collective-permute-done((bf16[64,512]{1,0:T(8,128)(2,1)S(1)}, bf16[64,512]{1,0:T(8,128)(2,1)S(1)}, u32[]{:S(2)}, u32[]{:S(2)}) %collective-permute-start.2) | collective-permute-done | bytes 65568 | tf_op jit(solution)/shard_map/ppermute | solution.py:371
  17.0 1.5 %collective-permute-start.5 = (bf16[128,512]{1,0:T(8,128)(2,1)S(1)}, bf16[128,512]{1,0:T(8,128)(2,1)S(1)}, u32[]{:S(2)}, u32[]{:S(2)}) collective-permute-start(bf16[128,512]{1,0:T(8,128)(2,1)S(1)} %constant_dynamic-update-slice_fusion.2.refs_1_), channel_id=1, source_target_pairs={{0,2},{2,0},{4,6},{6,4},{8,10},{10,8},{12,14},{14,12},{1,3},{3,1},... | collective-permute-start | bytes 393224 | tf_op jit(solution)/shard_map/ppermute | solution.py:371
  19.1 4.0 %collective-permute-done.5.refs_3_ = bf16[128,512]{1,0:T(8,128)(2,1)S(1)} collective-permute-done((bf16[128,512]{1,0:T(8,128)(2,1)S(1)}, bf16[128,512]{1,0:T(8,128)(2,1)S(1)}, u32[]{:S(2)}, u32[]{:S(2)}) %collective-permute-start.5) | collective-permute-done | bytes 131104 | tf_op jit(solution)/shard_map/ppermute | solution.py:371
  24.5 4.6 %patch_attention_and_ffn.3 = (bf16[64,512]{1,0:T(8,128)(2,1)S(1)}, bf16[64,512]{1,0:T(8,128)(2,1)S(1)}, bf16[64,512]{1,0:T(8,128)(2,1)S(1)}, bf16[64,512]{1,0:T(8,128)(2,1)S(1)}) custom-call(s32[3]{0:T(128)S(1)} %pad_add_fusion.place_ref, s32[2,2]{1,0:T(2,128)S(1)} %copy-done.5, bf16[128,512]{1,0:T(8,128)(2,1)S(1)} %constant_dynamic-update-slice_fusion.refs_0_, ...), custom_call_target="tpu_custom_call" | custom-call | flops 5368709120 | bytes 1048576 | tf_op jit(solution)/shard_map/patch_attention_and_ffn/pallas_call | solution.py:333
  29.2 5.0 %collective-permute-start.6 = (bf16[64,512]{1,0:T(8,128)(2,1)S(1)}, bf16[64,512]{1,0:T(8,128)(2,1)S(1)}, u32[]{:S(2)}, u32[]{:S(2)}) collective-permute-start(bf16[64,512]{1,0:T(8,128)(2,1)S(1)} %get-tuple-element.39), channel_id=1, source_target_pairs={{0,24},{2,26},{4,28},{6,30},{8,16},{10,18},{12,20},{14,22},{16,8},... | collective-permute-start | bytes 196616 | tf_op jit(solution)/shard_map/ppermute | solution.py:381
  35.1 4.7 %collective-permute-done.9 = bf16[64,512]{1,0:T(8,128)(2,1)S(1)} collective-permute-done((bf16[64,512]{1,0:T(8,128)(2,1)S(1)}, bf16[64,512]{1,0:T(8,128)(2,1)S(1)}, u32[]{:S(2)}, u32[]{:S(2)}) %collective-permute-start.9) | collective-permute-done | bytes 65568 | tf_op jit(solution)/shard_map/ppermute | solution.py:381
  42.6 2.9 %time_attention.4 = (bf16[64,512]{1,0:T(8,128)(2,1)S(1)}, bf16[64,512]{1,0:T(8,128)(2,1)S(1)}, bf16[64,512]{1,0:T(8,128)(2,1)S(1)}, bf16[64,512]{1,0:T(8,128)(2,1)S(1)}) custom-call(s32[3]{0:T(128)S(1)} %pad_add_fusion.place_ref, bf16[256,256]{1,0:T(8,128)(2,1)S(1)} %input_order.1.refs_0_, bf16[2,256,512]{2,1,0:T(8,128)(2,1)S(1)} %bitcast.7, ...), custom_call_target="tpu_custom_call" | custom-call | flops 5368709120 | bytes 1048576 | tf_op jit(solution)/shard_map/time_attention/pallas_call | solution.py:319
  45.5 1.6 %collective-permute-start.12 = (bf16[64,512]{1,0:T(8,128)(2,1)S(1)}, bf16[64,512]{1,0:T(8,128)(2,1)S(1)}, u32[]{:S(2)}, u32[]{:S(2)}) collective-permute-start(bf16[64,512]{1,0:T(8,128)(2,1)S(1)} %get-tuple-element.44), channel_id=1, source_target_pairs={{0,8},{2,10},{4,12},{6,14},{8,0},{10,2},{12,4},{14,6},{1,9},{3,11}... | collective-permute-start | bytes 196616 | tf_op jit(solution)/shard_map/ppermute | solution.py:371
  49.0 4.6 %collective-permute-done.13 = bf16[64,512]{1,0:T(8,128)(2,1)S(1)} collective-permute-done((bf16[64,512]{1,0:T(8,128)(2,1)S(1)}, bf16[64,512]{1,0:T(8,128)(2,1)S(1)}, u32[]{:S(2)}, u32[]{:S(2)}) %collective-permute-start.13) | collective-permute-done | bytes 65568 | tf_op jit(solution)/shard_map/ppermute | solution.py:371
  54.4 1.5 %collective-permute-start.16 = (bf16[128,512]{1,0:T(8,128)(2,1)S(1)}, bf16[128,512]{1,0:T(8,128)(2,1)S(1)}, u32[]{:S(2)}, u32[]{:S(2)}) collective-permute-start(bf16[128,512]{1,0:T(8,128)(2,1)S(1)} %constant_dynamic-update-slice_fusion.10.refs_1_), channel_id=1, source_target_pairs={{0,2},{2,0},{4,6},{6,4},{8,10},{10,8},{12,14},{14,12},{1,3},{3,1},... | collective-permute-start | bytes 393224 | tf_op jit(solution)/shard_map/ppermute | solution.py:371
  56.5 4.3 %collective-permute-done.16.refs_3_ = bf16[128,512]{1,0:T(8,128)(2,1)S(1)} collective-permute-done((bf16[128,512]{1,0:T(8,128)(2,1)S(1)}, bf16[128,512]{1,0:T(8,128)(2,1)S(1)}, u32[]{:S(2)}, u32[]{:S(2)}) %collective-permute-start.16) | collective-permute-done | bytes 131104 | tf_op jit(solution)/shard_map/ppermute | solution.py:371
  60.8 1.8 %collective-permute-done.15.refs_2_ = bf16[128,512]{1,0:T(8,128)(2,1)S(1)} collective-permute-done((bf16[128,512]{1,0:T(8,128)(2,1)S(1)}, bf16[128,512]{1,0:T(8,128)(2,1)S(1)}, u32[]{:S(2)}, u32[]{:S(2)}) %collective-permute-start.15) | collective-permute-done | bytes 131104 | tf_op jit(solution)/shard_map/ppermute | solution.py:371
  62.6 4.8 %patch_attention_and_ffn.4 = (bf16[64,512]{1,0:T(8,128)(2,1)S(1)}, bf16[64,512]{1,0:T(8,128)(2,1)S(1)}, bf16[64,512]{1,0:T(8,128)(2,1)S(1)}, bf16[64,512]{1,0:T(8,128)(2,1)S(1)}) custom-call(s32[3]{0:T(128)S(1)} %pad_add_fusion.place_ref, s32[2,2]{1,0:T(2,128)S(1)} %copy-done.5, bf16[128,512]{1,0:T(8,128)(2,1)S(1)} %constant_dynamic-update-slice_fusion.8.refs_0_, ...), custom_call_target="tpu_custom_call" | custom-call | flops 5368709120 | bytes 1048576 | tf_op jit(solution)/shard_map/patch_attention_and_ffn/pallas_call | solution.py:333
  67.4 1.5 %collective-permute-start.19 = (bf16[64,512]{1,0:T(8,128)(2,1)S(1)}, bf16[64,512]{1,0:T(8,128)(2,1)S(1)}, u32[]{:S(2)}, u32[]{:S(2)}) collective-permute-start(bf16[64,512]{1,0:T(8,128)(2,1)S(1)} %get-tuple-element.49), channel_id=1, source_target_pairs={{0,16},{2,18},{4,20},{6,22},{8,24},{10,26},{12,28},{14,30},{16,0},... | collective-permute-start | bytes 196616 | tf_op jit(solution)/shard_map/ppermute | solution.py:381
  70.2 2.6 %collective-permute-start.18 = (bf16[64,512]{1,0:T(8,128)(2,1)S(1)}, bf16[64,512]{1,0:T(8,128)(2,1)S(1)}, u32[]{:S(2)}, u32[]{:S(2)}) collective-permute-start(bf16[64,512]{1,0:T(8,128)(2,1)S(1)} %get-tuple-element.48), channel_id=1, source_target_pairs={{0,28},{2,30},{4,24},{6,26},{8,20},{10,22},{12,16},{14,18},{16,12}... | collective-permute-start | bytes 196616 | tf_op jit(solution)/shard_map/ppermute | solution.py:381
  73.4 4.6 %collective-permute-done.20 = bf16[64,512]{1,0:T(8,128)(2,1)S(1)} collective-permute-done((bf16[64,512]{1,0:T(8,128)(2,1)S(1)}, bf16[64,512]{1,0:T(8,128)(2,1)S(1)}, u32[]{:S(2)}, u32[]{:S(2)}) %collective-permute-start.20) | collective-permute-done | bytes 65568 | tf_op jit(solution)/shard_map/ppermute | solution.py:381
  78.6 1.5 %collective-permute-start.28 = (bf16[256,512]{1,0:T(8,128)(2,1)S(1)}, bf16[256,512]{1,0:T(8,128)(2,1)S(1)}, u32[]{:S(2)}, u32[]{:S(2)}) collective-permute-start(bf16[256,512]{1,0:T(8,128)(2,1)S(1)} %get-tuple-element.63.refs_0_), channel_id=1, source_target_pairs={{0,16},{16,0},{1,17},{17,1},{2,18},{18,2},{3,19},{19,3},{4,20},{20... | collective-permute-start | bytes 786440 | tf_op jit(solution)/shard_map/ppermute | solution.py:414
  81.9 1.7 %collective-permute-start.24 = (bf16[64,512]{1,0:T(8,128)(2,1)S(1)}, bf16[64,512]{1,0:T(8,128)(2,1)S(1)}, u32[]{:S(2)}, u32[]{:S(2)}) collective-permute-start(bf16[64,512]{1,0:T(8,128)(2,1)S(1)} %get-tuple-element.53), channel_id=1, source_target_pairs={{0,12},{2,14},{4,8},{6,10},{8,4},{10,6},{12,0},{14,2},{1,13},{3,15... | collective-permute-start | bytes 196616 | tf_op jit(solution)/shard_map/ppermute | solution.py:371
  84.2 4.2 %collective-permute-done.24 = bf16[64,512]{1,0:T(8,128)(2,1)S(1)} collective-permute-done((bf16[64,512]{1,0:T(8,128)(2,1)S(1)}, bf16[64,512]{1,0:T(8,128)(2,1)S(1)}, u32[]{:S(2)}, u32[]{:S(2)}) %collective-permute-start.24) | collective-permute-done | bytes 65568 | tf_op jit(solution)/shard_map/ppermute | solution.py:371
  89.7 1.5 %collective-permute-start.27 = (bf16[128,512]{1,0:T(8,128)(2,1)S(1)}, bf16[128,512]{1,0:T(8,128)(2,1)S(1)}, u32[]{:S(2)}, u32[]{:S(2)}) collective-permute-start(bf16[128,512]{1,0:T(8,128)(2,1)S(1)} %constant_dynamic-update-slice_fusion.18.refs_1_), channel_id=1, source_target_pairs={{0,2},{2,0},{4,6},{6,4},{8,10},{10,8},{12,14},{14,12},{1,3},{3,1},... | collective-permute-start | bytes 393224 | tf_op jit(solution)/shard_map/ppermute | solution.py:371
  91.8 4.3 %collective-permute-done.27.refs_3_ = bf16[128,512]{1,0:T(8,128)(2,1)S(1)} collective-permute-done((bf16[128,512]{1,0:T(8,128)(2,1)S(1)}, bf16[128,512]{1,0:T(8,128)(2,1)S(1)}, u32[]{:S(2)}, u32[]{:S(2)}) %collective-permute-start.27) | collective-permute-done | bytes 131104 | tf_op jit(solution)/shard_map/ppermute | solution.py:371
  96.1 1.8 %collective-permute-done.26.refs_2_ = bf16[128,512]{1,0:T(8,128)(2,1)S(1)} collective-permute-done((bf16[128,512]{1,0:T(8,128)(2,1)S(1)}, bf16[128,512]{1,0:T(8,128)(2,1)S(1)}, u32[]{:S(2)}, u32[]{:S(2)}) %collective-permute-start.26) | collective-permute-done | bytes 131104 | tf_op jit(solution)/shard_map/ppermute | solution.py:371
  98.5 5.2 %collective-permute-start.29 = (bf16[256,512]{1,0:T(8,128)(2,1)S(1)}, bf16[256,512]{1,0:T(8,128)(2,1)S(1)}, u32[]{:S(2)}, u32[]{:S(2)}) collective-permute-start(bf16[256,512]{1,0:T(8,128)(2,1)S(1)} %patch_attention_and_ffn.5.refs_0_), channel_id=1, source_target_pairs={{0,16},{16,0},{1,17},{17,1},{2,18},{18,2},{3,19},{19,3},{4,20},{20... | collective-permute-start | bytes 786440 | tf_op jit(solution)/shard_map/ppermute | solution.py:414
  103.7 4.4 %collective-permute-done.29.refs_1_ = bf16[256,512]{1,0:T(8,128)(2,1)S(1)} collective-permute-done((bf16[256,512]{1,0:T(8,128)(2,1)S(1)}, bf16[256,512]{1,0:T(8,128)(2,1)S(1)}, u32[]{:S(2)}, u32[]{:S(2)}) %collective-permute-start.29) | collective-permute-done | bytes 262176 | tf_op jit(solution)/shard_map/ppermute | solution.py:414
  108.6 3.2 %collective-permute-start.30 = (bf16[64,512]{1,0:T(8,128)(2,1)S(1)}, bf16[64,512]{1,0:T(8,128)(2,1)S(1)}, u32[]{:S(2)}, u32[]{:S(2)}) collective-permute-start(bf16[64,512]{1,0:T(8,128)(2,1)S(1)} %get-tuple-element.60), channel_id=1, source_target_pairs={{0,4},{2,6},{4,0},{6,2},{8,12},{10,14},{12,8},{14,10},{1,5},{3,7},... | collective-permute-start | bytes 196616 | tf_op jit(solution)/shard_map/ppermute | solution.py:371
  111.8 2.1 %collective-permute-start.31 = (bf16[64,512]{1,0:T(8,128)(2,1)S(1)}, bf16[64,512]{1,0:T(8,128)(2,1)S(1)}, u32[]{:S(2)}, u32[]{:S(2)}) collective-permute-start(bf16[64,512]{1,0:T(8,128)(2,1)S(1)} %get-tuple-element.61), channel_id=1, source_target_pairs={{0,8},{2,10},{4,12},{6,14},{8,0},{10,2},{12,4},{14,6},{1,9},{3,11}... | collective-permute-start | bytes 196616 | tf_op jit(solution)/shard_map/ppermute | solution.py:371
  114.3 1.5 %final_order.2.refs_4_ = bf16[2,256,512]{2,1,0:T(8,128)(2,1)} custom-call(s32[3]{0:T(128)S(1)} %pad_add_fusion.place_ref, bf16[256,512]{1,0:T(8,128)(2,1)S(1)} %get-tuple-element.63.refs_0_, bf16[256,512]{1,0:T(8,128)(2,1)S(1)} %collective-permute-done.28.refs_1_), custom_call_target="tpu_custom_call" | custom-call | tf_op jit(solution)/shard_map/final_order/pallas_call | solution.py:358
  115.8 2.4 %collective-permute-done.31.refs_2_ = bf16[64,512]{1,0:T(8,128)(2,1)S(1)} collective-permute-done((bf16[64,512]{1,0:T(8,128)(2,1)S(1)}, bf16[64,512]{1,0:T(8,128)(2,1)S(1)}, u32[]{:S(2)}, u32[]{:S(2)}) %collective-permute-start.31) | collective-permute-done | bytes 65568 | tf_op jit(solution)/shard_map/ppermute | solution.py:371
  118.2 1.7 %collective-permute-done.32.refs_3_ = bf16[64,512]{1,0:T(8,128)(2,1)S(1)} collective-permute-done((bf16[64,512]{1,0:T(8,128)(2,1)S(1)}, bf16[64,512]{1,0:T(8,128)(2,1)S(1)}, u32[]{:S(2)}, u32[]{:S(2)}) %collective-permute-start.32) | collective-permute-done | bytes 65568 | tf_op jit(solution)/shard_map/ppermute | solution.py:371
  120.0 1.5 %final_order.3 = bf16[2,256,512]{2,1,0:T(8,128)(2,1)} custom-call(s32[3]{0:T(128)S(1)} %pad_add_fusion.place_ref, bf16[64,512]{1,0:T(8,128)(2,1)S(1)} %get-tuple-element.59.refs_0_, bf16[64,512]{1,0:T(8,128)(2,1)S(1)} %collective-permute-done.30.refs_1_, bf16[64,512]{1,0:T(8,128)(2,1)S(1)} %collective-permute-done.31.refs_2_, ...), custom_call_target="tpu_custom_call", output_to_operand_aliasing={{}: (5, {})} | custom-call | tf_op jit(solution)/shard_map/final_order/pallas_call | solution.py:358
  (80 shorter events, 22.7 us)
Async XLA Ops:
  0.0 2.2 %collective-permute-start = (bf16[2,256,512]{2,1,0:T(8,128)(2,1)}, bf16[2,256,512]{2,1,0:T(8,128)(2,1)S(1)}, u32[]{:S(2)}, u32[]{:S(2)}) collective-permute-start(bf16[2,256,512]{2,1,0:T(8,128)(2,1)} %bitcast.5), channel_id=1, source_target_pairs={{0,1},{1,0},{2,3},{3,2},{4,5},{5,4},{6,7},{7,6},{8,9},{9,8},{10,11... | collective-permute-start | bytes 1572872 | tf_op jit(solution)/shard_map/ppermute | solution.py:371
  6.4 12.2 %collective-permute-start.1 = (bf16[64,512]{1,0:T(8,128)(2,1)S(1)}, bf16[64,512]{1,0:T(8,128)(2,1)S(1)}, u32[]{:S(2)}, u32[]{:S(2)}) collective-permute-start(bf16[64,512]{1,0:T(8,128)(2,1)S(1)} %get-tuple-element.36), channel_id=1, source_target_pairs={{0,8},{2,10},{4,12},{6,14},{8,0},{10,2},{12,4},{14,6},{1,9},{3,11}... | collective-permute-start | bytes 196616 | tf_op jit(solution)/shard_map/ppermute | solution.py:371
  10.0 6.7 %collective-permute-start.2 = (bf16[64,512]{1,0:T(8,128)(2,1)S(1)}, bf16[64,512]{1,0:T(8,128)(2,1)S(1)}, u32[]{:S(2)}, u32[]{:S(2)}) collective-permute-start(bf16[64,512]{1,0:T(8,128)(2,1)S(1)} %get-tuple-element.37), channel_id=1, source_target_pairs={{0,12},{2,14},{4,8},{6,10},{8,4},{10,6},{12,0},{14,2},{1,13},{3,15... | collective-permute-start | bytes 196616 | tf_op jit(solution)/shard_map/ppermute | solution.py:371
  11.4 5.6 %collective-permute-start.3 = (bf16[64,512]{1,0:T(8,128)(2,1)S(1)}, bf16[64,512]{1,0:T(8,128)(2,1)S(1)}, u32[]{:S(2)}, u32[]{:S(2)}) collective-permute-start(bf16[64,512]{1,0:T(8,128)(2,1)S(1)} %get-tuple-element.38), channel_id=1, source_target_pairs={{0,4},{2,6},{4,0},{6,2},{8,12},{10,14},{12,8},{14,10},{1,5},{3,7},... | collective-permute-start | bytes 196616 | tf_op jit(solution)/shard_map/ppermute | solution.py:371
  17.0 6.1 %collective-permute-start.5 = (bf16[128,512]{1,0:T(8,128)(2,1)S(1)}, bf16[128,512]{1,0:T(8,128)(2,1)S(1)}, u32[]{:S(2)}, u32[]{:S(2)}) collective-permute-start(bf16[128,512]{1,0:T(8,128)(2,1)S(1)} %constant_dynamic-update-slice_fusion.2.refs_1_), channel_id=1, source_target_pairs={{0,2},{2,0},{4,6},{6,4},{8,10},{10,8},{12,14},{14,12},{1,3},{3,1},... | collective-permute-start | bytes 393224 | tf_op jit(solution)/shard_map/ppermute | solution.py:371
  18.6 5.9 %collective-permute-start.4 = (bf16[128,512]{1,0:T(8,128)(2,1)S(1)}, bf16[128,512]{1,0:T(8,128)(2,1)S(1)}, u32[]{:S(2)}, u32[]{:S(2)}) collective-permute-start(bf16[128,512]{1,0:T(8,128)(2,1)S(1)} %constant_dynamic-update-slice_fusion.refs_0_), channel_id=1, source_target_pairs={{0,2},{2,0},{4,6},{6,4},{8,10},{10,8},{12,14},{14,12},{1,3},{3,1},... | collective-permute-start | bytes 393224 | tf_op jit(solution)/shard_map/ppermute | solution.py:371
  29.1 5.9 %collective-permute-start.8 = (bf16[64,512]{1,0:T(8,128)(2,1)S(1)}, bf16[64,512]{1,0:T(8,128)(2,1)S(1)}, u32[]{:S(2)}, u32[]{:S(2)}) collective-permute-start(bf16[64,512]{1,0:T(8,128)(2,1)S(1)} %get-tuple-element.41), channel_id=1, source_target_pairs={{0,16},{2,18},{4,20},{6,22},{8,24},{10,26},{12,28},{14,30},{16,0},... | collective-permute-start | bytes 196616 | tf_op jit(solution)/shard_map/ppermute | solution.py:381
  29.2 10.5 %collective-permute-start.6 = (bf16[64,512]{1,0:T(8,128)(2,1)S(1)}, bf16[64,512]{1,0:T(8,128)(2,1)S(1)}, u32[]{:S(2)}, u32[]{:S(2)}) collective-permute-start(bf16[64,512]{1,0:T(8,128)(2,1)S(1)} %get-tuple-element.39), channel_id=1, source_target_pairs={{0,24},{2,26},{4,28},{6,30},{8,16},{10,18},{12,20},{14,22},{16,8},... | collective-permute-start | bytes 196616 | tf_op jit(solution)/shard_map/ppermute | solution.py:381
  34.3 7.0 %collective-permute-start.7 = (bf16[64,512]{1,0:T(8,128)(2,1)S(1)}, bf16[64,512]{1,0:T(8,128)(2,1)S(1)}, u32[]{:S(2)}, u32[]{:S(2)}) collective-permute-start(bf16[64,512]{1,0:T(8,128)(2,1)S(1)} %get-tuple-element.40), channel_id=1, source_target_pairs={{0,28},{2,30},{4,24},{6,26},{8,20},{10,22},{12,16},{14,18},{16,12}... | collective-permute-start | bytes 196616 | tf_op jit(solution)/shard_map/ppermute | solution.py:381
  34.6 5.2 %collective-permute-start.9 = (bf16[64,512]{1,0:T(8,128)(2,1)S(1)}, bf16[64,512]{1,0:T(8,128)(2,1)S(1)}, u32[]{:S(2)}, u32[]{:S(2)}) collective-permute-start(bf16[64,512]{1,0:T(8,128)(2,1)S(1)} %get-tuple-element.42), channel_id=1, source_target_pairs={{0,20},{2,22},{4,16},{6,18},{8,28},{10,30},{12,24},{14,26},{16,4},... | collective-permute-start | bytes 196616 | tf_op jit(solution)/shard_map/ppermute | solution.py:381
  39.8 1.5 %collective-permute-start.11 = (bf16[128,512]{1,0:T(8,128)(2,1)S(1)}, bf16[128,512]{1,0:T(8,128)(2,1)S(1)}, u32[]{:S(2)}, u32[]{:S(2)}) collective-permute-start(bf16[128,512]{1,0:T(8,128)(2,1)S(1)} %constant_dynamic-update-slice_fusion.6.refs_4_), channel_id=1, source_target_pairs={{0,1},{1,0},{2,3},{3,2},{4,5},{5,4},{6,7},{7,6},{8,9},{9,8},{10,11... | collective-permute-start | bytes 393224 | tf_op jit(solution)/shard_map/ppermute | solution.py:371
  45.5 10.5 %collective-permute-start.12 = (bf16[64,512]{1,0:T(8,128)(2,1)S(1)}, bf16[64,512]{1,0:T(8,128)(2,1)S(1)}, u32[]{:S(2)}, u32[]{:S(2)}) collective-permute-start(bf16[64,512]{1,0:T(8,128)(2,1)S(1)} %get-tuple-element.44), channel_id=1, source_target_pairs={{0,8},{2,10},{4,12},{6,14},{8,0},{10,2},{12,4},{14,6},{1,9},{3,11}... | collective-permute-start | bytes 196616 | tf_op jit(solution)/shard_map/ppermute | solution.py:371
  47.0 6.6 %collective-permute-start.13 = (bf16[64,512]{1,0:T(8,128)(2,1)S(1)}, bf16[64,512]{1,0:T(8,128)(2,1)S(1)}, u32[]{:S(2)}, u32[]{:S(2)}) collective-permute-start(bf16[64,512]{1,0:T(8,128)(2,1)S(1)} %get-tuple-element.45), channel_id=1, source_target_pairs={{0,12},{2,14},{4,8},{6,10},{8,4},{10,6},{12,0},{14,2},{1,13},{3,15... | collective-permute-start | bytes 196616 | tf_op jit(solution)/shard_map/ppermute | solution.py:371
  47.9 6.5 %collective-permute-start.14 = (bf16[64,512]{1,0:T(8,128)(2,1)S(1)}, bf16[64,512]{1,0:T(8,128)(2,1)S(1)}, u32[]{:S(2)}, u32[]{:S(2)}) collective-permute-start(bf16[64,512]{1,0:T(8,128)(2,1)S(1)} %get-tuple-element.46), channel_id=1, source_target_pairs={{0,4},{2,6},{4,0},{6,2},{8,12},{10,14},{12,8},{14,10},{1,5},{3,7},... | collective-permute-start | bytes 196616 | tf_op jit(solution)/shard_map/ppermute | solution.py:371
  54.4 6.4 %collective-permute-start.16 = (bf16[128,512]{1,0:T(8,128)(2,1)S(1)}, bf16[128,512]{1,0:T(8,128)(2,1)S(1)}, u32[]{:S(2)}, u32[]{:S(2)}) collective-permute-start(bf16[128,512]{1,0:T(8,128)(2,1)S(1)} %constant_dynamic-update-slice_fusion.10.refs_1_), channel_id=1, source_target_pairs={{0,2},{2,0},{4,6},{6,4},{8,10},{10,8},{12,14},{14,12},{1,3},{3,1},... | collective-permute-start | bytes 393224 | tf_op jit(solution)/shard_map/ppermute | solution.py:371
  55.9 6.7 %collective-permute-start.15 = (bf16[128,512]{1,0:T(8,128)(2,1)S(1)}, bf16[128,512]{1,0:T(8,128)(2,1)S(1)}, u32[]{:S(2)}, u32[]{:S(2)}) collective-permute-start(bf16[128,512]{1,0:T(8,128)(2,1)S(1)} %constant_dynamic-update-slice_fusion.8.refs_0_), channel_id=1, source_target_pairs={{0,2},{2,0},{4,6},{6,4},{8,10},{10,8},{12,14},{14,12},{1,3},{3,1},... | collective-permute-start | bytes 393224 | tf_op jit(solution)/shard_map/ppermute | solution.py:371
  67.4 5.9 %collective-permute-start.19 = (bf16[64,512]{1,0:T(8,128)(2,1)S(1)}, bf16[64,512]{1,0:T(8,128)(2,1)S(1)}, u32[]{:S(2)}, u32[]{:S(2)}) collective-permute-start(bf16[64,512]{1,0:T(8,128)(2,1)S(1)} %get-tuple-element.49), channel_id=1, source_target_pairs={{0,16},{2,18},{4,20},{6,22},{8,24},{10,26},{12,28},{14,30},{16,0},... | collective-permute-start | bytes 196616 | tf_op jit(solution)/shard_map/ppermute | solution.py:381
  68.9 9.1 %collective-permute-start.17 = (bf16[64,512]{1,0:T(8,128)(2,1)S(1)}, bf16[64,512]{1,0:T(8,128)(2,1)S(1)}, u32[]{:S(2)}, u32[]{:S(2)}) collective-permute-start(bf16[64,512]{1,0:T(8,128)(2,1)S(1)} %get-tuple-element.47), channel_id=1, source_target_pairs={{0,24},{2,26},{4,28},{6,30},{8,16},{10,18},{12,20},{14,22},{16,8},... | collective-permute-start | bytes 196616 | tf_op jit(solution)/shard_map/ppermute | solution.py:381
  70.2 7.8 %collective-permute-start.18 = (bf16[64,512]{1,0:T(8,128)(2,1)S(1)}, bf16[64,512]{1,0:T(8,128)(2,1)S(1)}, u32[]{:S(2)}, u32[]{:S(2)}) collective-permute-start(bf16[64,512]{1,0:T(8,128)(2,1)S(1)} %get-tuple-element.48), channel_id=1, source_target_pairs={{0,28},{2,30},{4,24},{6,26},{8,20},{10,22},{12,16},{14,18},{16,12}... | collective-permute-start | bytes 196616 | tf_op jit(solution)/shard_map/ppermute | solution.py:381
  72.8 5.2 %collective-permute-start.20 = (bf16[64,512]{1,0:T(8,128)(2,1)S(1)}, bf16[64,512]{1,0:T(8,128)(2,1)S(1)}, u32[]{:S(2)}, u32[]{:S(2)}) collective-permute-start(bf16[64,512]{1,0:T(8,128)(2,1)S(1)} %get-tuple-element.50), channel_id=1, source_target_pairs={{0,20},{2,22},{4,16},{6,18},{8,28},{10,30},{12,24},{14,26},{16,4},... | collective-permute-start | bytes 196616 | tf_op jit(solution)/shard_map/ppermute | solution.py:381
  78.1 2.1 %collective-permute-start.21 = (bf16[128,512]{1,0:T(8,128)(2,1)S(1)}, bf16[128,512]{1,0:T(8,128)(2,1)S(1)}, u32[]{:S(2)}, u32[]{:S(2)}) collective-permute-start(bf16[128,512]{1,0:T(8,128)(2,1)S(1)} %get-tuple-element.66.refs_0_), channel_id=1, source_target_pairs={{0,1},{1,0},{2,3},{3,2},{4,5},{5,4},{6,7},{7,6},{8,9},{9,8},{10,11... | collective-permute-start | bytes 393224 | tf_op jit(solution)/shard_map/ppermute | solution.py:371
  78.1 2.0 %collective-permute-start.22 = (bf16[128,512]{1,0:T(8,128)(2,1)S(1)}, bf16[128,512]{1,0:T(8,128)(2,1)S(1)}, u32[]{:S(2)}, u32[]{:S(2)}) collective-permute-start(bf16[128,512]{1,0:T(8,128)(2,1)S(1)} %get-tuple-element.70.refs_1_), channel_id=1, source_target_pairs={{0,1},{1,0},{2,3},{3,2},{4,5},{5,4},{6,7},{7,6},{8,9},{9,8},{10,11... | collective-permute-start | bytes 393224 | tf_op jit(solution)/shard_map/ppermute | solution.py:371
  78.6 13.2 %collective-permute-start.28 = (bf16[256,512]{1,0:T(8,128)(2,1)S(1)}, bf16[256,512]{1,0:T(8,128)(2,1)S(1)}, u32[]{:S(2)}, u32[]{:S(2)}) collective-permute-start(bf16[256,512]{1,0:T(8,128)(2,1)S(1)} %get-tuple-element.63.refs_0_), channel_id=1, source_target_pairs={{0,16},{16,0},{1,17},{17,1},{2,18},{18,2},{3,19},{19,3},{4,20},{20... | collective-permute-start | bytes 786440 | tf_op jit(solution)/shard_map/ppermute | solution.py:414
  80.7 10.5 %collective-permute-start.23 = (bf16[64,512]{1,0:T(8,128)(2,1)S(1)}, bf16[64,512]{1,0:T(8,128)(2,1)S(1)}, u32[]{:S(2)}, u32[]{:S(2)}) collective-permute-start(bf16[64,512]{1,0:T(8,128)(2,1)S(1)} %get-tuple-element.52), channel_id=1, source_target_pairs={{0,8},{2,10},{4,12},{6,14},{8,0},{10,2},{12,4},{14,6},{1,9},{3,11}... | collective-permute-start | bytes 196616 | tf_op jit(solution)/shard_map/ppermute | solution.py:371
  81.9 6.6 %collective-permute-start.24 = (bf16[64,512]{1,0:T(8,128)(2,1)S(1)}, bf16[64,512]{1,0:T(8,128)(2,1)S(1)}, u32[]{:S(2)}, u32[]{:S(2)}) collective-permute-start(bf16[64,512]{1,0:T(8,128)(2,1)S(1)} %get-tuple-element.53), channel_id=1, source_target_pairs={{0,12},{2,14},{4,8},{6,10},{8,4},{10,6},{12,0},{14,2},{1,13},{3,15... | collective-permute-start | bytes 196616 | tf_op jit(solution)/shard_map/ppermute | solution.py:371
  83.6 6.1 %collective-permute-start.25 = (bf16[64,512]{1,0:T(8,128)(2,1)S(1)}, bf16[64,512]{1,0:T(8,128)(2,1)S(1)}, u32[]{:S(2)}, u32[]{:S(2)}) collective-permute-start(bf16[64,512]{1,0:T(8,128)(2,1)S(1)} %get-tuple-element.54), channel_id=1, source_target_pairs={{0,4},{2,6},{4,0},{6,2},{8,12},{10,14},{12,8},{14,10},{1,5},{3,7},... | collective-permute-start | bytes 196616 | tf_op jit(solution)/shard_map/ppermute | solution.py:371
  89.7 6.4 %collective-permute-start.27 = (bf16[128,512]{1,0:T(8,128)(2,1)S(1)}, bf16[128,512]{1,0:T(8,128)(2,1)S(1)}, u32[]{:S(2)}, u32[]{:S(2)}) collective-permute-start(bf16[128,512]{1,0:T(8,128)(2,1)S(1)} %constant_dynamic-update-slice_fusion.18.refs_1_), channel_id=1, source_target_pairs={{0,2},{2,0},{4,6},{6,4},{8,10},{10,8},{12,14},{14,12},{1,3},{3,1},... | collective-permute-start | bytes 393224 | tf_op jit(solution)/shard_map/ppermute | solution.py:371
  91.2 6.7 %collective-permute-start.26 = (bf16[128,512]{1,0:T(8,128)(2,1)S(1)}, bf16[128,512]{1,0:T(8,128)(2,1)S(1)}, u32[]{:S(2)}, u32[]{:S(2)}) collective-permute-start(bf16[128,512]{1,0:T(8,128)(2,1)S(1)} %constant_dynamic-update-slice_fusion.16.refs_0_), channel_id=1, source_target_pairs={{0,2},{2,0},{4,6},{6,4},{8,10},{10,8},{12,14},{14,12},{1,3},{3,1},... | collective-permute-start | bytes 393224 | tf_op jit(solution)/shard_map/ppermute | solution.py:371
  98.5 9.6 %collective-permute-start.29 = (bf16[256,512]{1,0:T(8,128)(2,1)S(1)}, bf16[256,512]{1,0:T(8,128)(2,1)S(1)}, u32[]{:S(2)}, u32[]{:S(2)}) collective-permute-start(bf16[256,512]{1,0:T(8,128)(2,1)S(1)} %patch_attention_and_ffn.5.refs_0_), channel_id=1, source_target_pairs={{0,16},{16,0},{1,17},{17,1},{2,18},{18,2},{3,19},{19,3},{4,20},{20... | collective-permute-start | bytes 786440 | tf_op jit(solution)/shard_map/ppermute | solution.py:414
  108.6 7.2 %collective-permute-start.30 = (bf16[64,512]{1,0:T(8,128)(2,1)S(1)}, bf16[64,512]{1,0:T(8,128)(2,1)S(1)}, u32[]{:S(2)}, u32[]{:S(2)}) collective-permute-start(bf16[64,512]{1,0:T(8,128)(2,1)S(1)} %get-tuple-element.60), channel_id=1, source_target_pairs={{0,4},{2,6},{4,0},{6,2},{8,12},{10,14},{12,8},{14,10},{1,5},{3,7},... | collective-permute-start | bytes 196616 | tf_op jit(solution)/shard_map/ppermute | solution.py:371
  111.8 6.4 %collective-permute-start.31 = (bf16[64,512]{1,0:T(8,128)(2,1)S(1)}, bf16[64,512]{1,0:T(8,128)(2,1)S(1)}, u32[]{:S(2)}, u32[]{:S(2)}) collective-permute-start(bf16[64,512]{1,0:T(8,128)(2,1)S(1)} %get-tuple-element.61), channel_id=1, source_target_pairs={{0,8},{2,10},{4,12},{6,14},{8,0},{10,2},{12,4},{14,6},{1,9},{3,11}... | collective-permute-start | bytes 196616 | tf_op jit(solution)/shard_map/ppermute | solution.py:371
  113.9 6.1 %collective-permute-start.32 = (bf16[64,512]{1,0:T(8,128)(2,1)S(1)}, bf16[64,512]{1,0:T(8,128)(2,1)S(1)}, u32[]{:S(2)}, u32[]{:S(2)}) collective-permute-start(bf16[64,512]{1,0:T(8,128)(2,1)S(1)} %get-tuple-element.62), channel_id=1, source_target_pairs={{0,12},{2,14},{4,8},{6,10},{8,4},{10,6},{12,0},{14,2},{1,13},{3,15... | collective-permute-start | bytes 196616 | tf_op jit(solution)/shard_map/ppermute | solution.py:371
  (8 other events, 77.9 us)
where the time goes:
time: 122 us; the launch traced here: 121 us
  waiting for transfers between devices  54.6 us (45%)
  starting transfers between devices  43.9 us (36%)
  Pallas kernels  20.5 us (17%)
  local copies, waits for them, and re-layouts  2.18 us (2%)
    ppermute x23, waiting for transfers between devices, flipped(): lax.ppermute(x, axis, [(s, s ^ k) for s in range(lax.axis_size(axis))])  39.5 us
    ppermute x23, starting transfers between devices, flipped(): lax.ppermute(x, axis, [(s, s ^ k) for s in range(lax.axis_size(axis))])  25.3 us
    ppermute x8, starting transfers between devices, handed_on(): return lax.ppermute(x, ('pipe', 'patch'), pairs)  11.8 us
    ppermute x8, waiting for transfers between devices, handed_on(): return lax.ppermute(x, ('pipe', 'patch'), pairs)  10.7 us
    pallas_call x3, Pallas kernels, call_patch(): pl.pallas_call(functools.partial(patch_kernel, sizes, step, micro, outs),...  10 us
    ppermute x2, starting transfers between devices, onward(): return lax.ppermute(x, 'pipe', [(s, (s + 1) % pipes) for s in range(pipes)])  6.72 us
    pallas_call x3, Pallas kernels, call_time(): pl.pallas_call(functools.partial(time_kernel, sizes, step, micro), out_sh...  6.28 us
    ppermute x2, waiting for transfers between devices, onward(): return lax.ppermute(x, 'pipe', [(s, (s + 1) % pipes) for s in range(pipes)])  4.35 us
  transfers between devices with their start and end apart: 33, of which 20 were waited for; matrix products, arithmetic and copies ran while one was open for 1% of the time, Pallas kernels for 2%

commit v1 on v0

--- a/solution.py
+++ b/solution.py
@@ -107,8 +107,7 @@
 
 
 def pieces_of(sequence):
-    half = len(sequence) // 2
-    return [sequence[:half], sequence[half:]]
+    return [[k] for k in sequence]
 
 
 def row_sets(refs, slow, pieces):
@@ -193,9 +192,9 @@
             y_refs[k][...] = y[k * size : (k + 1) * size]
 
 
-def patch_kernel(sizes, step, micro, outs, place_ref, seen_ref, *refs):
+def patch_kernel(sizes, step, micro, place_ref, seen_ref, *refs):
     slow, _, patches, hl = sizes
-    count = len(refs) - 6 - outs
+    count = len(refs) - 6 - slow
     pieces = pieces_of([0] + [k for k in far_first(slow) if k])
     fast = count // len(pieces)
     x_refs, (gain_ref, scale_ref, w_in_ref, w_out_ref, up_ref, down_ref), y_refs = (
@@ -251,20 +250,9 @@
             hidden = (0.5 * u * (1.0 + bent)).astype(jnp.bfloat16)
             total = total + matmul(hidden, down_ref[0, start : start + chunk, :])
         y = regrouped(total, slow, inner).astype(jnp.bfloat16)
-        size = rows // outs
-        for k in range(outs):
+        size = rows // slow
+        for k in range(slow):
             y_refs[k][...] = y[k * size : (k + 1) * size]
-
-
-def pick_kernel(slow, last, place_ref, *refs):
-    x_refs, y_refs = refs[:-slow], refs[-slow:]
-    size = x_refs[0].shape[0] // slow
-    for hops, x_ref in enumerate(x_refs):
-
-        @pl.when(place_ref[0] == (last + hops) % len(x_refs))
-        def _():
-            for k, y_ref in enumerate(y_refs):
-                y_ref[...] = x_ref[k * size : (k + 1) * size, :]
 
 
 def write_rows(sizes, place_ref, x, y_ref):
@@ -328,29 +316,17 @@
     )(place, *xs, gains, scales, w_in, w_out)
 
 
-def call_patch(sizes, step, micro, shape, outs, place, seen, xs, gains, scales, w_in, w_out, w_up, w_down):
+def call_patch(sizes, step, micro, shape, place, seen, xs, gains, scales, w_in, w_out, w_up, w_down):
     rows, width = shape
     return pl.pallas_call(
-        functools.partial(patch_kernel, sizes, step, micro, outs),
-        out_shape=blocks_of(outs, rows, width),
+        functools.partial(patch_kernel, sizes, step, micro),
+        out_shape=blocks_of(sizes[0], rows, width),
         in_specs=[SMEM, SMEM] + [VMEM] * len(xs) + [VMEM, SMEM] + [VMEM] * 4,
-        out_specs=[VMEM] * outs,
+        out_specs=[VMEM] * sizes[0],
         compiler_params=PARAMS,
         cost_estimate=COST,
         name="patch_attention_and_ffn",
     )(place, seen, *xs, gains, scales, w_in, w_out, w_up, w_down)
-
-
-def call_pick(slow, last, place, xs):
-    rows, width = xs[0].shape
-    return pl.pallas_call(
-        functools.partial(pick_kernel, slow, last),
-        out_shape=blocks_of(slow, rows, width),
-        in_specs=[SMEM] + [VMEM] * len(xs),
-        out_specs=[VMEM] * slow,
-        compiler_params=PARAMS,
-        name="pick",
-    )(place, *xs)
 
 
 def call_write(kernel, sizes, place, shape, number, xs, out):
@@ -428,13 +404,11 @@
             write = functools.partial(early_kernel, sizes, pipes)
             out = call_write(write, sizes, place, x.shape, step - pipes, back, out)
         at_end = step == micro + pipes - 2
-        outs = 1 if at_end else slow
         done = call_patch(
             sizes,
             step,
             micro,
             x.shape[1:],
-            outs,
             place,
             seen,
             spread,
@@ -452,10 +426,19 @@
                 back = [jnp.concatenate(arrived)]
                 for _ in range(1, pipes):
                     back.append(onward(back[-1]))
-    done = list(done)
-    for _ in range(1, pipes):
-        done.append(onward(done[-1]))
-    blocks = along_slow(call_pick(slow, last, place, done), in_stage, 1)
+    stage = lax.axis_index("pipe")
+    blocks = {}
+    for count, k in enumerate(far):
+        own = done[k]
+        if count >= slow // 2:
+            own, blocks[far[0]] = lax.optimization_barrier((own, blocks[far[0]]))
+        chosen = block = own
+        for hop in range(pipes - 1):
+            block = onward(block)
+            chosen = jnp.where(stage == hop, block, chosen)
+        blocks[k] = chosen
+    blocks = {k: in_stage(blocks[k], k * fast) if k else blocks[k] for k in far}
+    blocks = [blocks[k] for k in range(slow)]
     write = functools.partial(final_kernel, sizes)
     out = call_write(write, sizes, place, x.shape, micro - 1, blocks, out)
     return out.reshape(inputs.shape)

time: 122 us -> 112 us (0.918)
  waiting for transfers between devices: 54.6 us -> 37.2 us
  starting transfers between devices: 43.9 us -> 52.3 us
    ppermute x23 -> x33, waiting for transfers between devices: 39.5 us -> 25.6 us  [flipped(): lax.ppermute(x, axis, [(s, s ^ k) for s in range(lax.axis_size(axis))])]
    ppermute x23 -> x33, starting transfers between devices: 25.3 us -> 31.1 us  [flipped(): lax.ppermute(x, axis, [(s, s ^ k) for s in range(lax.axis_size(axis))])]
    ppermute x2 -> x5, starting transfers between devices: 6.72 us -> 9.39 us  [onward(): return lax.ppermute(x, 'pipe', [(s, (s + 1) % pipes) for s in range(pipes)])]
    ppermute x8, waiting for transfers between devices: 10.7 us -> 9 us  [handed_on(): return lax.ppermute(x, ('pipe', 'patch'), pairs)]
    ppermute x2 -> x5, waiting for transfers between devices: 4.35 us -> 2.65 us  [onward(): return lax.ppermute(x, 'pipe', [(s, (s + 1) % pipes) for s in range(pipes)])]
    pallas_call x4 -> x3, Pallas kernels: 10.6 us -> 10.1 us  [call_patch(): pl.pallas_call(functools.partial(patch_kernel, sizes, step, micro), out_s...]
  transfers between devices with their start and end apart: 33 -> 46, of which waited for: 20 -> 30; matrix products, arithmetic and copies ran while one was open for 1% -> 1% of each run, Pallas kernels for 2% -> 2%
where the time goes in v1:
time: 112 us
  starting transfers between devices  52.3 us (47%)
  waiting for transfers between devices  37.2 us (33%)
  Pallas kernels  20.1 us (18%)
  local copies, waits for them, and re-layouts  2.07 us (2%)
    ppermute x33, starting transfers between devices, flipped(): lax.ppermute(x, axis, [(s, s ^ k) for s in range(lax.axis_size(axis))])  31.1 us
    ppermute x33, waiting for transfers between devices, flipped(): lax.ppermute(x, axis, [(s, s ^ k) for s in range(lax.axis_size(axis))])  25.6 us
    ppermute x8, starting transfers between devices, handed_on(): return lax.ppermute(x, ('pipe', 'patch'), pairs)  11.8 us
    pallas_call x3, Pallas kernels, call_patch(): pl.pallas_call(functools.partial(patch_kernel, sizes, step, micro), out_s...  10.1 us
    ppermute x5, starting transfers between devices, onward(): return lax.ppermute(x, 'pipe', [(s, (s + 1) % pipes) for s in range(pipes)])  9.39 us
    ppermute x8, waiting for transfers between devices, handed_on(): return lax.ppermute(x, ('pipe', 'patch'), pairs)  9 us
    pallas_call x3, Pallas kernels, call_time(): pl.pallas_call(functools.partial(time_kernel, sizes, step, micro), out_sh...  6.36 us
    pallas_call x2, Pallas kernels, call_write(): pl.pallas_call(kernel, out_shape=jax.ShapeDtypeStruct(shape, jnp.bfloat16...  2.95 us
  transfers between devices with their start and end apart: 46, of which 30 were waited for; matrix products, arithmetic and copies ran while one was open for 1% of the time, Pallas kernels for 2%

profile of v1, /device:TPU:0, one launch (start us, length us, event | category | flops | bytes accessed | tf_op | source)
XLA Modules:
  0.0 112.0 jit_solution(6920613065051852956)
XLA Ops:
  3.5 2.9 %time_attention.3 = (bf16[64,512]{1,0:T(8,128)(2,1)S(1)}, bf16[64,512]{1,0:T(8,128)(2,1)S(1)}, bf16[64,512]{1,0:T(8,128)(2,1)S(1)}, bf16[64,512]{1,0:T(8,128)(2,1)S(1)}) custom-call(s32[3]{0:T(128)S(1)} %pad_add_fusion.place_ref, bf16[256,256]{1,0:T(8,128)(2,1)S(1)} %input_order.1.refs_0_, bf16[2,256,512]{2,1,0:T(8,128)(2,1)S(1)} %bitcast.6, ...), custom_call_target="tpu_custom_call" | custom-call | flops 5368709120 | bytes 1048576 | tf_op jit(solution)/shard_map/time_attention/pallas_call | solution.py:307
  6.4 3.6 %collective-permute-start.1 = (bf16[64,512]{1,0:T(8,128)(2,1)S(1)}, bf16[64,512]{1,0:T(8,128)(2,1)S(1)}, u32[]{:S(2)}, u32[]{:S(2)}) collective-permute-start(bf16[64,512]{1,0:T(8,128)(2,1)S(1)} %get-tuple-element.44), channel_id=1, source_target_pairs={{0,8},{2,10},{4,12},{6,14},{8,0},{10,2},{12,4},{14,6},{1,9},{3,11}... | collective-permute-start | bytes 196616 | tf_op jit(solution)/shard_map/ppermute | solution.py:347
  10.1 1.3 %collective-permute-start.2 = (bf16[64,512]{1,0:T(8,128)(2,1)S(1)}, bf16[64,512]{1,0:T(8,128)(2,1)S(1)}, u32[]{:S(2)}, u32[]{:S(2)}) collective-permute-start(bf16[64,512]{1,0:T(8,128)(2,1)S(1)} %get-tuple-element.45), channel_id=1, source_target_pairs={{0,12},{2,14},{4,8},{6,10},{8,4},{10,6},{12,0},{14,2},{1,13},{3,15... | collective-permute-start | bytes 196616 | tf_op jit(solution)/shard_map/ppermute | solution.py:347
  11.7 1.5 %collective-permute-start.4 = (bf16[64,512]{1,0:T(8,128)(2,1)S(1)}, bf16[64,512]{1,0:T(8,128)(2,1)S(1)}, u32[]{:S(2)}, u32[]{:S(2)}) collective-permute-start(bf16[64,512]{1,0:T(8,128)(2,1)S(1)} %get-tuple-element.43.refs_0_), channel_id=1, source_target_pairs={{0,2},{2,0},{4,6},{6,4},{8,10},{10,8},{12,14},{14,12},{1,3},{3,1},... | collective-permute-start | bytes 196616 | tf_op jit(solution)/shard_map/ppermute | solution.py:347
  13.2 1.3 %collective-permute-done.1.refs_1_ = bf16[64,512]{1,0:T(8,128)(2,1)S(1)} collective-permute-done((bf16[64,512]{1,0:T(8,128)(2,1)S(1)}, bf16[64,512]{1,0:T(8,128)(2,1)S(1)}, u32[]{:S(2)}, u32[]{:S(2)}) %collective-permute-start.1) | collective-permute-done | bytes 65568 | tf_op jit(solution)/shard_map/ppermute | solution.py:347
  14.4 1.6 %collective-permute-start.5 = (bf16[64,512]{1,0:T(8,128)(2,1)S(1)}, bf16[64,512]{1,0:T(8,128)(2,1)S(1)}, u32[]{:S(2)}, u32[]{:S(2)}) collective-permute-start(bf16[64,512]{1,0:T(8,128)(2,1)S(1)} %collective-permute-done.1.refs_1_), channel_id=1, source_target_pairs={{0,2},{2,0},{4,6},{6,4},{8,10},{10,8},{12,14},{14,12},{1,3},{3,1},... | collective-permute-start | bytes 196616 | tf_op jit(solution)/shard_map/ppermute | solution.py:347
  16.8 1.5 %collective-permute-start.6 = (bf16[64,512]{1,0:T(8,128)(2,1)S(1)}, bf16[64,512]{1,0:T(8,128)(2,1)S(1)}, u32[]{:S(2)}, u32[]{:S(2)}) collective-permute-start(bf16[64,512]{1,0:T(8,128)(2,1)S(1)} %collective-permute-done.2.refs_2_), channel_id=1, source_target_pairs={{0,2},{2,0},{4,6},{6,4},{8,10},{10,8},{12,14},{14,12},{1,3},{3,1},... | collective-permute-start | bytes 196616 | tf_op jit(solution)/shard_map/ppermute | solution.py:347
  19.4 1.7 %collective-permute-done.6.refs_6_ = bf16[64,512]{1,0:T(8,128)(2,1)S(1)} collective-permute-done((bf16[64,512]{1,0:T(8,128)(2,1)S(1)}, bf16[64,512]{1,0:T(8,128)(2,1)S(1)}, u32[]{:S(2)}, u32[]{:S(2)}) %collective-permute-start.6) | collective-permute-done | bytes 65568 | tf_op jit(solution)/shard_map/ppermute | solution.py:347
  21.1 1.5 %collective-permute-done.7.refs_7_ = bf16[64,512]{1,0:T(8,128)(2,1)S(1)} collective-permute-done((bf16[64,512]{1,0:T(8,128)(2,1)S(1)}, bf16[64,512]{1,0:T(8,128)(2,1)S(1)}, u32[]{:S(2)}, u32[]{:S(2)}) %collective-permute-start.7) | collective-permute-done | bytes 65568 | tf_op jit(solution)/shard_map/ppermute | solution.py:347
  22.6 4.7 %patch_attention_and_ffn.3 = (bf16[64,512]{1,0:T(8,128)(2,1)S(1)}, bf16[64,512]{1,0:T(8,128)(2,1)S(1)}, bf16[64,512]{1,0:T(8,128)(2,1)S(1)}, bf16[64,512]{1,0:T(8,128)(2,1)S(1)}) custom-call(s32[3]{0:T(128)S(1)} %pad_add_fusion.place_ref, s32[2,2]{1,0:T(2,128)S(1)} %copy-done.5, bf16[64,512]{1,0:T(8,128)(2,1)S(1)} %get-tuple-element.43.refs_0_, ...), custom_call_target="tpu_custom_call" | custom-call | flops 5368709120 | bytes 1048576 | tf_op jit(solution)/shard_map/patch_attention_and_ffn/pallas_call | solution.py:321
  27.4 4.3 %collective-permute-start.9 = (bf16[64,512]{1,0:T(8,128)(2,1)S(1)}, bf16[64,512]{1,0:T(8,128)(2,1)S(1)}, u32[]{:S(2)}, u32[]{:S(2)}) collective-permute-start(bf16[64,512]{1,0:T(8,128)(2,1)S(1)} %get-tuple-element.48), channel_id=1, source_target_pairs={{0,28},{2,30},{4,24},{6,26},{8,20},{10,22},{12,16},{14,18},{16,12}... | collective-permute-start | bytes 196616 | tf_op jit(solution)/shard_map/ppermute | solution.py:357
  33.2 1.8 %collective-permute-done.8.refs_3_ = bf16[64,512]{1,0:T(8,128)(2,1)S(1)} collective-permute-done((bf16[64,512]{1,0:T(8,128)(2,1)S(1)}, bf16[64,512]{1,0:T(8,128)(2,1)S(1)}, u32[]{:S(2)}, u32[]{:S(2)}) %collective-permute-start.8) | collective-permute-done | bytes 65568 | tf_op jit(solution)/shard_map/ppermute | solution.py:357
  36.4 1.5 %collective-permute-done.11.refs_6_ = bf16[64,512]{1,0:T(8,128)(2,1)S(1)} collective-permute-done((bf16[64,512]{1,0:T(8,128)(2,1)S(1)}, bf16[64,512]{1,0:T(8,128)(2,1)S(1)}, u32[]{:S(2)}, u32[]{:S(2)}) %collective-permute-start.11) | collective-permute-done | bytes 65568 | tf_op jit(solution)/shard_map/ppermute | solution.py:357
  39.1 2.9 %time_attention.4 = (bf16[64,512]{1,0:T(8,128)(2,1)S(1)}, bf16[64,512]{1,0:T(8,128)(2,1)S(1)}, bf16[64,512]{1,0:T(8,128)(2,1)S(1)}, bf16[64,512]{1,0:T(8,128)(2,1)S(1)}) custom-call(s32[3]{0:T(128)S(1)} %pad_add_fusion.place_ref, bf16[256,256]{1,0:T(8,128)(2,1)S(1)} %input_order.1.refs_0_, bf16[2,256,512]{2,1,0:T(8,128)(2,1)S(1)} %bitcast.7, ...), custom_call_target="tpu_custom_call" | custom-call | flops 5368709120 | bytes 1048576 | tf_op jit(solution)/shard_map/time_attention/pallas_call | solution.py:307
  42.0 2.7 %collective-permute-start.16 = (bf16[64,512]{1,0:T(8,128)(2,1)S(1)}, bf16[64,512]{1,0:T(8,128)(2,1)S(1)}, u32[]{:S(2)}, u32[]{:S(2)}) collective-permute-start(bf16[64,512]{1,0:T(8,128)(2,1)S(1)} %get-tuple-element.52), channel_id=1, source_target_pairs={{0,8},{2,10},{4,12},{6,14},{8,0},{10,2},{12,4},{14,6},{1,9},{3,11}... | collective-permute-start | bytes 196616 | tf_op jit(solution)/shard_map/ppermute | solution.py:347
  45.9 1.3 %collective-permute-start.19 = (bf16[64,512]{1,0:T(8,128)(2,1)S(1)}, bf16[64,512]{1,0:T(8,128)(2,1)S(1)}, u32[]{:S(2)}, u32[]{:S(2)}) collective-permute-start(bf16[64,512]{1,0:T(8,128)(2,1)S(1)} %get-tuple-element.51.refs_0_), channel_id=1, source_target_pairs={{0,2},{2,0},{4,6},{6,4},{8,10},{10,8},{12,14},{14,12},{1,3},{3,1},... | collective-permute-start | bytes 196616 | tf_op jit(solution)/shard_map/ppermute | solution.py:347
  47.2 2.8 %collective-permute-done.16.refs_1_ = bf16[64,512]{1,0:T(8,128)(2,1)S(1)} collective-permute-done((bf16[64,512]{1,0:T(8,128)(2,1)S(1)}, bf16[64,512]{1,0:T(8,128)(2,1)S(1)}, u32[]{:S(2)}, u32[]{:S(2)}) %collective-permute-start.16) | collective-permute-done | bytes 65568 | tf_op jit(solution)/shard_map/ppermute | solution.py:347
  53.3 1.6 %collective-permute-done.20.refs_5_ = bf16[64,512]{1,0:T(8,128)(2,1)S(1)} collective-permute-done((bf16[64,512]{1,0:T(8,128)(2,1)S(1)}, bf16[64,512]{1,0:T(8,128)(2,1)S(1)}, u32[]{:S(2)}, u32[]{:S(2)}) %collective-permute-start.20) | collective-permute-done | bytes 65568 | tf_op jit(solution)/shard_map/ppermute | solution.py:347
  56.9 4.9 %patch_attention_and_ffn.4 = (bf16[64,512]{1,0:T(8,128)(2,1)S(1)}, bf16[64,512]{1,0:T(8,128)(2,1)S(1)}, bf16[64,512]{1,0:T(8,128)(2,1)S(1)}, bf16[64,512]{1,0:T(8,128)(2,1)S(1)}) custom-call(s32[3]{0:T(128)S(1)} %pad_add_fusion.place_ref, s32[2,2]{1,0:T(2,128)S(1)} %copy-done.5, bf16[64,512]{1,0:T(8,128)(2,1)S(1)} %get-tuple-element.51.refs_0_, ...), custom_call_target="tpu_custom_call" | custom-call | flops 5368709120 | bytes 1048576 | tf_op jit(solution)/shard_map/patch_attention_and_ffn/pallas_call | solution.py:321
  61.7 2.8 %collective-permute-start.23 = (bf16[64,512]{1,0:T(8,128)(2,1)S(1)}, bf16[64,512]{1,0:T(8,128)(2,1)S(1)}, u32[]{:S(2)}, u32[]{:S(2)}) collective-permute-start(bf16[64,512]{1,0:T(8,128)(2,1)S(1)} %get-tuple-element.55), channel_id=1, source_target_pairs={{0,24},{2,26},{4,28},{6,30},{8,16},{10,18},{12,20},{14,22},{16,8},... | collective-permute-start | bytes 196616 | tf_op jit(solution)/shard_map/ppermute | solution.py:357
  64.6 1.5 %collective-permute-start.24 = (bf16[64,512]{1,0:T(8,128)(2,1)S(1)}, bf16[64,512]{1,0:T(8,128)(2,1)S(1)}, u32[]{:S(2)}, u32[]{:S(2)}) collective-permute-start(bf16[64,512]{1,0:T(8,128)(2,1)S(1)} %get-tuple-element.56), channel_id=1, source_target_pairs={{0,28},{2,30},{4,24},{6,26},{8,20},{10,22},{12,16},{14,18},{16,12}... | collective-permute-start | bytes 196616 | tf_op jit(solution)/shard_map/ppermute | solution.py:357
  68.7 3.1 %collective-permute-done.24.refs_1_ = bf16[64,512]{1,0:T(8,128)(2,1)S(1)} collective-permute-done((bf16[64,512]{1,0:T(8,128)(2,1)S(1)}, bf16[64,512]{1,0:T(8,128)(2,1)S(1)}, u32[]{:S(2)}, u32[]{:S(2)}) %collective-permute-start.24) | collective-permute-done | bytes 65568 | tf_op jit(solution)/shard_map/ppermute | solution.py:357
  74.6 1.8 %collective-permute-start.31 = (bf16[64,512]{1,0:T(8,128)(2,1)S(1)}, bf16[64,512]{1,0:T(8,128)(2,1)S(1)}, u32[]{:S(2)}, u32[]{:S(2)}) collective-permute-start(bf16[64,512]{1,0:T(8,128)(2,1)S(1)} %get-tuple-element.60), channel_id=1, source_target_pairs={{0,8},{2,10},{4,12},{6,14},{8,0},{10,2},{12,4},{14,6},{1,9},{3,11}... | collective-permute-start | bytes 196616 | tf_op jit(solution)/shard_map/ppermute | solution.py:347
  78.9 3.6 %collective-permute-done.31.refs_1_ = bf16[64,512]{1,0:T(8,128)(2,1)S(1)} collective-permute-done((bf16[64,512]{1,0:T(8,128)(2,1)S(1)}, bf16[64,512]{1,0:T(8,128)(2,1)S(1)}, u32[]{:S(2)}, u32[]{:S(2)}) %collective-permute-start.31) | collective-permute-done | bytes 65568 | tf_op jit(solution)/shard_map/ppermute | solution.py:347
  83.0 1.5 %collective-permute-start.36 = (bf16[64,512]{1,0:T(8,128)(2,1)S(1)}, bf16[64,512]{1,0:T(8,128)(2,1)S(1)}, u32[]{:S(2)}, u32[]{:S(2)}) collective-permute-start(bf16[64,512]{1,0:T(8,128)(2,1)S(1)} %collective-permute-done.32.refs_2_), channel_id=1, source_target_pairs={{0,2},{2,0},{4,6},{6,4},{8,10},{10,8},{12,14},{14,12},{1,3},{3,1},... | collective-permute-start | bytes 196616 | tf_op jit(solution)/shard_map/ppermute | solution.py:347
  85.0 2.1 %collective-permute-done.35.refs_5_ = bf16[64,512]{1,0:T(8,128)(2,1)S(1)} collective-permute-done((bf16[64,512]{1,0:T(8,128)(2,1)S(1)}, bf16[64,512]{1,0:T(8,128)(2,1)S(1)}, u32[]{:S(2)}, u32[]{:S(2)}) %collective-permute-start.35) | collective-permute-done | bytes 65568 | tf_op jit(solution)/shard_map/ppermute | solution.py:347
  89.6 6.7 %collective-permute-start.39 = (bf16[64,512]{1,0:T(8,128)(2,1)S(1)}, bf16[64,512]{1,0:T(8,128)(2,1)S(1)}, u32[]{:S(2)}, u32[]{:S(2)}) collective-permute-start(bf16[64,512]{1,0:T(8,128)(2,1)S(1)} %get-tuple-element.72), channel_id=1, source_target_pairs={{0,16},{16,0},{1,17},{17,1},{2,18},{18,2},{3,19},{19,3},{4,20},{20... | collective-permute-start | bytes 196616 | tf_op jit(solution)/shard_map/ppermute | solution.py:390
  96.4 1.5 %final_order.2.refs_4_ = bf16[2,256,512]{2,1,0:T(8,128)(2,1)} custom-call(s32[3]{0:T(128)S(1)} %pad_add_fusion.place_ref, bf16[256,512]{1,0:T(8,128)(2,1)S(1)} %constant_dynamic-update-slice_fusion.refs_0_, bf16[256,512]{1,0:T(8,128)(2,1)S(1)} %collective-permute-done.38.refs_1_), custom_call_target="tpu_custom_call" | custom-call | tf_op jit(solution)/shard_map/final_order/pallas_call | solution.py:334
  99.0 2.6 %collective-permute-start.43 = (bf16[64,512]{1,0:T(8,128)(2,1)S(1)}, bf16[64,512]{1,0:T(8,128)(2,1)S(1)}, u32[]{:S(2)}, u32[]{:S(2)}) collective-permute-start(bf16[64,512]{1,0:T(8,128)(2,1)S(1)} %broadcast_select_fusion.3), channel_id=1, source_target_pairs={{0,8},{2,10},{4,12},{6,14},{8,0},{10,2},{12,4},{14,6},{1,9},{3,11}... | collective-permute-start | bytes 196616 | tf_op jit(solution)/shard_map/ppermute | solution.py:347
  101.7 1.5 %collective-permute-start.41 = (bf16[64,512]{1,0:T(8,128)(2,1)S(1)}, bf16[64,512]{1,0:T(8,128)(2,1)S(1)}, u32[]{:S(2)}, u32[]{:S(2)}) collective-permute-start(bf16[64,512]{1,0:T(8,128)(2,1)S(1)} %get-tuple-element.76), channel_id=1, source_target_pairs={{0,16},{16,0},{1,17},{17,1},{2,18},{18,2},{3,19},{19,3},{4,20},{20... | collective-permute-start | bytes 196616 | tf_op jit(solution)/shard_map/ppermute | solution.py:390
  107.4 2.4 %collective-permute-done.45.refs_3_ = bf16[64,512]{1,0:T(8,128)(2,1)S(1)} collective-permute-done((bf16[64,512]{1,0:T(8,128)(2,1)S(1)}, bf16[64,512]{1,0:T(8,128)(2,1)S(1)}, u32[]{:S(2)}, u32[]{:S(2)}) %collective-permute-start.45) | collective-permute-done | bytes 65568 | tf_op jit(solution)/shard_map/ppermute | solution.py:347
  110.5 1.5 %final_order.3 = bf16[2,256,512]{2,1,0:T(8,128)(2,1)} custom-call(s32[3]{0:T(128)S(1)} %pad_add_fusion.place_ref, bf16[64,512]{1,0:T(8,128)(2,1)S(1)} %broadcast_select_fusion.2.refs_0_, bf16[64,512]{1,0:T(8,128)(2,1)S(1)} %collective-permute-done.42.refs_1_, bf16[64,512]{1,0:T(8,128)(2,1)S(1)} %collective-permute-done.43.refs_2_, ...), custom_call_target="tpu_custom_call", output_to_operand_aliasing={{}: (5, {})} | custom-call | tf_op jit(solution)/shard_map/final_order/pallas_call | solution.py:334
  (93 shorter events, 33.7 us)
Async XLA Ops:
  6.4 8.0 %collective-permute-start.1 = (bf16[64,512]{1,0:T(8,128)(2,1)S(1)}, bf16[64,512]{1,0:T(8,128)(2,1)S(1)}, u32[]{:S(2)}, u32[]{:S(2)}) collective-permute-start(bf16[64,512]{1,0:T(8,128)(2,1)S(1)} %get-tuple-element.44), channel_id=1, source_target_pairs={{0,8},{2,10},{4,12},{6,14},{8,0},{10,2},{12,4},{14,6},{1,9},{3,11}... | collective-permute-start | bytes 196616 | tf_op jit(solution)/shard_map/ppermute | solution.py:347
  10.1 6.7 %collective-permute-start.2 = (bf16[64,512]{1,0:T(8,128)(2,1)S(1)}, bf16[64,512]{1,0:T(8,128)(2,1)S(1)}, u32[]{:S(2)}, u32[]{:S(2)}) collective-permute-start(bf16[64,512]{1,0:T(8,128)(2,1)S(1)} %get-tuple-element.45), channel_id=1, source_target_pairs={{0,12},{2,14},{4,8},{6,10},{8,4},{10,6},{12,0},{14,2},{1,13},{3,15... | collective-permute-start | bytes 196616 | tf_op jit(solution)/shard_map/ppermute | solution.py:347
  11.4 6.9 %collective-permute-start.3 = (bf16[64,512]{1,0:T(8,128)(2,1)S(1)}, bf16[64,512]{1,0:T(8,128)(2,1)S(1)}, u32[]{:S(2)}, u32[]{:S(2)}) collective-permute-start(bf16[64,512]{1,0:T(8,128)(2,1)S(1)} %get-tuple-element.46), channel_id=1, source_target_pairs={{0,4},{2,6},{4,0},{6,2},{8,12},{10,14},{12,8},{14,10},{1,5},{3,7},... | collective-permute-start | bytes 196616 | tf_op jit(solution)/shard_map/ppermute | solution.py:347
  11.7 7.2 %collective-permute-start.4 = (bf16[64,512]{1,0:T(8,128)(2,1)S(1)}, bf16[64,512]{1,0:T(8,128)(2,1)S(1)}, u32[]{:S(2)}, u32[]{:S(2)}) collective-permute-start(bf16[64,512]{1,0:T(8,128)(2,1)S(1)} %get-tuple-element.43.refs_0_), channel_id=1, source_target_pairs={{0,2},{2,0},{4,6},{6,4},{8,10},{10,8},{12,14},{14,12},{1,3},{3,1},... | collective-permute-start | bytes 196616 | tf_op jit(solution)/shard_map/ppermute | solution.py:347
  14.4 5.0 %collective-permute-start.5 = (bf16[64,512]{1,0:T(8,128)(2,1)S(1)}, bf16[64,512]{1,0:T(8,128)(2,1)S(1)}, u32[]{:S(2)}, u32[]{:S(2)}) collective-permute-start(bf16[64,512]{1,0:T(8,128)(2,1)S(1)} %collective-permute-done.1.refs_1_), channel_id=1, source_target_pairs={{0,2},{2,0},{4,6},{6,4},{8,10},{10,8},{12,14},{14,12},{1,3},{3,1},... | collective-permute-start | bytes 196616 | tf_op jit(solution)/shard_map/ppermute | solution.py:347
  27.3 7.7 %collective-permute-start.8 = (bf16[64,512]{1,0:T(8,128)(2,1)S(1)}, bf16[64,512]{1,0:T(8,128)(2,1)S(1)}, u32[]{:S(2)}, u32[]{:S(2)}) collective-permute-start(bf16[64,512]{1,0:T(8,128)(2,1)S(1)} %get-tuple-element.47), channel_id=1, source_target_pairs={{0,24},{2,26},{4,28},{6,30},{8,16},{10,18},{12,20},{14,22},{16,8},... | collective-permute-start | bytes 196616 | tf_op jit(solution)/shard_map/ppermute | solution.py:357
  27.4 7.6 %collective-permute-start.9 = (bf16[64,512]{1,0:T(8,128)(2,1)S(1)}, bf16[64,512]{1,0:T(8,128)(2,1)S(1)}, u32[]{:S(2)}, u32[]{:S(2)}) collective-permute-start(bf16[64,512]{1,0:T(8,128)(2,1)S(1)} %get-tuple-element.48), channel_id=1, source_target_pairs={{0,28},{2,30},{4,24},{6,26},{8,20},{10,22},{12,16},{14,18},{16,12}... | collective-permute-start | bytes 196616 | tf_op jit(solution)/shard_map/ppermute | solution.py:357
  31.7 4.7 %collective-permute-start.10 = (bf16[64,512]{1,0:T(8,128)(2,1)S(1)}, bf16[64,512]{1,0:T(8,128)(2,1)S(1)}, u32[]{:S(2)}, u32[]{:S(2)}) collective-permute-start(bf16[64,512]{1,0:T(8,128)(2,1)S(1)} %get-tuple-element.49), channel_id=1, source_target_pairs={{0,16},{2,18},{4,20},{6,22},{8,24},{10,26},{12,28},{14,30},{16,0},... | collective-permute-start | bytes 196616 | tf_op jit(solution)/shard_map/ppermute | solution.py:357
  32.7 5.2 %collective-permute-start.11 = (bf16[64,512]{1,0:T(8,128)(2,1)S(1)}, bf16[64,512]{1,0:T(8,128)(2,1)S(1)}, u32[]{:S(2)}, u32[]{:S(2)}) collective-permute-start(bf16[64,512]{1,0:T(8,128)(2,1)S(1)} %get-tuple-element.50), channel_id=1, source_target_pairs={{0,20},{2,22},{4,16},{6,18},{8,28},{10,30},{12,24},{14,26},{16,4},... | collective-permute-start | bytes 196616 | tf_op jit(solution)/shard_map/ppermute | solution.py:357
  42.0 8.0 %collective-permute-start.16 = (bf16[64,512]{1,0:T(8,128)(2,1)S(1)}, bf16[64,512]{1,0:T(8,128)(2,1)S(1)}, u32[]{:S(2)}, u32[]{:S(2)}) collective-permute-start(bf16[64,512]{1,0:T(8,128)(2,1)S(1)} %get-tuple-element.52), channel_id=1, source_target_pairs={{0,8},{2,10},{4,12},{6,14},{8,0},{10,2},{12,4},{14,6},{1,9},{3,11}... | collective-permute-start | bytes 196616 | tf_op jit(solution)/shard_map/ppermute | solution.py:347
  44.8 6.5 %collective-permute-start.17 = (bf16[64,512]{1,0:T(8,128)(2,1)S(1)}, bf16[64,512]{1,0:T(8,128)(2,1)S(1)}, u32[]{:S(2)}, u32[]{:S(2)}) collective-permute-start(bf16[64,512]{1,0:T(8,128)(2,1)S(1)} %get-tuple-element.53), channel_id=1, source_target_pairs={{0,12},{2,14},{4,8},{6,10},{8,4},{10,6},{12,0},{14,2},{1,13},{3,15... | collective-permute-start | bytes 196616 | tf_op jit(solution)/shard_map/ppermute | solution.py:347
  45.4 7.2 %collective-permute-start.18 = (bf16[64,512]{1,0:T(8,128)(2,1)S(1)}, bf16[64,512]{1,0:T(8,128)(2,1)S(1)}, u32[]{:S(2)}, u32[]{:S(2)}) collective-permute-start(bf16[64,512]{1,0:T(8,128)(2,1)S(1)} %get-tuple-element.54), channel_id=1, source_target_pairs={{0,4},{2,6},{4,0},{6,2},{8,12},{10,14},{12,8},{14,10},{1,5},{3,7},... | collective-permute-start | bytes 196616 | tf_op jit(solution)/shard_map/ppermute | solution.py:347
  45.9 7.5 %collective-permute-start.19 = (bf16[64,512]{1,0:T(8,128)(2,1)S(1)}, bf16[64,512]{1,0:T(8,128)(2,1)S(1)}, u32[]{:S(2)}, u32[]{:S(2)}) collective-permute-start(bf16[64,512]{1,0:T(8,128)(2,1)S(1)} %get-tuple-element.51.refs_0_), channel_id=1, source_target_pairs={{0,2},{2,0},{4,6},{6,4},{8,10},{10,8},{12,14},{14,12},{1,3},{3,1},... | collective-permute-start | bytes 196616 | tf_op jit(solution)/shard_map/ppermute | solution.py:347
  50.0 4.9 %collective-permute-start.20 = (bf16[64,512]{1,0:T(8,128)(2,1)S(1)}, bf16[64,512]{1,0:T(8,128)(2,1)S(1)}, u32[]{:S(2)}, u32[]{:S(2)}) collective-permute-start(bf16[64,512]{1,0:T(8,128)(2,1)S(1)} %collective-permute-done.16.refs_1_), channel_id=1, source_target_pairs={{0,2},{2,0},{4,6},{6,4},{8,10},{10,8},{12,14},{14,12},{1,3},{3,1},... | collective-permute-start | bytes 196616 | tf_op jit(solution)/shard_map/ppermute | solution.py:347
  61.7 7.0 %collective-permute-start.23 = (bf16[64,512]{1,0:T(8,128)(2,1)S(1)}, bf16[64,512]{1,0:T(8,128)(2,1)S(1)}, u32[]{:S(2)}, u32[]{:S(2)}) collective-permute-start(bf16[64,512]{1,0:T(8,128)(2,1)S(1)} %get-tuple-element.55), channel_id=1, source_target_pairs={{0,24},{2,26},{4,28},{6,30},{8,16},{10,18},{12,20},{14,22},{16,8},... | collective-permute-start | bytes 196616 | tf_op jit(solution)/shard_map/ppermute | solution.py:357
  64.6 7.2 %collective-permute-start.24 = (bf16[64,512]{1,0:T(8,128)(2,1)S(1)}, bf16[64,512]{1,0:T(8,128)(2,1)S(1)}, u32[]{:S(2)}, u32[]{:S(2)}) collective-permute-start(bf16[64,512]{1,0:T(8,128)(2,1)S(1)} %get-tuple-element.56), channel_id=1, source_target_pairs={{0,28},{2,30},{4,24},{6,26},{8,20},{10,22},{12,16},{14,18},{16,12}... | collective-permute-start | bytes 196616 | tf_op jit(solution)/shard_map/ppermute | solution.py:357
  66.1 6.4 %collective-permute-start.25 = (bf16[64,512]{1,0:T(8,128)(2,1)S(1)}, bf16[64,512]{1,0:T(8,128)(2,1)S(1)}, u32[]{:S(2)}, u32[]{:S(2)}) collective-permute-start(bf16[64,512]{1,0:T(8,128)(2,1)S(1)} %get-tuple-element.57), channel_id=1, source_target_pairs={{0,16},{2,18},{4,20},{6,22},{8,24},{10,26},{12,28},{14,30},{16,0},... | collective-permute-start | bytes 196616 | tf_op jit(solution)/shard_map/ppermute | solution.py:357
  67.1 5.4 %collective-permute-start.26 = (bf16[64,512]{1,0:T(8,128)(2,1)S(1)}, bf16[64,512]{1,0:T(8,128)(2,1)S(1)}, u32[]{:S(2)}, u32[]{:S(2)}) collective-permute-start(bf16[64,512]{1,0:T(8,128)(2,1)S(1)} %get-tuple-element.58), channel_id=1, source_target_pairs={{0,20},{2,22},{4,16},{6,18},{8,28},{10,30},{12,24},{14,26},{16,4},... | collective-permute-start | bytes 196616 | tf_op jit(solution)/shard_map/ppermute | solution.py:357
  68.7 4.9 %collective-permute-start.27 = (bf16[64,512]{1,0:T(8,128)(2,1)S(1)}, bf16[64,512]{1,0:T(8,128)(2,1)S(1)}, u32[]{:S(2)}, u32[]{:S(2)}) collective-permute-start(bf16[64,512]{1,0:T(8,128)(2,1)S(1)} %collective-permute-done.23.refs_0_), channel_id=1, source_target_pairs={{0,1},{1,0},{2,3},{3,2},{4,5},{5,4},{6,7},{7,6},{8,9},{9,8},{10,11... | collective-permute-start | bytes 196616 | tf_op jit(solution)/shard_map/ppermute | solution.py:347
  73.1 15.9 %collective-permute-start.38 = (bf16[256,512]{1,0:T(8,128)(2,1)S(1)}, bf16[256,512]{1,0:T(8,128)(2,1)S(1)}, u32[]{:S(2)}, u32[]{:S(2)}) collective-permute-start(bf16[256,512]{1,0:T(8,128)(2,1)S(1)} %constant_dynamic-update-slice_fusion.refs_0_), channel_id=1, source_target_pairs={{0,16},{16,0},{1,17},{17,1},{2,18},{18,2},{3,19},{19,3},{4,20},{20... | collective-permute-start | bytes 786440 | tf_op jit(solution)/shard_map/ppermute | solution.py:390
  74.6 7.9 %collective-permute-start.31 = (bf16[64,512]{1,0:T(8,128)(2,1)S(1)}, bf16[64,512]{1,0:T(8,128)(2,1)S(1)}, u32[]{:S(2)}, u32[]{:S(2)}) collective-permute-start(bf16[64,512]{1,0:T(8,128)(2,1)S(1)} %get-tuple-element.60), channel_id=1, source_target_pairs={{0,8},{2,10},{4,12},{6,14},{8,0},{10,2},{12,4},{14,6},{1,9},{3,11}... | collective-permute-start | bytes 196616 | tf_op jit(solution)/shard_map/ppermute | solution.py:347
  76.4 6.6 %collective-permute-start.32 = (bf16[64,512]{1,0:T(8,128)(2,1)S(1)}, bf16[64,512]{1,0:T(8,128)(2,1)S(1)}, u32[]{:S(2)}, u32[]{:S(2)}) collective-permute-start(bf16[64,512]{1,0:T(8,128)(2,1)S(1)} %get-tuple-element.61), channel_id=1, source_target_pairs={{0,12},{2,14},{4,8},{6,10},{8,4},{10,6},{12,0},{14,2},{1,13},{3,15... | collective-permute-start | bytes 196616 | tf_op jit(solution)/shard_map/ppermute | solution.py:347
  77.4 7.2 %collective-permute-start.33 = (bf16[64,512]{1,0:T(8,128)(2,1)S(1)}, bf16[64,512]{1,0:T(8,128)(2,1)S(1)}, u32[]{:S(2)}, u32[]{:S(2)}) collective-permute-start(bf16[64,512]{1,0:T(8,128)(2,1)S(1)} %get-tuple-element.62), channel_id=1, source_target_pairs={{0,4},{2,6},{4,0},{6,2},{8,12},{10,14},{12,8},{14,10},{1,5},{3,7},... | collective-permute-start | bytes 196616 | tf_op jit(solution)/shard_map/ppermute | solution.py:347
  78.1 6.9 %collective-permute-start.34 = (bf16[64,512]{1,0:T(8,128)(2,1)S(1)}, bf16[64,512]{1,0:T(8,128)(2,1)S(1)}, u32[]{:S(2)}, u32[]{:S(2)}) collective-permute-start(bf16[64,512]{1,0:T(8,128)(2,1)S(1)} %get-tuple-element.63.refs_0_), channel_id=1, source_target_pairs={{0,2},{2,0},{4,6},{6,4},{8,10},{10,8},{12,14},{14,12},{1,3},{3,1},... | collective-permute-start | bytes 196616 | tf_op jit(solution)/shard_map/ppermute | solution.py:347
  82.5 4.6 %collective-permute-start.35 = (bf16[64,512]{1,0:T(8,128)(2,1)S(1)}, bf16[64,512]{1,0:T(8,128)(2,1)S(1)}, u32[]{:S(2)}, u32[]{:S(2)}) collective-permute-start(bf16[64,512]{1,0:T(8,128)(2,1)S(1)} %collective-permute-done.31.refs_1_), channel_id=1, source_target_pairs={{0,2},{2,0},{4,6},{6,4},{8,10},{10,8},{12,14},{14,12},{1,3},{3,1},... | collective-permute-start | bytes 196616 | tf_op jit(solution)/shard_map/ppermute | solution.py:347
  83.0 5.3 %collective-permute-start.36 = (bf16[64,512]{1,0:T(8,128)(2,1)S(1)}, bf16[64,512]{1,0:T(8,128)(2,1)S(1)}, u32[]{:S(2)}, u32[]{:S(2)}) collective-permute-start(bf16[64,512]{1,0:T(8,128)(2,1)S(1)} %collective-permute-done.32.refs_2_), channel_id=1, source_target_pairs={{0,2},{2,0},{4,6},{6,4},{8,10},{10,8},{12,14},{14,12},{1,3},{3,1},... | collective-permute-start | bytes 196616 | tf_op jit(solution)/shard_map/ppermute | solution.py:347
  84.5 4.5 %collective-permute-start.37 = (bf16[64,512]{1,0:T(8,128)(2,1)S(1)}, bf16[64,512]{1,0:T(8,128)(2,1)S(1)}, u32[]{:S(2)}, u32[]{:S(2)}) collective-permute-start(bf16[64,512]{1,0:T(8,128)(2,1)S(1)} %collective-permute-done.33.refs_3_), channel_id=1, source_target_pairs={{0,2},{2,0},{4,6},{6,4},{8,10},{10,8},{12,14},{14,12},{1,3},{3,1},... | collective-permute-start | bytes 196616 | tf_op jit(solution)/shard_map/ppermute | solution.py:347
  89.6 9.4 %collective-permute-start.39 = (bf16[64,512]{1,0:T(8,128)(2,1)S(1)}, bf16[64,512]{1,0:T(8,128)(2,1)S(1)}, u32[]{:S(2)}, u32[]{:S(2)}) collective-permute-start(bf16[64,512]{1,0:T(8,128)(2,1)S(1)} %get-tuple-element.72), channel_id=1, source_target_pairs={{0,16},{16,0},{1,17},{17,1},{2,18},{18,2},{3,19},{19,3},{4,20},{20... | collective-permute-start | bytes 196616 | tf_op jit(solution)/shard_map/ppermute | solution.py:390
  96.3 7.4 %collective-permute-start.44 = (bf16[64,512]{1,0:T(8,128)(2,1)S(1)}, bf16[64,512]{1,0:T(8,128)(2,1)S(1)}, u32[]{:S(2)}, u32[]{:S(2)}) collective-permute-start(bf16[64,512]{1,0:T(8,128)(2,1)S(1)} %get-tuple-element.78), channel_id=1, source_target_pairs={{0,16},{16,0},{1,17},{17,1},{2,18},{18,2},{3,19},{19,3},{4,20},{20... | collective-permute-start | bytes 196616 | tf_op jit(solution)/shard_map/ppermute | solution.py:390
  99.0 8.4 %collective-permute-start.43 = (bf16[64,512]{1,0:T(8,128)(2,1)S(1)}, bf16[64,512]{1,0:T(8,128)(2,1)S(1)}, u32[]{:S(2)}, u32[]{:S(2)}) collective-permute-start(bf16[64,512]{1,0:T(8,128)(2,1)S(1)} %broadcast_select_fusion.3), channel_id=1, source_target_pairs={{0,8},{2,10},{4,12},{6,14},{8,0},{10,2},{12,4},{14,6},{1,9},{3,11}... | collective-permute-start | bytes 196616 | tf_op jit(solution)/shard_map/ppermute | solution.py:347
  103.7 6.2 %collective-permute-start.45 = (bf16[64,512]{1,0:T(8,128)(2,1)S(1)}, bf16[64,512]{1,0:T(8,128)(2,1)S(1)}, u32[]{:S(2)}, u32[]{:S(2)}) collective-permute-start(bf16[64,512]{1,0:T(8,128)(2,1)S(1)} %broadcast_select_fusion), channel_id=1, source_target_pairs={{0,12},{2,14},{4,8},{6,10},{8,4},{10,6},{12,0},{14,2},{1,13},{3,15... | collective-permute-start | bytes 196616 | tf_op jit(solution)/shard_map/ppermute | solution.py:347
  105.9 4.6 %collective-permute-start.42 = (bf16[64,512]{1,0:T(8,128)(2,1)S(1)}, bf16[64,512]{1,0:T(8,128)(2,1)S(1)}, u32[]{:S(2)}, u32[]{:S(2)}) collective-permute-start(bf16[64,512]{1,0:T(8,128)(2,1)S(1)} %broadcast_select_fusion.1), channel_id=1, source_target_pairs={{0,4},{2,6},{4,0},{6,2},{8,12},{10,14},{12,8},{14,10},{1,5},{3,7},... | collective-permute-start | bytes 196616 | tf_op jit(solution)/shard_map/ppermute | solution.py:347
  (21 other events, 111.8 us)

commit v2 on v1

--- a/solution.py
+++ b/solution.py
@@ -43,50 +43,65 @@
     return jnp.concatenate([x[start : start + inner] for start in starts], axis=0)
 
 
-def attention_update(xs, groups, gain, scale_of, w_in, w_out, mask):
-    rows, width = xs[0].shape
-    normed = row_norm(xs[0], gain)
-    seen = jnp.concatenate([normed] + [row_norm(t, gain) for t in xs[1:]], axis=0)
-    same = same_head()
+def queries(normed, scale_of, w_in):
+    width = normed.shape[1]
     head = lax.broadcasted_iota(jnp.int32, (1, width), 1) // HEAD_DIM
     scale = jnp.zeros((1, width), jnp.float32)
     for n in range(HEADS):
         scale = jnp.where(head == n, scale_of(n) * (LOG2E / HEAD_DIM), scale)
     q = matmul(normed, w_in[:, :width])
-    k = matmul(seen, w_in[:, width : 2 * width])
-    v = matmul(seen, w_in[:, 2 * width :]).astype(jnp.bfloat16)
-    q = (q * head_factor(q, same) * scale).astype(jnp.bfloat16)
-    k = (k * head_factor(k, same)).astype(jnp.bfloat16)
+    return (q * head_factor(q, same_head()) * scale).astype(jnp.bfloat16)
+
+
+def keys_and_values(normed, w_in):
+    width = normed.shape[1]
+    k = matmul(normed, w_in[:, width : 2 * width])
+    v = matmul(normed, w_in[:, 2 * width :]).astype(jnp.bfloat16)
+    return (k * head_factor(k, same_head())).astype(jnp.bfloat16), v
+
+
+def attention_sums(q, k, v, groups, mask):
+    rows, width = q.shape
     pair = 2 * HEAD_DIM
     size = rows // groups
+    sets = k.shape[0] // rows
+    keys = size * sets
     first = lax.broadcasted_iota(jnp.int32, (1, pair), 1) < HEAD_DIM
     low = jnp.where(first, 1.0, 0.0).astype(jnp.bfloat16)
     high = jnp.where(first, 0.0, 1.0).astype(jnp.bfloat16)
-    keys = size * len(xs)
     low_all = jnp.broadcast_to(low, (keys, pair))
     high_all = jnp.broadcast_to(high, (keys, pair))
-    done = []
+    both = jnp.concatenate([mask, mask], axis=1)
+    out = []
     for g in range(groups):
         q_g = q[g * size : (g + 1) * size]
-        spans = [slice(i * rows + g * size, i * rows + (g + 1) * size) for i in range(len(xs))]
+        spans = [slice(i * rows + g * size, i * rows + (g + 1) * size) for i in range(sets)]
         k_g = jnp.concatenate([k[span] for span in spans], axis=0)
         v_g = jnp.concatenate([v[span] for span in spans], axis=0)
         parts = []
         for start in range(0, width, pair):
             q2, k2, v2 = (t[:, start : start + pair] for t in (q_g, k_g, v_g))
-            powers = []
-            for side in (low, high):
-                scores = lax.dot_general(
-                    q2 * side, k2, (((1,), (1,)), ((), ())), preferred_element_type=jnp.float32
-                )
-                powers.append(jnp.exp2(scores).astype(jnp.bfloat16) * mask)
-            powers = jnp.concatenate(powers, axis=1)
+            scores = lax.dot_general(
+                q2,
+                jnp.concatenate([k2 * low, k2 * high], axis=0),
+                (((1,), (1,)), ((), ())),
+                preferred_element_type=jnp.float32,
+            )
+            powers = jnp.exp2(scores).astype(jnp.bfloat16) * both
             upper = jnp.concatenate([v2 * low, low_all], axis=1)
             lower = jnp.concatenate([v2 * high, high_all], axis=1)
-            sums = matmul(powers, jnp.concatenate([upper, lower], axis=0))
-            parts.append((sums[:, :pair] / sums[:, pair:]).astype(jnp.bfloat16))
-        done.append(jnp.concatenate(parts, axis=1))
-    return matmul(jnp.concatenate(done, axis=0), w_out[...])
+            parts.append(matmul(powers, jnp.concatenate([upper, lower], axis=0)))
+        out.append(parts)
+    return out
+
+
+def projected(sums, w_out):
+    pair = 2 * HEAD_DIM
+    rows = [
+        jnp.concatenate([(t[:, :pair] / t[:, pair:]).astype(jnp.bfloat16) for t in parts], axis=1)
+        for parts in sums
+    ]
+    return matmul(jnp.concatenate(rows, axis=0), w_out[...])
 
 
 def rounded(x):
@@ -177,70 +192,97 @@
         mine = digits(shape, 0, inner)[0]
         theirs = digits(shape, 1, inner)[0]
         mask = jnp.where(mine == theirs, 1.0, 0.0).astype(jnp.bfloat16)
-        update = attention_update(
-            xs,
-            groups,
-            gain_ref[0, 0:1, :],
-            lambda n: scale_ref[0, 0, n],
-            w_in_ref.at[0, 0],
-            w_out_ref.at[0, 0],
-            mask,
-        )
+        normed = [row_norm(x, gain_ref[0, 0:1, :]) for x in xs]
+        w_in = w_in_ref.at[0, 0]
+        q = queries(normed[0], lambda n: scale_ref[0, 0, n], w_in)
+        k, v = keys_and_values(jnp.concatenate(normed, axis=0), w_in)
+        update = projected(attention_sums(q, k, v, groups, mask), w_out_ref.at[0, 0])
         y = regrouped(xs[0] + update, rows // (groups * inner), inner).astype(jnp.bfloat16)
         size = rows // shards
         for k in range(shards):
             y_refs[k][...] = y[k * size : (k + 1) * size]
 
 
-def patch_kernel(sizes, step, micro, place_ref, seen_ref, *refs):
+def hour_groups(sizes):
+    _, _, patches, hl = sizes
+    groups = 2 if hl % 2 == 0 else 1
+    return groups, hl // groups * patches
+
+
+def patch_mask(sizes, fast, others, place_ref, seen_ref):
     slow, _, patches, hl = sizes
-    count = len(refs) - 6 - slow
-    pieces = pieces_of([0] + [k for k in far_first(slow) if k])
-    fast = count // len(pieces)
-    x_refs, (gain_ref, scale_ref, w_in_ref, w_out_ref, up_ref, down_ref), y_refs = (
-        refs[:count],
-        refs[count : count + 6],
-        refs[count + 6 :],
+    groups, inner = hour_groups(sizes)
+    size = slow * inner
+    shape = (size, size * len(others))
+
+    def block_and_hour(dimension, first):
+        patch, late, offset, other = digits(shape, dimension, patches, hl // groups, slow)
+        shard = (offset ^ place_ref[1]) * fast + ((other + first) ^ place_ref[2])
+        return (shard * patches + patch) // PB, late
+
+    query_block, query_hour = block_and_hour(0, 0)
+    key_block, key_hour = block_and_hour(1, others[0])
+    seen = None
+    for kv in range(seen_ref.shape[1]):
+        chosen = jnp.full(shape, seen_ref[0, kv], jnp.int32)
+        for b in range(1, seen_ref.shape[0]):
+            chosen = jnp.where(query_block == b, seen_ref[b, kv], chosen)
+        hit = jnp.where(chosen == key_block, 1.0, 0.0)
+        seen = hit if seen is None else jnp.maximum(seen, hit)
+    return jnp.where(query_hour == key_hour, seen, 0.0).astype(jnp.bfloat16)
+
+
+def own_patch_kernel(sizes, fast, step, micro, place_ref, seen_ref, *refs):
+    slow = sizes[0]
+    x_refs, (gain_ref, scale_ref, w_in_ref), (q_ref, sums_ref) = (
+        refs[:slow],
+        refs[slow : slow + 3],
+        refs[slow + 3 :],
     )
 
     @pl.when(at_work(place_ref, step, micro))
     def _():
+        groups, inner = hour_groups(sizes)
+        x = jnp.concatenate([ref[...] for ref in x_refs], axis=0).astype(jnp.float32)
+        normed = row_norm(regrouped(x, groups, inner), gain_ref[0, 1:2, :])
+        w_in = w_in_ref.at[0, 1]
+        q = queries(normed, lambda n: scale_ref[0, 1, n], w_in)
+        k, v = keys_and_values(normed, w_in)
+        q_ref[...] = q
+        mask = patch_mask(sizes, fast, [0], place_ref, seen_ref)
+        sums = attention_sums(q, k, v, groups, mask)
+        sums_ref[...] = jnp.concatenate([jnp.concatenate(t, axis=1) for t in sums], axis=0)
+
+
+def patch_kernel(sizes, fast, step, micro, place_ref, seen_ref, *refs):
+    slow = sizes[0]
+    count = fast * slow
+    x_refs, refs, y_refs = refs[:count], refs[count:-slow], refs[-slow:]
+    q_ref, sums_ref, gain_ref, w_in_ref, w_out_ref, up_ref, down_ref = refs
+    pieces = pieces_of([0] + [k for k in far_first(slow) if k])
+
+    @pl.when(at_work(place_ref, step, micro))
+    def _():
+        groups, inner = hour_groups(sizes)
         xs = [
-            jnp.concatenate(blocks, axis=0).astype(jnp.float32)
+            regrouped(jnp.concatenate(blocks, axis=0).astype(jnp.float32), groups, inner)
             for blocks in row_sets(x_refs, slow, pieces)
         ]
-        rows = xs[0].shape[0]
-        groups = 2 if hl % 2 == 0 else 1
-        inner = hl // groups * patches
-        xs = [regrouped(x, groups, inner) for x in xs]
         x = xs[0]
-        shape = (rows // groups, rows // groups * fast)
-
-        def block_and_hour(dimension):
-            patch, late, offset, other = digits(shape, dimension, patches, hl // groups, slow)
-            shard = (offset ^ place_ref[1]) * fast + (other ^ place_ref[2])
-            return (shard * patches + patch) // PB, late
-
-        query_block, query_hour = block_and_hour(0)
-        key_block, key_hour = block_and_hour(1)
-        seen = None
-        for kv in range(seen_ref.shape[1]):
-            chosen = jnp.full(shape, seen_ref[0, kv], jnp.int32)
-            for b in range(1, seen_ref.shape[0]):
-                chosen = jnp.where(query_block == b, seen_ref[b, kv], chosen)
-            hit = jnp.where(chosen == key_block, 1.0, 0.0)
-            seen = hit if seen is None else jnp.maximum(seen, hit)
-        mask = jnp.where(query_hour == key_hour, seen, 0.0).astype(jnp.bfloat16)
-        update = attention_update(
-            xs,
-            groups,
-            gain_ref[0, 1:2, :],
-            lambda n: scale_ref[0, 1, n],
-            w_in_ref.at[0, 1],
-            w_out_ref.at[0, 1],
-            mask,
-        )
-        x = rounded(x + update)
+        rows, width = x.shape
+        normed = jnp.concatenate([row_norm(t, gain_ref[0, 1:2, :]) for t in xs[1:]], axis=0)
+        k, v = keys_and_values(normed, w_in_ref.at[0, 1])
+        mask = patch_mask(sizes, fast, range(1, fast), place_ref, seen_ref)
+        more = attention_sums(q_ref[...], k, v, groups, mask)
+        size = rows // groups
+        sums = [
+            [
+                t + sums_ref[g * size : (g + 1) * size, i * 256 : (i + 1) * 256]
+                for i, t in enumerate(parts)
+            ]
+            for g, parts in enumerate(more)
+        ]
+        x = rounded(x + projected(sums, w_out_ref.at[0, 1]))
         normed = row_norm(x, gain_ref[0, 2:3, :])
         total = x
         chunk = 512
@@ -316,17 +358,33 @@
     )(place, *xs, gains, scales, w_in, w_out)
 
 
-def call_patch(sizes, step, micro, shape, place, seen, xs, gains, scales, w_in, w_out, w_up, w_down):
+def call_own_patch(sizes, fast, step, micro, shape, place, seen, xs, gains, scales, w_in):
     rows, width = shape
     return pl.pallas_call(
-        functools.partial(patch_kernel, sizes, step, micro),
+        functools.partial(own_patch_kernel, sizes, fast, step, micro),
+        out_shape=[
+            jax.ShapeDtypeStruct((rows, width), jnp.bfloat16),
+            jax.ShapeDtypeStruct((rows, 2 * width), jnp.float32),
+        ],
+        in_specs=[SMEM, SMEM] + [VMEM] * len(xs) + [VMEM, SMEM, VMEM],
+        out_specs=[VMEM, VMEM],
+        compiler_params=PARAMS,
+        cost_estimate=COST,
+        name="own_patch_attention",
+    )(place, seen, *xs, gains, scales, w_in)
+
+
+def call_patch(sizes, fast, step, micro, shape, place, seen, xs, weights):
+    rows, width = shape
+    return pl.pallas_call(
+        functools.partial(patch_kernel, sizes, fast, step, micro),
         out_shape=blocks_of(sizes[0], rows, width),
-        in_specs=[SMEM, SMEM] + [VMEM] * len(xs) + [VMEM, SMEM] + [VMEM] * 4,
+        in_specs=[SMEM, SMEM] + [VMEM] * (len(xs) + len(weights)),
         out_specs=[VMEM] * sizes[0],
         compiler_params=PARAMS,
         cost_estimate=COST,
         name="patch_attention_and_ffn",
-    )(place, seen, *xs, gains, scales, w_in, w_out, w_up, w_down)
+    )(place, seen, *xs, *weights)
 
 
 def call_write(kernel, sizes, place, shape, number, xs, out):
@@ -396,29 +454,21 @@
     back = []
     for step in range(micro + pipes - 1):
         now = given if step < micro else []
-        mixed = call_time(sizes, step, micro, x.shape[1:], place, order, now, came, gains, scales, w_in, w_out)
+        mixed = call_time(
+            sizes, step, micro, x.shape[1:], place, order, now, came, gains, scales, w_in, w_out
+        )
         own = along_slow(mixed, in_stage, 1)
         spread = gathered(own, "patch", fast, [0] + [k for k in far if k])
+        begun = call_own_patch(
+            sizes, fast, step, micro, x.shape[1:], place, seen, own, gains, scales, w_in
+        )
         if back:
-            spread, back = lax.optimization_barrier((spread, back))
             write = functools.partial(early_kernel, sizes, pipes)
             out = call_write(write, sizes, place, x.shape, step - pipes, back, out)
+            spread, out = lax.optimization_barrier((spread, out))
         at_end = step == micro + pipes - 2
-        done = call_patch(
-            sizes,
-            step,
-            micro,
-            x.shape[1:],
-            place,
-            seen,
-            spread,
-            gains,
-            scales,
-            w_in,
-            w_out,
-            w_up,
-            w_down,
-        )
+        weights = [*begun, gains, w_in, w_out, w_up, w_down]
+        done = call_patch(sizes, fast, step, micro, x.shape[1:], place, seen, spread, weights)
         if not at_end:
             arrived = along_slow(done, handed_on, 0)
             came = gathered(arrived, "hour", peers, far)

time: 112 us -> 110 us (0.982)
  waiting for transfers between devices: 37.2 us -> 30 us
  Pallas kernels: 20.1 us -> 22.8 us
  starting transfers between devices: 52.3 us -> 54.2 us
    ppermute x33, waiting for transfers between devices: 25.6 us -> 15.8 us  [flipped(): lax.ppermute(x, axis, [(s, s ^ k) for s in range(lax.axis_size(axis))])]
    pallas_call x3 -> x6, Pallas kernels: 10.1 us -> 12.8 us  [the longest x3 8.22 us: call_patch(): pl.pallas_call(functools.partial(patch_kernel, sizes, fast, step, micro),...]
    ppermute x5, waiting for transfers between devices: 2.65 us -> 5.09 us  [onward(): return lax.ppermute(x, 'pipe', [(s, (s + 1) % pipes) for s in range(pipes)])]
    ppermute x5, starting transfers between devices: 9.39 us -> 10.6 us  [onward(): return lax.ppermute(x, 'pipe', [(s, (s + 1) % pipes) for s in range(pipes)])]
  transfers between devices with their start and end apart: 46 -> 46, of which waited for: 30 -> 27; matrix products, arithmetic and copies ran while one was open for 1% -> 1% of each run, Pallas kernels for 2% -> 6%
where the time goes in v2:
time: 110 us; the launch traced here: 109 us
  starting transfers between devices  54.2 us (49%)
  waiting for transfers between devices  30 us (27%)
  Pallas kernels  22.8 us (21%)
  local copies, waits for them, and re-layouts  2.07 us (2%)
    ppermute x33, starting transfers between devices, flipped(): lax.ppermute(x, axis, [(s, s ^ k) for s in range(lax.axis_size(axis))])  31.7 us
    ppermute x33, waiting for transfers between devices, flipped(): lax.ppermute(x, axis, [(s, s ^ k) for s in range(lax.axis_size(axis))])  15.8 us
    ppermute x8, starting transfers between devices, handed_on(): return lax.ppermute(x, ('pipe', 'patch'), pairs)  11.8 us
    ppermute x5, starting transfers between devices, onward(): return lax.ppermute(x, 'pipe', [(s, (s + 1) % pipes) for s in range(pipes)])  10.6 us
    ppermute x8, waiting for transfers between devices, handed_on(): return lax.ppermute(x, ('pipe', 'patch'), pairs)  9.08 us
    pallas_call x3, Pallas kernels, call_patch(): pl.pallas_call(functools.partial(patch_kernel, sizes, fast, step, micro),...  8.22 us
    pallas_call x3, Pallas kernels, call_time(): pl.pallas_call(functools.partial(time_kernel, sizes, step, micro), out_sh...  6.39 us
    ppermute x5, waiting for transfers between devices, onward(): return lax.ppermute(x, 'pipe', [(s, (s + 1) % pipes) for s in range(pipes)])  5.09 us
  transfers between devices with their start and end apart: 46, of which 27 were waited for; matrix products, arithmetic and copies ran while one was open for 1% of the time, Pallas kernels for 6%

profile of v2, /device:TPU:0, one launch (start us, length us, event | category | flops | bytes accessed | tf_op | source)
XLA Modules:
  0.0 109.4 jit_solution(17091016762020939037)
XLA Ops:
  3.5 2.9 %time_attention.3 = (bf16[64,512]{1,0:T(8,128)(2,1)S(1)}, bf16[64,512]{1,0:T(8,128)(2,1)S(1)}, bf16[64,512]{1,0:T(8,128)(2,1)S(1)}, bf16[64,512]{1,0:T(8,128)(2,1)S(1)}) custom-call(s32[3]{0:T(128)S(1)} %pad_add_fusion.place_ref, bf16[256,256]{1,0:T(8,128)(2,1)S(1)} %input_order.1.refs_0_, bf16[2,256,512]{2,1,0:T(8,128)(2,1)S(1)} %bitcast.6, ...), custom_call_target="tpu_custom_call" | custom-call | flops 5368709120 | bytes 1048576 | tf_op jit(solution)/shard_map/time_attention/pallas_call | solution.py:349
  6.5 3.6 %collective-permute-start.1 = (bf16[64,512]{1,0:T(8,128)(2,1)S(1)}, bf16[64,512]{1,0:T(8,128)(2,1)S(1)}, u32[]{:S(2)}, u32[]{:S(2)}) collective-permute-start(bf16[64,512]{1,0:T(8,128)(2,1)S(1)} %get-tuple-element.49), channel_id=1, source_target_pairs={{0,8},{2,10},{4,12},{6,14},{8,0},{10,2},{12,4},{14,6},{1,9},{3,11}... | collective-permute-start | bytes 196616 | tf_op jit(solution)/shard_map/ppermute | solution.py:405
  10.1 1.3 %collective-permute-start.2 = (bf16[64,512]{1,0:T(8,128)(2,1)S(1)}, bf16[64,512]{1,0:T(8,128)(2,1)S(1)}, u32[]{:S(2)}, u32[]{:S(2)}) collective-permute-start(bf16[64,512]{1,0:T(8,128)(2,1)S(1)} %get-tuple-element.50), channel_id=1, source_target_pairs={{0,12},{2,14},{4,8},{6,10},{8,4},{10,6},{12,0},{14,2},{1,13},{3,15... | collective-permute-start | bytes 196616 | tf_op jit(solution)/shard_map/ppermute | solution.py:405
  11.7 1.5 %collective-permute-start.4 = (bf16[64,512]{1,0:T(8,128)(2,1)S(1)}, bf16[64,512]{1,0:T(8,128)(2,1)S(1)}, u32[]{:S(2)}, u32[]{:S(2)}) collective-permute-start(bf16[64,512]{1,0:T(8,128)(2,1)S(1)} %get-tuple-element.48.refs_0_), channel_id=1, source_target_pairs={{0,2},{2,0},{4,6},{6,4},{8,10},{10,8},{12,14},{14,12},{1,3},{3,1},... | collective-permute-start | bytes 196616 | tf_op jit(solution)/shard_map/ppermute | solution.py:405
  14.4 1.6 %collective-permute-start.5 = (bf16[64,512]{1,0:T(8,128)(2,1)S(1)}, bf16[64,512]{1,0:T(8,128)(2,1)S(1)}, u32[]{:S(2)}, u32[]{:S(2)}) collective-permute-start(bf16[64,512]{1,0:T(8,128)(2,1)S(1)} %collective-permute-done.1.refs_2_.refs_1_), channel_id=1, source_target_pairs={{0,2},{2,0},{4,6},{6,4},{8,10},{10,8},{12,14},{14,12},{1,3},{3,1},... | collective-permute-start | bytes 196616 | tf_op jit(solution)/shard_map/ppermute | solution.py:405
  16.8 1.5 %collective-permute-start.6 = (bf16[64,512]{1,0:T(8,128)(2,1)S(1)}, bf16[64,512]{1,0:T(8,128)(2,1)S(1)}, u32[]{:S(2)}, u32[]{:S(2)}) collective-permute-start(bf16[64,512]{1,0:T(8,128)(2,1)S(1)} %collective-permute-done.2.refs_3_.refs_2_), channel_id=1, source_target_pairs={{0,2},{2,0},{4,6},{6,4},{8,10},{10,8},{12,14},{14,12},{1,3},{3,1},... | collective-permute-start | bytes 196616 | tf_op jit(solution)/shard_map/ppermute | solution.py:405
  18.9 2.0 %own_patch_attention.3 = (bf16[256,512]{1,0:T(8,128)(2,1)S(1)}, f32[256,1024]{1,0:T(8,128)S(1)}) custom-call(s32[3]{0:T(128)S(1)} %pad_add_fusion.place_ref, s32[2,2]{1,0:T(2,128)S(1)} %copy-done.6, bf16[64,512]{1,0:T(8,128)(2,1)S(1)} %get-tuple-element.48.refs_0_, bf16[64,512]{1,0:T(8,128)(2,1)S(1)} %collective-permute-done.3.refs_1_.refs_3_, ...), custom_call_target="tpu_custom_call" | custom-call | flops 5368709120 | bytes 1048576 | tf_op jit(solution)/shard_map/own_patch_attention/pallas_call | solution.py:363
  21.1 1.5 %collective-permute-done.7.refs_7_ = bf16[64,512]{1,0:T(8,128)(2,1)S(1)} collective-permute-done((bf16[64,512]{1,0:T(8,128)(2,1)S(1)}, bf16[64,512]{1,0:T(8,128)(2,1)S(1)}, u32[]{:S(2)}, u32[]{:S(2)}) %collective-permute-start.7) | collective-permute-done | bytes 65568 | tf_op jit(solution)/shard_map/ppermute | solution.py:405
  22.6 3.8 %patch_attention_and_ffn.3 = (bf16[64,512]{1,0:T(8,128)(2,1)S(1)}, bf16[64,512]{1,0:T(8,128)(2,1)S(1)}, bf16[64,512]{1,0:T(8,128)(2,1)S(1)}, bf16[64,512]{1,0:T(8,128)(2,1)S(1)}) custom-call(s32[3]{0:T(128)S(1)} %pad_add_fusion.place_ref, s32[2,2]{1,0:T(2,128)S(1)} %copy-done.6, bf16[64,512]{1,0:T(8,128)(2,1)S(1)} %get-tuple-element.48.refs_0_, ...), custom_call_target="tpu_custom_call" | custom-call | flops 5368709120 | bytes 1048576 | tf_op jit(solution)/shard_map/patch_attention_and_ffn/pallas_call | solution.py:379
  26.4 4.3 %collective-permute-start.9 = (bf16[64,512]{1,0:T(8,128)(2,1)S(1)}, bf16[64,512]{1,0:T(8,128)(2,1)S(1)}, u32[]{:S(2)}, u32[]{:S(2)}) collective-permute-start(bf16[64,512]{1,0:T(8,128)(2,1)S(1)} %get-tuple-element.55), channel_id=1, source_target_pairs={{0,28},{2,30},{4,24},{6,26},{8,20},{10,22},{12,16},{14,18},{16,12}... | collective-permute-start | bytes 196616 | tf_op jit(solution)/shard_map/ppermute | solution.py:415
  32.3 1.8 %collective-permute-done.8.refs_3_ = bf16[64,512]{1,0:T(8,128)(2,1)S(1)} collective-permute-done((bf16[64,512]{1,0:T(8,128)(2,1)S(1)}, bf16[64,512]{1,0:T(8,128)(2,1)S(1)}, u32[]{:S(2)}, u32[]{:S(2)}) %collective-permute-start.8) | collective-permute-done | bytes 65568 | tf_op jit(solution)/shard_map/ppermute | solution.py:415
  35.4 1.5 %collective-permute-done.11.refs_6_ = bf16[64,512]{1,0:T(8,128)(2,1)S(1)} collective-permute-done((bf16[64,512]{1,0:T(8,128)(2,1)S(1)}, bf16[64,512]{1,0:T(8,128)(2,1)S(1)}, u32[]{:S(2)}, u32[]{:S(2)}) %collective-permute-start.11) | collective-permute-done | bytes 65568 | tf_op jit(solution)/shard_map/ppermute | solution.py:415
  38.2 2.9 %time_attention.4 = (bf16[64,512]{1,0:T(8,128)(2,1)S(1)}, bf16[64,512]{1,0:T(8,128)(2,1)S(1)}, bf16[64,512]{1,0:T(8,128)(2,1)S(1)}, bf16[64,512]{1,0:T(8,128)(2,1)S(1)}) custom-call(s32[3]{0:T(128)S(1)} %pad_add_fusion.place_ref, bf16[256,256]{1,0:T(8,128)(2,1)S(1)} %input_order.1.refs_0_, bf16[2,256,512]{2,1,0:T(8,128)(2,1)S(1)} %bitcast.7, ...), custom_call_target="tpu_custom_call" | custom-call | flops 5368709120 | bytes 1048576 | tf_op jit(solution)/shard_map/time_attention/pallas_call | solution.py:349
  41.1 2.8 %collective-permute-start.16 = (bf16[64,512]{1,0:T(8,128)(2,1)S(1)}, bf16[64,512]{1,0:T(8,128)(2,1)S(1)}, u32[]{:S(2)}, u32[]{:S(2)}) collective-permute-start(bf16[64,512]{1,0:T(8,128)(2,1)S(1)} %get-tuple-element.59), channel_id=1, source_target_pairs={{0,8},{2,10},{4,12},{6,14},{8,0},{10,2},{12,4},{14,6},{1,9},{3,11}... | collective-permute-start | bytes 196616 | tf_op jit(solution)/shard_map/ppermute | solution.py:405
  45.0 1.3 %collective-permute-start.19 = (bf16[64,512]{1,0:T(8,128)(2,1)S(1)}, bf16[64,512]{1,0:T(8,128)(2,1)S(1)}, u32[]{:S(2)}, u32[]{:S(2)}) collective-permute-start(bf16[64,512]{1,0:T(8,128)(2,1)S(1)} %get-tuple-element.58.refs_0_), channel_id=1, source_target_pairs={{0,2},{2,0},{4,6},{6,4},{8,10},{10,8},{12,14},{14,12},{1,3},{3,1},... | collective-permute-start | bytes 196616 | tf_op jit(solution)/shard_map/ppermute | solution.py:405
  46.3 2.8 %collective-permute-done.16.refs_2_.refs_1_ = bf16[64,512]{1,0:T(8,128)(2,1)S(1)} collective-permute-done((bf16[64,512]{1,0:T(8,128)(2,1)S(1)}, bf16[64,512]{1,0:T(8,128)(2,1)S(1)}, u32[]{:S(2)}, u32[]{:S(2)}) %collective-permute-start.16) | collective-permute-done | bytes 65568 | tf_op jit(solution)/shard_map/ppermute | solution.py:405
  52.4 2.0 %own_patch_attention.4 = (bf16[256,512]{1,0:T(8,128)(2,1)S(1)}, f32[256,1024]{1,0:T(8,128)S(1)}) custom-call(s32[3]{0:T(128)S(1)} %pad_add_fusion.place_ref, s32[2,2]{1,0:T(2,128)S(1)} %copy-done.6, bf16[64,512]{1,0:T(8,128)(2,1)S(1)} %get-tuple-element.58.refs_0_, bf16[64,512]{1,0:T(8,128)(2,1)S(1)} %collective-permute-done.18.refs_1_.refs_3_, ...), custom_call_target="tpu_custom_call" | custom-call | flops 5368709120 | bytes 1048576 | tf_op jit(solution)/shard_map/own_patch_attention/pallas_call | solution.py:363
  55.9 3.9 %patch_attention_and_ffn.4 = (bf16[64,512]{1,0:T(8,128)(2,1)S(1)}, bf16[64,512]{1,0:T(8,128)(2,1)S(1)}, bf16[64,512]{1,0:T(8,128)(2,1)S(1)}, bf16[64,512]{1,0:T(8,128)(2,1)S(1)}) custom-call(s32[3]{0:T(128)S(1)} %pad_add_fusion.place_ref, s32[2,2]{1,0:T(2,128)S(1)} %copy-done.6, bf16[64,512]{1,0:T(8,128)(2,1)S(1)} %get-tuple-element.58.refs_0_, ...), custom_call_target="tpu_custom_call" | custom-call | flops 5368709120 | bytes 1048576 | tf_op jit(solution)/shard_map/patch_attention_and_ffn/pallas_call | solution.py:379
  59.9 2.8 %collective-permute-start.23 = (bf16[64,512]{1,0:T(8,128)(2,1)S(1)}, bf16[64,512]{1,0:T(8,128)(2,1)S(1)}, u32[]{:S(2)}, u32[]{:S(2)}) collective-permute-start(bf16[64,512]{1,0:T(8,128)(2,1)S(1)} %get-tuple-element.64), channel_id=1, source_target_pairs={{0,24},{2,26},{4,28},{6,30},{8,16},{10,18},{12,20},{14,22},{16,8},... | collective-permute-start | bytes 196616 | tf_op jit(solution)/shard_map/ppermute | solution.py:415
  62.7 1.5 %collective-permute-start.24 = (bf16[64,512]{1,0:T(8,128)(2,1)S(1)}, bf16[64,512]{1,0:T(8,128)(2,1)S(1)}, u32[]{:S(2)}, u32[]{:S(2)}) collective-permute-start(bf16[64,512]{1,0:T(8,128)(2,1)S(1)} %get-tuple-element.65), channel_id=1, source_target_pairs={{0,28},{2,30},{4,24},{6,26},{8,20},{10,22},{12,16},{14,18},{16,12}... | collective-permute-start | bytes 196616 | tf_op jit(solution)/shard_map/ppermute | solution.py:415
  66.9 3.0 %collective-permute-done.24.refs_1_ = bf16[64,512]{1,0:T(8,128)(2,1)S(1)} collective-permute-done((bf16[64,512]{1,0:T(8,128)(2,1)S(1)}, bf16[64,512]{1,0:T(8,128)(2,1)S(1)}, u32[]{:S(2)}, u32[]{:S(2)}) %collective-permute-start.24) | collective-permute-done | bytes 65568 | tf_op jit(solution)/shard_map/ppermute | solution.py:415
  72.8 1.8 %collective-permute-start.31 = (bf16[64,512]{1,0:T(8,128)(2,1)S(1)}, bf16[64,512]{1,0:T(8,128)(2,1)S(1)}, u32[]{:S(2)}, u32[]{:S(2)}) collective-permute-start(bf16[64,512]{1,0:T(8,128)(2,1)S(1)} %get-tuple-element.69), channel_id=1, source_target_pairs={{0,8},{2,10},{4,12},{6,14},{8,0},{10,2},{12,4},{14,6},{1,9},{3,11}... | collective-permute-start | bytes 196616 | tf_op jit(solution)/shard_map/ppermute | solution.py:405
  76.3 2.9 %collective-permute-start.38 = (bf16[256,512]{1,0:T(8,128)(2,1)S(1)}, bf16[256,512]{1,0:T(8,128)(2,1)S(1)}, u32[]{:S(2)}, u32[]{:S(2)}) collective-permute-start(bf16[256,512]{1,0:T(8,128)(2,1)S(1)} %constant_dynamic-update-slice_fusion.refs_0_), channel_id=1, source_target_pairs={{0,16},{16,0},{1,17},{17,1},{2,18},{18,2},{3,19},{19,3},{4,20},{20... | collective-permute-start | bytes 786440 | tf_op jit(solution)/shard_map/ppermute | solution.py:448
  81.2 1.4 %collective-permute-start.36 = (bf16[64,512]{1,0:T(8,128)(2,1)S(1)}, bf16[64,512]{1,0:T(8,128)(2,1)S(1)}, u32[]{:S(2)}, u32[]{:S(2)}) collective-permute-start(bf16[64,512]{1,0:T(8,128)(2,1)S(1)} %collective-permute-done.32.refs_3_.refs_2_), channel_id=1, source_target_pairs={{0,2},{2,0},{4,6},{6,4},{8,10},{10,8},{12,14},{14,12},{1,3},{3,1},... | collective-permute-start | bytes 196616 | tf_op jit(solution)/shard_map/ppermute | solution.py:405
  85.1 1.5 %final_order.2.refs_4_ = bf16[2,256,512]{2,1,0:T(8,128)(2,1)} custom-call(s32[3]{0:T(128)S(1)} %pad_add_fusion.place_ref, bf16[256,512]{1,0:T(8,128)(2,1)S(1)} %constant_dynamic-update-slice_fusion.refs_0_, bf16[256,512]{1,0:T(8,128)(2,1)S(1)} %collective-permute-done.38.refs_1_), custom_call_target="tpu_custom_call" | custom-call | tf_op jit(solution)/shard_map/final_order/pallas_call | solution.py:392
  88.2 5.7 %collective-permute-start.39 = (bf16[64,512]{1,0:T(8,128)(2,1)S(1)}, bf16[64,512]{1,0:T(8,128)(2,1)S(1)}, u32[]{:S(2)}, u32[]{:S(2)}) collective-permute-start(bf16[64,512]{1,0:T(8,128)(2,1)S(1)} %get-tuple-element.83), channel_id=1, source_target_pairs={{0,16},{16,0},{1,17},{17,1},{2,18},{18,2},{3,19},{19,3},{4,20},{20... | collective-permute-start | bytes 196616 | tf_op jit(solution)/shard_map/ppermute | solution.py:448
  94.0 2.7 %collective-permute-done.39 = bf16[64,512]{1,0:T(8,128)(2,1)S(1)} collective-permute-done((bf16[64,512]{1,0:T(8,128)(2,1)S(1)}, bf16[64,512]{1,0:T(8,128)(2,1)S(1)}, u32[]{:S(2)}, u32[]{:S(2)}) %collective-permute-start.39) | collective-permute-done | bytes 65568 | tf_op jit(solution)/shard_map/ppermute | solution.py:448
  96.7 2.3 %collective-permute-start.43 = (bf16[64,512]{1,0:T(8,128)(2,1)S(1)}, bf16[64,512]{1,0:T(8,128)(2,1)S(1)}, u32[]{:S(2)}, u32[]{:S(2)}) collective-permute-start(bf16[64,512]{1,0:T(8,128)(2,1)S(1)} %broadcast_select_fusion.3), channel_id=1, source_target_pairs={{0,8},{2,10},{4,12},{6,14},{8,0},{10,2},{12,4},{14,6},{1,9},{3,11}... | collective-permute-start | bytes 196616 | tf_op jit(solution)/shard_map/ppermute | solution.py:405
  99.0 1.5 %collective-permute-start.41 = (bf16[64,512]{1,0:T(8,128)(2,1)S(1)}, bf16[64,512]{1,0:T(8,128)(2,1)S(1)}, u32[]{:S(2)}, u32[]{:S(2)}) collective-permute-start(bf16[64,512]{1,0:T(8,128)(2,1)S(1)} %get-tuple-element.87), channel_id=1, source_target_pairs={{0,16},{16,0},{1,17},{17,1},{2,18},{18,2},{3,19},{19,3},{4,20},{20... | collective-permute-start | bytes 196616 | tf_op jit(solution)/shard_map/ppermute | solution.py:448
  103.3 1.4 %collective-permute-start.42 = (bf16[64,512]{1,0:T(8,128)(2,1)S(1)}, bf16[64,512]{1,0:T(8,128)(2,1)S(1)}, u32[]{:S(2)}, u32[]{:S(2)}) collective-permute-start(bf16[64,512]{1,0:T(8,128)(2,1)S(1)} %broadcast_select_fusion.1), channel_id=1, source_target_pairs={{0,4},{2,6},{4,0},{6,2},{8,12},{10,14},{12,8},{14,10},{1,5},{3,7},... | collective-permute-start | bytes 196616 | tf_op jit(solution)/shard_map/ppermute | solution.py:405
  104.8 2.4 %collective-permute-done.45.refs_3_ = bf16[64,512]{1,0:T(8,128)(2,1)S(1)} collective-permute-done((bf16[64,512]{1,0:T(8,128)(2,1)S(1)}, bf16[64,512]{1,0:T(8,128)(2,1)S(1)}, u32[]{:S(2)}, u32[]{:S(2)}) %collective-permute-start.45) | collective-permute-done | bytes 65568 | tf_op jit(solution)/shard_map/ppermute | solution.py:405
  107.9 1.5 %final_order.3 = bf16[2,256,512]{2,1,0:T(8,128)(2,1)} custom-call(s32[3]{0:T(128)S(1)} %pad_add_fusion.place_ref, bf16[64,512]{1,0:T(8,128)(2,1)S(1)} %broadcast_select_fusion.2.refs_0_, bf16[64,512]{1,0:T(8,128)(2,1)S(1)} %collective-permute-done.42.refs_1_, bf16[64,512]{1,0:T(8,128)(2,1)S(1)} %collective-permute-done.43.refs_2_, ...), custom_call_target="tpu_custom_call", output_to_operand_aliasing={{}: (5, {})} | custom-call | tf_op jit(solution)/shard_map/final_order/pallas_call | solution.py:392
  (96 shorter events, 33.7 us)
Async XLA Ops:
  6.5 8.0 %collective-permute-start.1 = (bf16[64,512]{1,0:T(8,128)(2,1)S(1)}, bf16[64,512]{1,0:T(8,128)(2,1)S(1)}, u32[]{:S(2)}, u32[]{:S(2)}) collective-permute-start(bf16[64,512]{1,0:T(8,128)(2,1)S(1)} %get-tuple-element.49), channel_id=1, source_target_pairs={{0,8},{2,10},{4,12},{6,14},{8,0},{10,2},{12,4},{14,6},{1,9},{3,11}... | collective-permute-start | bytes 196616 | tf_op jit(solution)/shard_map/ppermute | solution.py:405
  10.1 6.7 %collective-permute-start.2 = (bf16[64,512]{1,0:T(8,128)(2,1)S(1)}, bf16[64,512]{1,0:T(8,128)(2,1)S(1)}, u32[]{:S(2)}, u32[]{:S(2)}) collective-permute-start(bf16[64,512]{1,0:T(8,128)(2,1)S(1)} %get-tuple-element.50), channel_id=1, source_target_pairs={{0,12},{2,14},{4,8},{6,10},{8,4},{10,6},{12,0},{14,2},{1,13},{3,15... | collective-permute-start | bytes 196616 | tf_op jit(solution)/shard_map/ppermute | solution.py:405
  11.4 6.9 %collective-permute-start.3 = (bf16[64,512]{1,0:T(8,128)(2,1)S(1)}, bf16[64,512]{1,0:T(8,128)(2,1)S(1)}, u32[]{:S(2)}, u32[]{:S(2)}) collective-permute-start(bf16[64,512]{1,0:T(8,128)(2,1)S(1)} %get-tuple-element.51), channel_id=1, source_target_pairs={{0,4},{2,6},{4,0},{6,2},{8,12},{10,14},{12,8},{14,10},{1,5},{3,7},... | collective-permute-start | bytes 196616 | tf_op jit(solution)/shard_map/ppermute | solution.py:405
  11.7 9.2 %collective-permute-start.4 = (bf16[64,512]{1,0:T(8,128)(2,1)S(1)}, bf16[64,512]{1,0:T(8,128)(2,1)S(1)}, u32[]{:S(2)}, u32[]{:S(2)}) collective-permute-start(bf16[64,512]{1,0:T(8,128)(2,1)S(1)} %get-tuple-element.48.refs_0_), channel_id=1, source_target_pairs={{0,2},{2,0},{4,6},{6,4},{8,10},{10,8},{12,14},{14,12},{1,3},{3,1},... | collective-permute-start | bytes 196616 | tf_op jit(solution)/shard_map/ppermute | solution.py:405
  14.4 6.4 %collective-permute-start.5 = (bf16[64,512]{1,0:T(8,128)(2,1)S(1)}, bf16[64,512]{1,0:T(8,128)(2,1)S(1)}, u32[]{:S(2)}, u32[]{:S(2)}) collective-permute-start(bf16[64,512]{1,0:T(8,128)(2,1)S(1)} %collective-permute-done.1.refs_2_.refs_1_), channel_id=1, source_target_pairs={{0,2},{2,0},{4,6},{6,4},{8,10},{10,8},{12,14},{14,12},{1,3},{3,1},... | collective-permute-start | bytes 196616 | tf_op jit(solution)/shard_map/ppermute | solution.py:405
  26.4 7.7 %collective-permute-start.8 = (bf16[64,512]{1,0:T(8,128)(2,1)S(1)}, bf16[64,512]{1,0:T(8,128)(2,1)S(1)}, u32[]{:S(2)}, u32[]{:S(2)}) collective-permute-start(bf16[64,512]{1,0:T(8,128)(2,1)S(1)} %get-tuple-element.54), channel_id=1, source_target_pairs={{0,24},{2,26},{4,28},{6,30},{8,16},{10,18},{12,20},{14,22},{16,8},... | collective-permute-start | bytes 196616 | tf_op jit(solution)/shard_map/ppermute | solution.py:415
  26.4 7.6 %collective-permute-start.9 = (bf16[64,512]{1,0:T(8,128)(2,1)S(1)}, bf16[64,512]{1,0:T(8,128)(2,1)S(1)}, u32[]{:S(2)}, u32[]{:S(2)}) collective-permute-start(bf16[64,512]{1,0:T(8,128)(2,1)S(1)} %get-tuple-element.55), channel_id=1, source_target_pairs={{0,28},{2,30},{4,24},{6,26},{8,20},{10,22},{12,16},{14,18},{16,12}... | collective-permute-start | bytes 196616 | tf_op jit(solution)/shard_map/ppermute | solution.py:415
  30.7 4.7 %collective-permute-start.10 = (bf16[64,512]{1,0:T(8,128)(2,1)S(1)}, bf16[64,512]{1,0:T(8,128)(2,1)S(1)}, u32[]{:S(2)}, u32[]{:S(2)}) collective-permute-start(bf16[64,512]{1,0:T(8,128)(2,1)S(1)} %get-tuple-element.56), channel_id=1, source_target_pairs={{0,16},{2,18},{4,20},{6,22},{8,24},{10,26},{12,28},{14,30},{16,0},... | collective-permute-start | bytes 196616 | tf_op jit(solution)/shard_map/ppermute | solution.py:415
  31.8 5.2 %collective-permute-start.11 = (bf16[64,512]{1,0:T(8,128)(2,1)S(1)}, bf16[64,512]{1,0:T(8,128)(2,1)S(1)}, u32[]{:S(2)}, u32[]{:S(2)}) collective-permute-start(bf16[64,512]{1,0:T(8,128)(2,1)S(1)} %get-tuple-element.57), channel_id=1, source_target_pairs={{0,20},{2,22},{4,16},{6,18},{8,28},{10,30},{12,24},{14,26},{16,4},... | collective-permute-start | bytes 196616 | tf_op jit(solution)/shard_map/ppermute | solution.py:415
  41.1 8.0 %collective-permute-start.16 = (bf16[64,512]{1,0:T(8,128)(2,1)S(1)}, bf16[64,512]{1,0:T(8,128)(2,1)S(1)}, u32[]{:S(2)}, u32[]{:S(2)}) collective-permute-start(bf16[64,512]{1,0:T(8,128)(2,1)S(1)} %get-tuple-element.59), channel_id=1, source_target_pairs={{0,8},{2,10},{4,12},{6,14},{8,0},{10,2},{12,4},{14,6},{1,9},{3,11}... | collective-permute-start | bytes 196616 | tf_op jit(solution)/shard_map/ppermute | solution.py:405
  43.9 6.5 %collective-permute-start.17 = (bf16[64,512]{1,0:T(8,128)(2,1)S(1)}, bf16[64,512]{1,0:T(8,128)(2,1)S(1)}, u32[]{:S(2)}, u32[]{:S(2)}) collective-permute-start(bf16[64,512]{1,0:T(8,128)(2,1)S(1)} %get-tuple-element.60), channel_id=1, source_target_pairs={{0,12},{2,14},{4,8},{6,10},{8,4},{10,6},{12,0},{14,2},{1,13},{3,15... | collective-permute-start | bytes 196616 | tf_op jit(solution)/shard_map/ppermute | solution.py:405
  44.5 7.2 %collective-permute-start.18 = (bf16[64,512]{1,0:T(8,128)(2,1)S(1)}, bf16[64,512]{1,0:T(8,128)(2,1)S(1)}, u32[]{:S(2)}, u32[]{:S(2)}) collective-permute-start(bf16[64,512]{1,0:T(8,128)(2,1)S(1)} %get-tuple-element.61), channel_id=1, source_target_pairs={{0,4},{2,6},{4,0},{6,2},{8,12},{10,14},{12,8},{14,10},{1,5},{3,7},... | collective-permute-start | bytes 196616 | tf_op jit(solution)/shard_map/ppermute | solution.py:405
  45.0 9.5 %collective-permute-start.19 = (bf16[64,512]{1,0:T(8,128)(2,1)S(1)}, bf16[64,512]{1,0:T(8,128)(2,1)S(1)}, u32[]{:S(2)}, u32[]{:S(2)}) collective-permute-start(bf16[64,512]{1,0:T(8,128)(2,1)S(1)} %get-tuple-element.58.refs_0_), channel_id=1, source_target_pairs={{0,2},{2,0},{4,6},{6,4},{8,10},{10,8},{12,14},{14,12},{1,3},{3,1},... | collective-permute-start | bytes 196616 | tf_op jit(solution)/shard_map/ppermute | solution.py:405
  49.1 5.3 %collective-permute-start.20 = (bf16[64,512]{1,0:T(8,128)(2,1)S(1)}, bf16[64,512]{1,0:T(8,128)(2,1)S(1)}, u32[]{:S(2)}, u32[]{:S(2)}) collective-permute-start(bf16[64,512]{1,0:T(8,128)(2,1)S(1)} %collective-permute-done.16.refs_2_.refs_1_), channel_id=1, source_target_pairs={{0,2},{2,0},{4,6},{6,4},{8,10},{10,8},{12,14},{14,12},{1,3},{3,1},... | collective-permute-start | bytes 196616 | tf_op jit(solution)/shard_map/ppermute | solution.py:405
  59.9 7.0 %collective-permute-start.23 = (bf16[64,512]{1,0:T(8,128)(2,1)S(1)}, bf16[64,512]{1,0:T(8,128)(2,1)S(1)}, u32[]{:S(2)}, u32[]{:S(2)}) collective-permute-start(bf16[64,512]{1,0:T(8,128)(2,1)S(1)} %get-tuple-element.64), channel_id=1, source_target_pairs={{0,24},{2,26},{4,28},{6,30},{8,16},{10,18},{12,20},{14,22},{16,8},... | collective-permute-start | bytes 196616 | tf_op jit(solution)/shard_map/ppermute | solution.py:415
  62.7 7.2 %collective-permute-start.24 = (bf16[64,512]{1,0:T(8,128)(2,1)S(1)}, bf16[64,512]{1,0:T(8,128)(2,1)S(1)}, u32[]{:S(2)}, u32[]{:S(2)}) collective-permute-start(bf16[64,512]{1,0:T(8,128)(2,1)S(1)} %get-tuple-element.65), channel_id=1, source_target_pairs={{0,28},{2,30},{4,24},{6,26},{8,20},{10,22},{12,16},{14,18},{16,12}... | collective-permute-start | bytes 196616 | tf_op jit(solution)/shard_map/ppermute | solution.py:415
  64.2 6.5 %collective-permute-start.25 = (bf16[64,512]{1,0:T(8,128)(2,1)S(1)}, bf16[64,512]{1,0:T(8,128)(2,1)S(1)}, u32[]{:S(2)}, u32[]{:S(2)}) collective-permute-start(bf16[64,512]{1,0:T(8,128)(2,1)S(1)} %get-tuple-element.66), channel_id=1, source_target_pairs={{0,16},{2,18},{4,20},{6,22},{8,24},{10,26},{12,28},{14,30},{16,0},... | collective-permute-start | bytes 196616 | tf_op jit(solution)/shard_map/ppermute | solution.py:415
  65.2 5.5 %collective-permute-start.26 = (bf16[64,512]{1,0:T(8,128)(2,1)S(1)}, bf16[64,512]{1,0:T(8,128)(2,1)S(1)}, u32[]{:S(2)}, u32[]{:S(2)}) collective-permute-start(bf16[64,512]{1,0:T(8,128)(2,1)S(1)} %get-tuple-element.67), channel_id=1, source_target_pairs={{0,20},{2,22},{4,16},{6,18},{8,28},{10,30},{12,24},{14,26},{16,4},... | collective-permute-start | bytes 196616 | tf_op jit(solution)/shard_map/ppermute | solution.py:415
  66.9 4.4 %collective-permute-start.27 = (bf16[64,512]{1,0:T(8,128)(2,1)S(1)}, bf16[64,512]{1,0:T(8,128)(2,1)S(1)}, u32[]{:S(2)}, u32[]{:S(2)}) collective-permute-start(bf16[64,512]{1,0:T(8,128)(2,1)S(1)} %collective-permute-done.23.refs_0_), channel_id=1, source_target_pairs={{0,1},{1,0},{2,3},{3,2},{4,5},{5,4},{6,7},{7,6},{8,9},{9,8},{10,11... | collective-permute-start | bytes 196616 | tf_op jit(solution)/shard_map/ppermute | solution.py:405
  72.8 7.9 %collective-permute-start.31 = (bf16[64,512]{1,0:T(8,128)(2,1)S(1)}, bf16[64,512]{1,0:T(8,128)(2,1)S(1)}, u32[]{:S(2)}, u32[]{:S(2)}) collective-permute-start(bf16[64,512]{1,0:T(8,128)(2,1)S(1)} %get-tuple-element.69), channel_id=1, source_target_pairs={{0,8},{2,10},{4,12},{6,14},{8,0},{10,2},{12,4},{14,6},{1,9},{3,11}... | collective-permute-start | bytes 196616 | tf_op jit(solution)/shard_map/ppermute | solution.py:405
  74.5 6.7 %collective-permute-start.32 = (bf16[64,512]{1,0:T(8,128)(2,1)S(1)}, bf16[64,512]{1,0:T(8,128)(2,1)S(1)}, u32[]{:S(2)}, u32[]{:S(2)}) collective-permute-start(bf16[64,512]{1,0:T(8,128)(2,1)S(1)} %get-tuple-element.70), channel_id=1, source_target_pairs={{0,12},{2,14},{4,8},{6,10},{8,4},{10,6},{12,0},{14,2},{1,13},{3,15... | collective-permute-start | bytes 196616 | tf_op jit(solution)/shard_map/ppermute | solution.py:405
  75.5 7.1 %collective-permute-start.33 = (bf16[64,512]{1,0:T(8,128)(2,1)S(1)}, bf16[64,512]{1,0:T(8,128)(2,1)S(1)}, u32[]{:S(2)}, u32[]{:S(2)}) collective-permute-start(bf16[64,512]{1,0:T(8,128)(2,1)S(1)} %get-tuple-element.71), channel_id=1, source_target_pairs={{0,4},{2,6},{4,0},{6,2},{8,12},{10,14},{12,8},{14,10},{1,5},{3,7},... | collective-permute-start | bytes 196616 | tf_op jit(solution)/shard_map/ppermute | solution.py:405
  76.3 8.8 %collective-permute-start.38 = (bf16[256,512]{1,0:T(8,128)(2,1)S(1)}, bf16[256,512]{1,0:T(8,128)(2,1)S(1)}, u32[]{:S(2)}, u32[]{:S(2)}) collective-permute-start(bf16[256,512]{1,0:T(8,128)(2,1)S(1)} %constant_dynamic-update-slice_fusion.refs_0_), channel_id=1, source_target_pairs={{0,16},{16,0},{1,17},{17,1},{2,18},{18,2},{3,19},{19,3},{4,20},{20... | collective-permute-start | bytes 786440 | tf_op jit(solution)/shard_map/ppermute | solution.py:448
  79.2 7.4 %collective-permute-start.34 = (bf16[64,512]{1,0:T(8,128)(2,1)S(1)}, bf16[64,512]{1,0:T(8,128)(2,1)S(1)}, u32[]{:S(2)}, u32[]{:S(2)}) collective-permute-start(bf16[64,512]{1,0:T(8,128)(2,1)S(1)} %get-tuple-element.72.refs_0_), channel_id=1, source_target_pairs={{0,2},{2,0},{4,6},{6,4},{8,10},{10,8},{12,14},{14,12},{1,3},{3,1},... | collective-permute-start | bytes 196616 | tf_op jit(solution)/shard_map/ppermute | solution.py:405
  80.6 6.0 %collective-permute-start.35 = (bf16[64,512]{1,0:T(8,128)(2,1)S(1)}, bf16[64,512]{1,0:T(8,128)(2,1)S(1)}, u32[]{:S(2)}, u32[]{:S(2)}) collective-permute-start(bf16[64,512]{1,0:T(8,128)(2,1)S(1)} %collective-permute-done.31.refs_2_.refs_1_), channel_id=1, source_target_pairs={{0,2},{2,0},{4,6},{6,4},{8,10},{10,8},{12,14},{14,12},{1,3},{3,1},... | collective-permute-start | bytes 196616 | tf_op jit(solution)/shard_map/ppermute | solution.py:405
  81.2 5.7 %collective-permute-start.36 = (bf16[64,512]{1,0:T(8,128)(2,1)S(1)}, bf16[64,512]{1,0:T(8,128)(2,1)S(1)}, u32[]{:S(2)}, u32[]{:S(2)}) collective-permute-start(bf16[64,512]{1,0:T(8,128)(2,1)S(1)} %collective-permute-done.32.refs_3_.refs_2_), channel_id=1, source_target_pairs={{0,2},{2,0},{4,6},{6,4},{8,10},{10,8},{12,14},{14,12},{1,3},{3,1},... | collective-permute-start | bytes 196616 | tf_op jit(solution)/shard_map/ppermute | solution.py:405
  82.7 5.0 %collective-permute-start.37 = (bf16[64,512]{1,0:T(8,128)(2,1)S(1)}, bf16[64,512]{1,0:T(8,128)(2,1)S(1)}, u32[]{:S(2)}, u32[]{:S(2)}) collective-permute-start(bf16[64,512]{1,0:T(8,128)(2,1)S(1)} %collective-permute-done.33.refs_1_.refs_3_), channel_id=1, source_target_pairs={{0,2},{2,0},{4,6},{6,4},{8,10},{10,8},{12,14},{14,12},{1,3},{3,1},... | collective-permute-start | bytes 196616 | tf_op jit(solution)/shard_map/ppermute | solution.py:405
  88.2 8.5 %collective-permute-start.39 = (bf16[64,512]{1,0:T(8,128)(2,1)S(1)}, bf16[64,512]{1,0:T(8,128)(2,1)S(1)}, u32[]{:S(2)}, u32[]{:S(2)}) collective-permute-start(bf16[64,512]{1,0:T(8,128)(2,1)S(1)} %get-tuple-element.83), channel_id=1, source_target_pairs={{0,16},{16,0},{1,17},{17,1},{2,18},{18,2},{3,19},{19,3},{4,20},{20... | collective-permute-start | bytes 196616 | tf_op jit(solution)/shard_map/ppermute | solution.py:448
  93.9 7.2 %collective-permute-start.44 = (bf16[64,512]{1,0:T(8,128)(2,1)S(1)}, bf16[64,512]{1,0:T(8,128)(2,1)S(1)}, u32[]{:S(2)}, u32[]{:S(2)}) collective-permute-start(bf16[64,512]{1,0:T(8,128)(2,1)S(1)} %get-tuple-element.89), channel_id=1, source_target_pairs={{0,16},{16,0},{1,17},{17,1},{2,18},{18,2},{3,19},{19,3},{4,20},{20... | collective-permute-start | bytes 196616 | tf_op jit(solution)/shard_map/ppermute | solution.py:448
  96.7 8.1 %collective-permute-start.43 = (bf16[64,512]{1,0:T(8,128)(2,1)S(1)}, bf16[64,512]{1,0:T(8,128)(2,1)S(1)}, u32[]{:S(2)}, u32[]{:S(2)}) collective-permute-start(bf16[64,512]{1,0:T(8,128)(2,1)S(1)} %broadcast_select_fusion.3), channel_id=1, source_target_pairs={{0,8},{2,10},{4,12},{6,14},{8,0},{10,2},{12,4},{14,6},{1,9},{3,11}... | collective-permute-start | bytes 196616 | tf_op jit(solution)/shard_map/ppermute | solution.py:405
  101.1 6.2 %collective-permute-start.45 = (bf16[64,512]{1,0:T(8,128)(2,1)S(1)}, bf16[64,512]{1,0:T(8,128)(2,1)S(1)}, u32[]{:S(2)}, u32[]{:S(2)}) collective-permute-start(bf16[64,512]{1,0:T(8,128)(2,1)S(1)} %broadcast_select_fusion), channel_id=1, source_target_pairs={{0,12},{2,14},{4,8},{6,10},{8,4},{10,6},{12,0},{14,2},{1,13},{3,15... | collective-permute-start | bytes 196616 | tf_op jit(solution)/shard_map/ppermute | solution.py:405
  103.3 4.6 %collective-permute-start.42 = (bf16[64,512]{1,0:T(8,128)(2,1)S(1)}, bf16[64,512]{1,0:T(8,128)(2,1)S(1)}, u32[]{:S(2)}, u32[]{:S(2)}) collective-permute-start(bf16[64,512]{1,0:T(8,128)(2,1)S(1)} %broadcast_select_fusion.1), channel_id=1, source_target_pairs={{0,4},{2,6},{4,0},{6,2},{8,12},{10,14},{12,8},{14,10},{1,5},{3,7},... | collective-permute-start | bytes 196616 | tf_op jit(solution)/shard_map/ppermute | solution.py:405
  (21 other events, 87.9 us)

commit v3 on v2

--- a/solution.py
+++ b/solution.py
@@ -10,6 +10,7 @@
 HEADS = 8
 HEAD_DIM = 64
 PB = 64
+FAST = 2
 LOG2E = 1.4426950408889634
 
 
@@ -137,21 +138,26 @@
     return sets
 
 
-def at_work(place_ref, step, micro):
-    number = step - place_ref[0]
+def here():
+    shard = lax.axis_index("patch")
+    return lax.axis_index("pipe"), lax.div(shard, FAST), lax.rem(shard, FAST)
+
+
+def at_work(stage, step, micro):
+    number = step - stage
     return jnp.logical_and(number >= 0, number < micro)
 
 
-def order_kernel(sizes, place_ref, order_ref):
+def order_kernel(sizes, order_ref):
     slow, _, patches, hl = sizes
     shape = order_ref.shape
     patch, late, offset = digits(shape, 0, patches, hl)
     source = lax.broadcasted_iota(jnp.int32, shape, 1)
-    wanted = (patch * slow + (offset ^ place_ref[1])) * hl + late
+    wanted = (patch * slow + (offset ^ here()[1])) * hl + late
     order_ref[...] = jnp.where(wanted == source, 1.0, 0.0).astype(jnp.bfloat16)
 
 
-def time_kernel(sizes, step, micro, place_ref, *refs):
+def time_kernel(sizes, step, micro, *refs):
     shards, peers, patches, hl = sizes
     given = peers if step < micro else 0
     order_refs, refs = refs[: min(given, 1)], refs[min(given, 1) :]
@@ -163,12 +169,13 @@
     y_refs, refs = refs[:shards], refs[shards:]
     x_ref = refs[0]
     rows = x_ref.shape[0] // peers
-
-    @pl.when(at_work(place_ref, step, micro))
+    stage = here()[0]
+
+    @pl.when(at_work(stage, step, micro))
     def _():
         if given:
 
-            @pl.when(place_ref[0] == 0)
+            @pl.when(stage == 0)
             def _():
                 order = order_refs[0][...]
                 for j, ref in enumerate(input_refs):
@@ -177,7 +184,7 @@
 
         if came:
 
-            @pl.when(place_ref[0] != 0)
+            @pl.when(stage != 0)
             def _():
                 for j, blocks in enumerate(row_sets(came_refs, shards, pieces)):
                     x_ref[j * rows : (j + 1) * rows, :] = jnp.concatenate(blocks, axis=0)
@@ -192,9 +199,9 @@
         mine = digits(shape, 0, inner)[0]
         theirs = digits(shape, 1, inner)[0]
         mask = jnp.where(mine == theirs, 1.0, 0.0).astype(jnp.bfloat16)
-        normed = [row_norm(x, gain_ref[0, 0:1, :]) for x in xs]
+        normed = [row_norm(x, gain_ref[0]) for x in xs]
         w_in = w_in_ref.at[0, 0]
-        q = queries(normed[0], lambda n: scale_ref[0, 0, n], w_in)
+        q = queries(normed[0], lambda n: scale_ref[0, 0:1, n : n + 1], w_in)
         k, v = keys_and_values(jnp.concatenate(normed, axis=0), w_in)
         update = projected(attention_sums(q, k, v, groups, mask), w_out_ref.at[0, 0])
         y = regrouped(xs[0] + update, rows // (groups * inner), inner).astype(jnp.bfloat16)
@@ -209,30 +216,31 @@
     return groups, hl // groups * patches
 
 
-def patch_mask(sizes, fast, others, place_ref, seen_ref):
+def patch_mask(sizes, fast, others, seen_ref):
     slow, _, patches, hl = sizes
     groups, inner = hour_groups(sizes)
     size = slow * inner
     shape = (size, size * len(others))
+    _, my_slow, my_fast = here()
 
     def block_and_hour(dimension, first):
         patch, late, offset, other = digits(shape, dimension, patches, hl // groups, slow)
-        shard = (offset ^ place_ref[1]) * fast + ((other + first) ^ place_ref[2])
+        shard = (offset ^ my_slow) * fast + ((other + first) ^ my_fast)
         return (shard * patches + patch) // PB, late
 
     query_block, query_hour = block_and_hour(0, 0)
     key_block, key_hour = block_and_hour(1, others[0])
     seen = None
     for kv in range(seen_ref.shape[1]):
-        chosen = jnp.full(shape, seen_ref[0, kv], jnp.int32)
+        chosen = jnp.broadcast_to(seen_ref[0:1, kv : kv + 1], shape)
         for b in range(1, seen_ref.shape[0]):
-            chosen = jnp.where(query_block == b, seen_ref[b, kv], chosen)
+            chosen = jnp.where(query_block == b, seen_ref[b : b + 1, kv : kv + 1], chosen)
         hit = jnp.where(chosen == key_block, 1.0, 0.0)
         seen = hit if seen is None else jnp.maximum(seen, hit)
     return jnp.where(query_hour == key_hour, seen, 0.0).astype(jnp.bfloat16)
 
 
-def own_patch_kernel(sizes, fast, step, micro, place_ref, seen_ref, *refs):
+def own_patch_kernel(sizes, fast, step, micro, seen_ref, *refs):
     slow = sizes[0]
     x_refs, (gain_ref, scale_ref, w_in_ref), (q_ref, sums_ref) = (
         refs[:slow],
@@ -240,28 +248,28 @@
         refs[slow + 3 :],
     )
 
-    @pl.when(at_work(place_ref, step, micro))
+    @pl.when(at_work(here()[0], step, micro))
     def _():
         groups, inner = hour_groups(sizes)
         x = jnp.concatenate([ref[...] for ref in x_refs], axis=0).astype(jnp.float32)
-        normed = row_norm(regrouped(x, groups, inner), gain_ref[0, 1:2, :])
+        normed = row_norm(regrouped(x, groups, inner), gain_ref[1])
         w_in = w_in_ref.at[0, 1]
-        q = queries(normed, lambda n: scale_ref[0, 1, n], w_in)
+        q = queries(normed, lambda n: scale_ref[0, 1:2, n : n + 1], w_in)
         k, v = keys_and_values(normed, w_in)
         q_ref[...] = q
-        mask = patch_mask(sizes, fast, [0], place_ref, seen_ref)
+        mask = patch_mask(sizes, fast, [0], seen_ref)
         sums = attention_sums(q, k, v, groups, mask)
         sums_ref[...] = jnp.concatenate([jnp.concatenate(t, axis=1) for t in sums], axis=0)
 
 
-def patch_kernel(sizes, fast, step, micro, place_ref, seen_ref, *refs):
+def patch_kernel(sizes, fast, step, micro, seen_ref, *refs):
     slow = sizes[0]
     count = fast * slow
     x_refs, refs, y_refs = refs[:count], refs[count:-slow], refs[-slow:]
     q_ref, sums_ref, gain_ref, w_in_ref, w_out_ref, up_ref, down_ref = refs
     pieces = pieces_of([0] + [k for k in far_first(slow) if k])
 
-    @pl.when(at_work(place_ref, step, micro))
+    @pl.when(at_work(here()[0], step, micro))
     def _():
         groups, inner = hour_groups(sizes)
         xs = [
@@ -270,9 +278,9 @@
         ]
         x = xs[0]
         rows, width = x.shape
-        normed = jnp.concatenate([row_norm(t, gain_ref[0, 1:2, :]) for t in xs[1:]], axis=0)
+        normed = jnp.concatenate([row_norm(t, gain_ref[1]) for t in xs[1:]], axis=0)
         k, v = keys_and_values(normed, w_in_ref.at[0, 1])
-        mask = patch_mask(sizes, fast, range(1, fast), place_ref, seen_ref)
+        mask = patch_mask(sizes, fast, range(1, fast), seen_ref)
         more = attention_sums(q_ref[...], k, v, groups, mask)
         size = rows // groups
         sums = [
@@ -283,7 +291,7 @@
             for g, parts in enumerate(more)
         ]
         x = rounded(x + projected(sums, w_out_ref.at[0, 1]))
-        normed = row_norm(x, gain_ref[0, 2:3, :])
+        normed = row_norm(x, gain_ref[2])
         total = x
         chunk = 512
         for start in range(0, up_ref.shape[2], chunk):
@@ -297,32 +305,31 @@
             y_refs[k][...] = y[k * size : (k + 1) * size]
 
 
-def write_rows(sizes, place_ref, x, y_ref):
+def write_rows(sizes, x, y_ref):
     slow, _, patches, hl = sizes
     rows = slow * patches * hl
     late, shard, patch = digits((rows, rows), 0, hl, slow)
     source = lax.broadcasted_iota(jnp.int32, (rows, rows), 1)
-    wanted = ((shard ^ place_ref[1]) * hl + late) * patches + patch
+    wanted = ((shard ^ here()[1]) * hl + late) * patches + patch
     order = jnp.where(wanted == source, 1.0, 0.0).astype(jnp.bfloat16)
     y_ref[...] = matmul(order, x).astype(jnp.bfloat16)
 
 
-def early_kernel(sizes, pipes, place_ref, *refs):
+def early_kernel(sizes, pipes, *refs):
     x_refs, y_ref = refs[:pipes], refs[-1]
     for stage, x_ref in enumerate(x_refs):
 
-        @pl.when(place_ref[0] == stage)
+        @pl.when(here()[0] == stage)
         def _():
-            write_rows(sizes, place_ref, x_ref[...], y_ref)
-
-
-def final_kernel(sizes, place_ref, *refs):
+            write_rows(sizes, x_ref[...], y_ref)
+
+
+def final_kernel(sizes, *refs):
     x_refs, y_ref = refs[: sizes[0]], refs[-1]
-    write_rows(sizes, place_ref, jnp.concatenate([ref[...] for ref in x_refs], axis=0), y_ref)
+    write_rows(sizes, jnp.concatenate([ref[...] for ref in x_refs], axis=0), y_ref)
 
 
 VMEM = pl.BlockSpec(memory_space=pltpu.VMEM)
-SMEM = pl.BlockSpec(memory_space=pltpu.SMEM)
 PARAMS = pltpu.CompilerParams(vmem_limit_bytes=32 << 20)
 COST = pl.CostEstimate(flops=5 << 30, bytes_accessed=1 << 20, transcendentals=1 << 20)
 
@@ -331,34 +338,34 @@
     return [jax.ShapeDtypeStruct((rows // count, width), jnp.bfloat16)] * count
 
 
-def call_order(sizes, place, rows):
+def call_order(sizes, rows):
     return pl.pallas_call(
         functools.partial(order_kernel, sizes),
         out_shape=jax.ShapeDtypeStruct((rows, rows), jnp.bfloat16),
-        in_specs=[SMEM],
+        in_specs=[],
         out_specs=VMEM,
         compiler_params=PARAMS,
         cost_estimate=COST,
         name="input_order",
-    )(place)
-
-
-def call_time(sizes, step, micro, shape, place, order, given, came, gains, scales, w_in, w_out):
+    )()
+
+
+def call_time(sizes, step, micro, shape, order, given, came, gains, scales, w_in, w_out):
     rows, width = shape
     xs = ([order] if given else []) + list(given) + list(came)
     return pl.pallas_call(
         functools.partial(time_kernel, sizes, step, micro),
         out_shape=blocks_of(sizes[0], rows, width),
-        in_specs=[SMEM] + [VMEM] * len(xs) + [VMEM, SMEM, VMEM, VMEM],
+        in_specs=[VMEM] * (len(xs) + 4),
         out_specs=[VMEM] * sizes[0],
         scratch_shapes=[pltpu.VMEM((rows * sizes[1], width), jnp.bfloat16)],
         compiler_params=PARAMS,
         cost_estimate=COST,
         name="time_attention",
-    )(place, *xs, gains, scales, w_in, w_out)
-
-
-def call_own_patch(sizes, fast, step, micro, shape, place, seen, xs, gains, scales, w_in):
+    )(*xs, gains, scales, w_in, w_out)
+
+
+def call_own_patch(sizes, fast, step, micro, shape, seen, xs, gains, scales, w_in):
     rows, width = shape
     return pl.pallas_call(
         functools.partial(own_patch_kernel, sizes, fast, step, micro),
@@ -366,39 +373,39 @@
             jax.ShapeDtypeStruct((rows, width), jnp.bfloat16),
             jax.ShapeDtypeStruct((rows, 2 * width), jnp.float32),
         ],
-        in_specs=[SMEM, SMEM] + [VMEM] * len(xs) + [VMEM, SMEM, VMEM],
+        in_specs=[VMEM] * (len(xs) + 4),
         out_specs=[VMEM, VMEM],
         compiler_params=PARAMS,
         cost_estimate=COST,
         name="own_patch_attention",
-    )(place, seen, *xs, gains, scales, w_in)
-
-
-def call_patch(sizes, fast, step, micro, shape, place, seen, xs, weights):
+    )(seen, *xs, gains, scales, w_in)
+
+
+def call_patch(sizes, fast, step, micro, shape, seen, xs, weights):
     rows, width = shape
     return pl.pallas_call(
         functools.partial(patch_kernel, sizes, fast, step, micro),
         out_shape=blocks_of(sizes[0], rows, width),
-        in_specs=[SMEM, SMEM] + [VMEM] * (len(xs) + len(weights)),
+        in_specs=[VMEM] * (1 + len(xs) + len(weights)),
         out_specs=[VMEM] * sizes[0],
         compiler_params=PARAMS,
         cost_estimate=COST,
         name="patch_attention_and_ffn",
-    )(place, seen, *xs, *weights)
-
-
-def call_write(kernel, sizes, place, shape, number, xs, out):
+    )(seen, *xs, *weights)
+
+
+def call_write(kernel, sizes, shape, number, xs, out):
     given = [] if out is None else [out]
     return pl.pallas_call(
         kernel,
         out_shape=jax.ShapeDtypeStruct(shape, jnp.bfloat16),
         grid=(1,),
-        in_specs=[SMEM] + [VMEM] * len(xs) + [pl.BlockSpec(memory_space=pl.ANY)] * len(given),
+        in_specs=[VMEM] * len(xs) + [pl.BlockSpec(memory_space=pl.ANY)] * len(given),
         out_specs=pl.BlockSpec((None,) + shape[1:], lambda i: (number, 0, 0)),
-        input_output_aliases={1 + len(xs): 0} if given else {},
+        input_output_aliases={len(xs): 0} if given else {},
         compiler_params=PARAMS,
         name="final_order",
-    )(place, *xs, *given)
+    )(*xs, *given)
 
 
 def flipped(x, axis, k):
@@ -421,14 +428,13 @@
     pipes = lax.axis_size("pipe")
     micro, patches, hours, width = inputs.shape
     rows = patches * hours
-    fast = 2
+    fast = FAST
     slow = shards // fast
     sizes = (slow, peers, patches, hours // slow)
     last = pipes - 1
-    shard = lax.axis_index("patch")
-    place = jnp.stack([lax.axis_index("pipe"), lax.div(shard, fast), lax.rem(shard, fast)])
+    gains = gains.reshape(gains.shape[1], 1, width)
     far = far_first(slow)
-    order = call_order(sizes, place, rows)
+    order = call_order(sizes, rows)
 
     def gathered(blocks, axis, count, sequence):
         own = [jnp.concatenate([blocks[k] for k in piece]) for piece in pieces_of(sequence)]
@@ -455,20 +461,20 @@
     for step in range(micro + pipes - 1):
         now = given if step < micro else []
         mixed = call_time(
-            sizes, step, micro, x.shape[1:], place, order, now, came, gains, scales, w_in, w_out
+            sizes, step, micro, x.shape[1:], order, now, came, gains, scales, w_in, w_out
         )
         own = along_slow(mixed, in_stage, 1)
         spread = gathered(own, "patch", fast, [0] + [k for k in far if k])
         begun = call_own_patch(
-            sizes, fast, step, micro, x.shape[1:], place, seen, own, gains, scales, w_in
+            sizes, fast, step, micro, x.shape[1:], seen, own, gains, scales, w_in
         )
         if back:
+            spread, back = lax.optimization_barrier((spread, back))
             write = functools.partial(early_kernel, sizes, pipes)
-            out = call_write(write, sizes, place, x.shape, step - pipes, back, out)
-            spread, out = lax.optimization_barrier((spread, out))
+            out = call_write(write, sizes, x.shape, step - pipes, back, out)
         at_end = step == micro + pipes - 2
         weights = [*begun, gains, w_in, w_out, w_up, w_down]
-        done = call_patch(sizes, fast, step, micro, x.shape[1:], place, seen, spread, weights)
+        done = call_patch(sizes, fast, step, micro, x.shape[1:], seen, spread, weights)
         if not at_end:
             arrived = along_slow(done, handed_on, 0)
             came = gathered(arrived, "hour", peers, far)
@@ -490,7 +496,7 @@
     blocks = {k: in_stage(blocks[k], k * fast) if k else blocks[k] for k in far}
     blocks = [blocks[k] for k in range(slow)]
     write = functools.partial(final_kernel, sizes)
-    out = call_write(write, sizes, place, x.shape, micro - 1, blocks, out)
+    out = call_write(write, sizes, x.shape, micro - 1, blocks, out)
     return out.reshape(inputs.shape)
 
 

time: 110 us -> 105 us (0.955)
  Pallas kernels: 22.8 us -> 16.2 us
  starting transfers between devices: 54.2 us -> 58.1 us
  local copies, waits for them, and re-layouts: 2.07 us -> 0.05 us
    ppermute x5, waiting for transfers between devices: 5.09 us -> 2.19 us  [onward(): return lax.ppermute(x, 'pipe', [(s, (s + 1) % pipes) for s in range(pipes)])]
    unnamed x18 -> x19, local copies, waits for them, and re-layouts: 2.06 us -> 0.05 us
    ppermute x5, starting transfers between devices: 10.6 us -> 12.5 us  [onward(): return lax.ppermute(x, 'pipe', [(s, (s + 1) % pipes) for s in range(pipes)])]
    pallas_call x3, Pallas kernels: 8.22 us -> 6.46 us  [call_patch(): pl.pallas_call(functools.partial(patch_kernel, sizes, fast, step, micro),...]
    pallas_call x3, Pallas kernels: 4.59 us -> 2.91 us  [call_own_patch(): pl.pallas_call(functools.partial(own_patch_kernel, sizes, fast, step, mic...]
    ppermute x33, waiting for transfers between devices: 15.8 us -> 17.5 us  [flipped(): lax.ppermute(x, axis, [(s, s ^ k) for s in range(lax.axis_size(axis))])]
    pallas_call x3, Pallas kernels: 6.39 us -> 4.87 us  [call_time(): pl.pallas_call(functools.partial(time_kernel, sizes, step, micro), out_sh...]
    ppermute x8, waiting for transfers between devices: 9.08 us -> 10.4 us  [handed_on(): return lax.ppermute(x, ('pipe', 'patch'), pairs)]
  transfers between devices with their start and end apart: 46 -> 46, of which waited for: 27 -> 24; matrix products, arithmetic and copies ran while one was open for 1% -> 0% of each run, Pallas kernels for 6% -> 4%
where the time goes in v3:
time: 105 us
  starting transfers between devices  58.1 us (55%)
  waiting for transfers between devices  30.1 us (29%)
  Pallas kernels  16.2 us (15%)
    ppermute x33, starting transfers between devices, flipped(): lax.ppermute(x, axis, [(s, s ^ k) for s in range(lax.axis_size(axis))])  32.8 us
    ppermute x33, waiting for transfers between devices, flipped(): lax.ppermute(x, axis, [(s, s ^ k) for s in range(lax.axis_size(axis))])  17.5 us
    ppermute x8, starting transfers between devices, handed_on(): return lax.ppermute(x, ('pipe', 'patch'), pairs)  12.7 us
    ppermute x5, starting transfers between devices, onward(): return lax.ppermute(x, 'pipe', [(s, (s + 1) % pipes) for s in range(pipes)])  12.5 us
    ppermute x8, waiting for transfers between devices, handed_on(): return lax.ppermute(x, ('pipe', 'patch'), pairs)  10.4 us
    pallas_call x3, Pallas kernels, call_patch(): pl.pallas_call(functools.partial(patch_kernel, sizes, fast, step, micro),...  6.46 us
    pallas_call x3, Pallas kernels, call_time(): pl.pallas_call(functools.partial(time_kernel, sizes, step, micro), out_sh...  4.87 us
    pallas_call x3, Pallas kernels, call_own_patch(): pl.pallas_call(functools.partial(own_patch_kernel, sizes, fast, step, mic...  2.91 us
  transfers between devices with their start and end apart: 46, of which 24 were waited for; matrix products, arithmetic and copies ran while one was open for 0% of the time, Pallas kernels for 4%

profile of v3, /device:TPU:0, one launch (start us, length us, event | category | flops | bytes accessed | tf_op | source)
XLA Modules:
  0.0 104.6 jit_solution(12414640941732655117)
XLA Ops:
  0.6 1.7 %collective-permute-done.refs_2_ = bf16[2,256,512]{2,1,0:T(8,128)(2,1)S(1)} collective-permute-done((bf16[2,256,512]{2,1,0:T(8,128)(2,1)}, bf16[2,256,512]{2,1,0:T(8,128)(2,1)S(1)}, u32[]{:S(2)}, u32[]{:S(2)}) %collective-permute-start) | collective-permute-done | bytes 524320 | tf_op jit(solution)/shard_map/ppermute | solution.py:412
  2.3 2.4 %time_attention.3 = (bf16[64,512]{1,0:T(8,128)(2,1)S(1)}, bf16[64,512]{1,0:T(8,128)(2,1)S(1)}, bf16[64,512]{1,0:T(8,128)(2,1)S(1)}, bf16[64,512]{1,0:T(8,128)(2,1)S(1)}) custom-call(bf16[256,256]{1,0:T(8,128)(2,1)S(1)} %input_order.1.refs_0_, bf16[2,256,512]{2,1,0:T(8,128)(2,1)S(1)} %bitcast.4, bf16[2,256,512]{2,1,0:T(8,128)(2,1)S(1)} %collective-permute-done.refs_2_, ...), custom_call_target="tpu_custom_call" | custom-call | flops 5368709120 | bytes 1048576 | tf_op jit(solution)/shard_map/time_attention/pallas_call | solution.py:356
  4.8 4.1 %collective-permute-start.1 = (bf16[64,512]{1,0:T(8,128)(2,1)S(1)}, bf16[64,512]{1,0:T(8,128)(2,1)S(1)}, u32[]{:S(2)}, u32[]{:S(2)}) collective-permute-start(bf16[64,512]{1,0:T(8,128)(2,1)S(1)} %get-tuple-element.50), channel_id=1, source_target_pairs={{0,8},{2,10},{4,12},{6,14},{8,0},{10,2},{12,4},{14,6},{1,9},{3,11}... | collective-permute-start | bytes 196616 | tf_op jit(solution)/shard_map/ppermute | solution.py:412
  8.8 1.3 %collective-permute-start.2 = (bf16[64,512]{1,0:T(8,128)(2,1)S(1)}, bf16[64,512]{1,0:T(8,128)(2,1)S(1)}, u32[]{:S(2)}, u32[]{:S(2)}) collective-permute-start(bf16[64,512]{1,0:T(8,128)(2,1)S(1)} %get-tuple-element.51), channel_id=1, source_target_pairs={{0,12},{2,14},{4,8},{6,10},{8,4},{10,6},{12,0},{14,2},{1,13},{3,15... | collective-permute-start | bytes 196616 | tf_op jit(solution)/shard_map/ppermute | solution.py:412
  10.4 1.5 %collective-permute-start.4 = (bf16[64,512]{1,0:T(8,128)(2,1)S(1)}, bf16[64,512]{1,0:T(8,128)(2,1)S(1)}, u32[]{:S(2)}, u32[]{:S(2)}) collective-permute-start(bf16[64,512]{1,0:T(8,128)(2,1)S(1)} %get-tuple-element.49.refs_0_), channel_id=1, source_target_pairs={{0,2},{2,0},{4,6},{6,4},{8,10},{10,8},{12,14},{14,12},{1,3},{3,1},... | collective-permute-start | bytes 196616 | tf_op jit(solution)/shard_map/ppermute | solution.py:412
  12.7 2.7 %collective-permute-start.5 = (bf16[64,512]{1,0:T(8,128)(2,1)S(1)}, bf16[64,512]{1,0:T(8,128)(2,1)S(1)}, u32[]{:S(2)}, u32[]{:S(2)}) collective-permute-start(bf16[64,512]{1,0:T(8,128)(2,1)S(1)} %collective-permute-done.1.refs_2_.refs_1_), channel_id=1, source_target_pairs={{0,2},{2,0},{4,6},{6,4},{8,10},{10,8},{12,14},{14,12},{1,3},{3,1},... | collective-permute-start | bytes 196616 | tf_op jit(solution)/shard_map/ppermute | solution.py:412
  15.4 1.3 %collective-permute-start.6 = (bf16[64,512]{1,0:T(8,128)(2,1)S(1)}, bf16[64,512]{1,0:T(8,128)(2,1)S(1)}, u32[]{:S(2)}, u32[]{:S(2)}) collective-permute-start(bf16[64,512]{1,0:T(8,128)(2,1)S(1)} %collective-permute-done.2.refs_3_.refs_2_), channel_id=1, source_target_pairs={{0,2},{2,0},{4,6},{6,4},{8,10},{10,8},{12,14},{14,12},{1,3},{3,1},... | collective-permute-start | bytes 196616 | tf_op jit(solution)/shard_map/ppermute | solution.py:412
  17.5 1.5 %own_patch_attention.3 = (bf16[256,512]{1,0:T(8,128)(2,1)S(1)}, f32[256,1024]{1,0:T(8,128)S(1)}) custom-call(s32[2,2]{1,0:T(2,128)S(1)} %copy-done.7, bf16[64,512]{1,0:T(8,128)(2,1)S(1)} %get-tuple-element.49.refs_0_, bf16[64,512]{1,0:T(8,128)(2,1)S(1)} %collective-permute-done.3.refs_1_.refs_3_, bf16[64,512]{1,0:T(8,128)(2,1)S(1)} %collective-permute-done.1.refs_2_.refs_1_, ...), custom_call_target="tpu_custom_call" | custom-call | flops 5368709120 | bytes 1048576 | tf_op jit(solution)/shard_map/own_patch_attention/pallas_call | solution.py:370
  19.7 1.3 %collective-permute-done.7.refs_7_ = bf16[64,512]{1,0:T(8,128)(2,1)S(1)} collective-permute-done((bf16[64,512]{1,0:T(8,128)(2,1)S(1)}, bf16[64,512]{1,0:T(8,128)(2,1)S(1)}, u32[]{:S(2)}, u32[]{:S(2)}) %collective-permute-start.7) | collective-permute-done | bytes 65568 | tf_op jit(solution)/shard_map/ppermute | solution.py:412
  21.0 3.2 %patch_attention_and_ffn.3 = (bf16[64,512]{1,0:T(8,128)(2,1)S(1)}, bf16[64,512]{1,0:T(8,128)(2,1)S(1)}, bf16[64,512]{1,0:T(8,128)(2,1)S(1)}, bf16[64,512]{1,0:T(8,128)(2,1)S(1)}) custom-call(s32[2,2]{1,0:T(2,128)S(1)} %copy-done.7, bf16[64,512]{1,0:T(8,128)(2,1)S(1)} %get-tuple-element.49.refs_0_, ...), custom_call_target="tpu_custom_call" | custom-call | flops 5368709120 | bytes 1048576 | tf_op jit(solution)/shard_map/patch_attention_and_ffn/pallas_call | solution.py:386
  24.3 4.2 %collective-permute-start.9 = (bf16[64,512]{1,0:T(8,128)(2,1)S(1)}, bf16[64,512]{1,0:T(8,128)(2,1)S(1)}, u32[]{:S(2)}, u32[]{:S(2)}) collective-permute-start(bf16[64,512]{1,0:T(8,128)(2,1)S(1)} %get-tuple-element.56), channel_id=1, source_target_pairs={{0,28},{2,30},{4,24},{6,26},{8,20},{10,22},{12,16},{14,18},{16,12}... | collective-permute-start | bytes 196616 | tf_op jit(solution)/shard_map/ppermute | solution.py:422
  30.1 1.8 %collective-permute-done.8.refs_3_ = bf16[64,512]{1,0:T(8,128)(2,1)S(1)} collective-permute-done((bf16[64,512]{1,0:T(8,128)(2,1)S(1)}, bf16[64,512]{1,0:T(8,128)(2,1)S(1)}, u32[]{:S(2)}, u32[]{:S(2)}) %collective-permute-start.8) | collective-permute-done | bytes 65568 | tf_op jit(solution)/shard_map/ppermute | solution.py:422
  33.4 1.5 %collective-permute-done.11.refs_6_ = bf16[64,512]{1,0:T(8,128)(2,1)S(1)} collective-permute-done((bf16[64,512]{1,0:T(8,128)(2,1)S(1)}, bf16[64,512]{1,0:T(8,128)(2,1)S(1)}, u32[]{:S(2)}, u32[]{:S(2)}) %collective-permute-start.11) | collective-permute-done | bytes 65568 | tf_op jit(solution)/shard_map/ppermute | solution.py:422
  36.1 2.4 %time_attention.4 = (bf16[64,512]{1,0:T(8,128)(2,1)S(1)}, bf16[64,512]{1,0:T(8,128)(2,1)S(1)}, bf16[64,512]{1,0:T(8,128)(2,1)S(1)}, bf16[64,512]{1,0:T(8,128)(2,1)S(1)}) custom-call(bf16[256,256]{1,0:T(8,128)(2,1)S(1)} %input_order.1.refs_0_, bf16[2,256,512]{2,1,0:T(8,128)(2,1)S(1)} %bitcast.5, bf16[2,256,512]{2,1,0:T(8,128)(2,1)S(1)} %collective-permute-done.refs_2_, ...), custom_call_target="tpu_custom_call" | custom-call | flops 5368709120 | bytes 1048576 | tf_op jit(solution)/shard_map/time_attention/pallas_call | solution.py:356
  38.5 2.8 %collective-permute-start.16 = (bf16[64,512]{1,0:T(8,128)(2,1)S(1)}, bf16[64,512]{1,0:T(8,128)(2,1)S(1)}, u32[]{:S(2)}, u32[]{:S(2)}) collective-permute-start(bf16[64,512]{1,0:T(8,128)(2,1)S(1)} %get-tuple-element.60), channel_id=1, source_target_pairs={{0,8},{2,10},{4,12},{6,14},{8,0},{10,2},{12,4},{14,6},{1,9},{3,11}... | collective-permute-start | bytes 196616 | tf_op jit(solution)/shard_map/ppermute | solution.py:412
  43.2 3.4 %collective-permute-done.16.refs_2_.refs_1_ = bf16[64,512]{1,0:T(8,128)(2,1)S(1)} collective-permute-done((bf16[64,512]{1,0:T(8,128)(2,1)S(1)}, bf16[64,512]{1,0:T(8,128)(2,1)S(1)}, u32[]{:S(2)}, u32[]{:S(2)}) %collective-permute-start.16) | collective-permute-done | bytes 65568 | tf_op jit(solution)/shard_map/ppermute | solution.py:412
  48.6 1.2 %collective-permute-start.22 = (bf16[64,512]{1,0:T(8,128)(2,1)S(1)}, bf16[64,512]{1,0:T(8,128)(2,1)S(1)}, u32[]{:S(2)}, u32[]{:S(2)}) collective-permute-start(bf16[64,512]{1,0:T(8,128)(2,1)S(1)} %collective-permute-done.18.refs_1_.refs_3_), channel_id=1, source_target_pairs={{0,2},{2,0},{4,6},{6,4},{8,10},{10,8},{12,14},{14,12},{1,3},{3,1},... | collective-permute-start | bytes 196616 | tf_op jit(solution)/shard_map/ppermute | solution.py:412
  49.8 1.4 %own_patch_attention.4 = (bf16[256,512]{1,0:T(8,128)(2,1)S(1)}, f32[256,1024]{1,0:T(8,128)S(1)}) custom-call(s32[2,2]{1,0:T(2,128)S(1)} %copy-done.7, bf16[64,512]{1,0:T(8,128)(2,1)S(1)} %get-tuple-element.59.refs_0_, bf16[64,512]{1,0:T(8,128)(2,1)S(1)} %collective-permute-done.18.refs_1_.refs_3_, ...), custom_call_target="tpu_custom_call" | custom-call | flops 5368709120 | bytes 1048576 | tf_op jit(solution)/shard_map/own_patch_attention/pallas_call | solution.py:370
  52.9 3.2 %patch_attention_and_ffn.4 = (bf16[64,512]{1,0:T(8,128)(2,1)S(1)}, bf16[64,512]{1,0:T(8,128)(2,1)S(1)}, bf16[64,512]{1,0:T(8,128)(2,1)S(1)}, bf16[64,512]{1,0:T(8,128)(2,1)S(1)}) custom-call(s32[2,2]{1,0:T(2,128)S(1)} %copy-done.7, bf16[64,512]{1,0:T(8,128)(2,1)S(1)} %get-tuple-element.59.refs_0_, ...), custom_call_target="tpu_custom_call" | custom-call | flops 5368709120 | bytes 1048576 | tf_op jit(solution)/shard_map/patch_attention_and_ffn/pallas_call | solution.py:386
  56.1 3.1 %collective-permute-start.23 = (bf16[64,512]{1,0:T(8,128)(2,1)S(1)}, bf16[64,512]{1,0:T(8,128)(2,1)S(1)}, u32[]{:S(2)}, u32[]{:S(2)}) collective-permute-start(bf16[64,512]{1,0:T(8,128)(2,1)S(1)} %get-tuple-element.65), channel_id=1, source_target_pairs={{0,24},{2,26},{4,28},{6,30},{8,16},{10,18},{12,20},{14,22},{16,8},... | collective-permute-start | bytes 196616 | tf_op jit(solution)/shard_map/ppermute | solution.py:422
  60.4 1.7 %collective-permute-start.26 = (bf16[64,512]{1,0:T(8,128)(2,1)S(1)}, bf16[64,512]{1,0:T(8,128)(2,1)S(1)}, u32[]{:S(2)}, u32[]{:S(2)}) collective-permute-start(bf16[64,512]{1,0:T(8,128)(2,1)S(1)} %get-tuple-element.68), channel_id=1, source_target_pairs={{0,20},{2,22},{4,16},{6,18},{8,28},{10,30},{12,24},{14,26},{16,4},... | collective-permute-start | bytes 196616 | tf_op jit(solution)/shard_map/ppermute | solution.py:422
  63.8 1.8 %collective-permute-done.26.refs_3_ = bf16[64,512]{1,0:T(8,128)(2,1)S(1)} collective-permute-done((bf16[64,512]{1,0:T(8,128)(2,1)S(1)}, bf16[64,512]{1,0:T(8,128)(2,1)S(1)}, u32[]{:S(2)}, u32[]{:S(2)}) %collective-permute-start.26) | collective-permute-done | bytes 65568 | tf_op jit(solution)/shard_map/ppermute | solution.py:422
  65.6 3.5 %collective-permute-done.24.refs_1_ = bf16[64,512]{1,0:T(8,128)(2,1)S(1)} collective-permute-done((bf16[64,512]{1,0:T(8,128)(2,1)S(1)}, bf16[64,512]{1,0:T(8,128)(2,1)S(1)}, u32[]{:S(2)}, u32[]{:S(2)}) %collective-permute-start.24) | collective-permute-done | bytes 65568 | tf_op jit(solution)/shard_map/ppermute | solution.py:422
  69.1 1.2 %collective-permute-done.28.refs_5_ = bf16[64,512]{1,0:T(8,128)(2,1)S(1)} collective-permute-done((bf16[64,512]{1,0:T(8,128)(2,1)S(1)}, bf16[64,512]{1,0:T(8,128)(2,1)S(1)}, u32[]{:S(2)}, u32[]{:S(2)}) %collective-permute-start.28) | collective-permute-done | bytes 65568 | tf_op jit(solution)/shard_map/ppermute | solution.py:412
  71.5 2.4 %collective-permute-start.33 = (bf16[64,512]{1,0:T(8,128)(2,1)S(1)}, bf16[64,512]{1,0:T(8,128)(2,1)S(1)}, u32[]{:S(2)}, u32[]{:S(2)}) collective-permute-start(bf16[64,512]{1,0:T(8,128)(2,1)S(1)} %get-tuple-element.72), channel_id=1, source_target_pairs={{0,4},{2,6},{4,0},{6,2},{8,12},{10,14},{12,8},{14,10},{1,5},{3,7},... | collective-permute-start | bytes 196616 | tf_op jit(solution)/shard_map/ppermute | solution.py:412
  73.9 3.4 %collective-permute-start.38 = (bf16[256,512]{1,0:T(8,128)(2,1)S(1)}, bf16[256,512]{1,0:T(8,128)(2,1)S(1)}, u32[]{:S(2)}, u32[]{:S(2)}) collective-permute-start(bf16[256,512]{1,0:T(8,128)(2,1)S(1)} %constant_dynamic-update-slice_fusion.refs_0_), channel_id=1, source_target_pairs={{0,16},{16,0},{1,17},{17,1},{2,18},{18,2},{3,19},{19,3},{4,20},{20... | collective-permute-start | bytes 786440 | tf_op jit(solution)/shard_map/ppermute | solution.py:454
  84.7 6.0 %collective-permute-start.39 = (bf16[64,512]{1,0:T(8,128)(2,1)S(1)}, bf16[64,512]{1,0:T(8,128)(2,1)S(1)}, u32[]{:S(2)}, u32[]{:S(2)}) collective-permute-start(bf16[64,512]{1,0:T(8,128)(2,1)S(1)} %get-tuple-element.84), channel_id=1, source_target_pairs={{0,16},{16,0},{1,17},{17,1},{2,18},{18,2},{3,19},{19,3},{4,20},{20... | collective-permute-start | bytes 196616 | tf_op jit(solution)/shard_map/ppermute | solution.py:454
  91.7 1.4 %collective-permute-done.39 = bf16[64,512]{1,0:T(8,128)(2,1)S(1)} collective-permute-done((bf16[64,512]{1,0:T(8,128)(2,1)S(1)}, bf16[64,512]{1,0:T(8,128)(2,1)S(1)}, u32[]{:S(2)}, u32[]{:S(2)}) %collective-permute-start.39) | collective-permute-done | bytes 65568 | tf_op jit(solution)/shard_map/ppermute | solution.py:454
  93.1 2.3 %collective-permute-start.41 = (bf16[64,512]{1,0:T(8,128)(2,1)S(1)}, bf16[64,512]{1,0:T(8,128)(2,1)S(1)}, u32[]{:S(2)}, u32[]{:S(2)}) collective-permute-start(bf16[64,512]{1,0:T(8,128)(2,1)S(1)} %get-tuple-element.88), channel_id=1, source_target_pairs={{0,16},{16,0},{1,17},{17,1},{2,18},{18,2},{3,19},{19,3},{4,20},{20... | collective-permute-start | bytes 196616 | tf_op jit(solution)/shard_map/ppermute | solution.py:454
  95.4 1.4 %collective-permute-start.45 = (bf16[64,512]{1,0:T(8,128)(2,1)S(1)}, bf16[64,512]{1,0:T(8,128)(2,1)S(1)}, u32[]{:S(2)}, u32[]{:S(2)}) collective-permute-start(bf16[64,512]{1,0:T(8,128)(2,1)S(1)} %broadcast_select_fusion), channel_id=1, source_target_pairs={{0,12},{2,14},{4,8},{6,10},{8,4},{10,6},{12,0},{14,2},{1,13},{3,15... | collective-permute-start | bytes 196616 | tf_op jit(solution)/shard_map/ppermute | solution.py:412
  98.1 2.8 %collective-permute-start.42 = (bf16[64,512]{1,0:T(8,128)(2,1)S(1)}, bf16[64,512]{1,0:T(8,128)(2,1)S(1)}, u32[]{:S(2)}, u32[]{:S(2)}) collective-permute-start(bf16[64,512]{1,0:T(8,128)(2,1)S(1)} %broadcast_select_fusion.1), channel_id=1, source_target_pairs={{0,4},{2,6},{4,0},{6,2},{8,12},{10,14},{12,8},{14,10},{1,5},{3,7},... | collective-permute-start | bytes 196616 | tf_op jit(solution)/shard_map/ppermute | solution.py:412
  101.6 1.4 %collective-permute-done.43.refs_2_ = bf16[64,512]{1,0:T(8,128)(2,1)S(1)} collective-permute-done((bf16[64,512]{1,0:T(8,128)(2,1)S(1)}, bf16[64,512]{1,0:T(8,128)(2,1)S(1)}, u32[]{:S(2)}, u32[]{:S(2)}) %collective-permute-start.43) | collective-permute-done | bytes 65568 | tf_op jit(solution)/shard_map/ppermute | solution.py:412
  (96 shorter events, 29.0 us)
Async XLA Ops:
  4.8 7.9 %collective-permute-start.1 = (bf16[64,512]{1,0:T(8,128)(2,1)S(1)}, bf16[64,512]{1,0:T(8,128)(2,1)S(1)}, u32[]{:S(2)}, u32[]{:S(2)}) collective-permute-start(bf16[64,512]{1,0:T(8,128)(2,1)S(1)} %get-tuple-element.50), channel_id=1, source_target_pairs={{0,8},{2,10},{4,12},{6,14},{8,0},{10,2},{12,4},{14,6},{1,9},{3,11}... | collective-permute-start | bytes 196616 | tf_op jit(solution)/shard_map/ppermute | solution.py:412
  8.8 6.6 %collective-permute-start.2 = (bf16[64,512]{1,0:T(8,128)(2,1)S(1)}, bf16[64,512]{1,0:T(8,128)(2,1)S(1)}, u32[]{:S(2)}, u32[]{:S(2)}) collective-permute-start(bf16[64,512]{1,0:T(8,128)(2,1)S(1)} %get-tuple-element.51), channel_id=1, source_target_pairs={{0,12},{2,14},{4,8},{6,10},{8,4},{10,6},{12,0},{14,2},{1,13},{3,15... | collective-permute-start | bytes 196616 | tf_op jit(solution)/shard_map/ppermute | solution.py:412
  10.2 6.5 %collective-permute-start.3 = (bf16[64,512]{1,0:T(8,128)(2,1)S(1)}, bf16[64,512]{1,0:T(8,128)(2,1)S(1)}, u32[]{:S(2)}, u32[]{:S(2)}) collective-permute-start(bf16[64,512]{1,0:T(8,128)(2,1)S(1)} %get-tuple-element.52), channel_id=1, source_target_pairs={{0,4},{2,6},{4,0},{6,2},{8,12},{10,14},{12,8},{14,10},{1,5},{3,7},... | collective-permute-start | bytes 196616 | tf_op jit(solution)/shard_map/ppermute | solution.py:412
  10.4 8.5 %collective-permute-start.4 = (bf16[64,512]{1,0:T(8,128)(2,1)S(1)}, bf16[64,512]{1,0:T(8,128)(2,1)S(1)}, u32[]{:S(2)}, u32[]{:S(2)}) collective-permute-start(bf16[64,512]{1,0:T(8,128)(2,1)S(1)} %get-tuple-element.49.refs_0_), channel_id=1, source_target_pairs={{0,2},{2,0},{4,6},{6,4},{8,10},{10,8},{12,14},{14,12},{1,3},{3,1},... | collective-permute-start | bytes 196616 | tf_op jit(solution)/shard_map/ppermute | solution.py:412
  12.7 6.2 %collective-permute-start.5 = (bf16[64,512]{1,0:T(8,128)(2,1)S(1)}, bf16[64,512]{1,0:T(8,128)(2,1)S(1)}, u32[]{:S(2)}, u32[]{:S(2)}) collective-permute-start(bf16[64,512]{1,0:T(8,128)(2,1)S(1)} %collective-permute-done.1.refs_2_.refs_1_), channel_id=1, source_target_pairs={{0,2},{2,0},{4,6},{6,4},{8,10},{10,8},{12,14},{14,12},{1,3},{3,1},... | collective-permute-start | bytes 196616 | tf_op jit(solution)/shard_map/ppermute | solution.py:412
  24.2 7.8 %collective-permute-start.8 = (bf16[64,512]{1,0:T(8,128)(2,1)S(1)}, bf16[64,512]{1,0:T(8,128)(2,1)S(1)}, u32[]{:S(2)}, u32[]{:S(2)}) collective-permute-start(bf16[64,512]{1,0:T(8,128)(2,1)S(1)} %get-tuple-element.55), channel_id=1, source_target_pairs={{0,24},{2,26},{4,28},{6,30},{8,16},{10,18},{12,20},{14,22},{16,8},... | collective-permute-start | bytes 196616 | tf_op jit(solution)/shard_map/ppermute | solution.py:422
  24.3 7.7 %collective-permute-start.9 = (bf16[64,512]{1,0:T(8,128)(2,1)S(1)}, bf16[64,512]{1,0:T(8,128)(2,1)S(1)}, u32[]{:S(2)}, u32[]{:S(2)}) collective-permute-start(bf16[64,512]{1,0:T(8,128)(2,1)S(1)} %get-tuple-element.56), channel_id=1, source_target_pairs={{0,28},{2,30},{4,24},{6,26},{8,20},{10,22},{12,16},{14,18},{16,12}... | collective-permute-start | bytes 196616 | tf_op jit(solution)/shard_map/ppermute | solution.py:422
  28.5 4.8 %collective-permute-start.10 = (bf16[64,512]{1,0:T(8,128)(2,1)S(1)}, bf16[64,512]{1,0:T(8,128)(2,1)S(1)}, u32[]{:S(2)}, u32[]{:S(2)}) collective-permute-start(bf16[64,512]{1,0:T(8,128)(2,1)S(1)} %get-tuple-element.57), channel_id=1, source_target_pairs={{0,16},{2,18},{4,20},{6,22},{8,24},{10,26},{12,28},{14,30},{16,0},... | collective-permute-start | bytes 196616 | tf_op jit(solution)/shard_map/ppermute | solution.py:422
  29.7 5.2 %collective-permute-start.11 = (bf16[64,512]{1,0:T(8,128)(2,1)S(1)}, bf16[64,512]{1,0:T(8,128)(2,1)S(1)}, u32[]{:S(2)}, u32[]{:S(2)}) collective-permute-start(bf16[64,512]{1,0:T(8,128)(2,1)S(1)} %get-tuple-element.58), channel_id=1, source_target_pairs={{0,20},{2,22},{4,16},{6,18},{8,28},{10,30},{12,24},{14,26},{16,4},... | collective-permute-start | bytes 196616 | tf_op jit(solution)/shard_map/ppermute | solution.py:422
  38.5 8.0 %collective-permute-start.16 = (bf16[64,512]{1,0:T(8,128)(2,1)S(1)}, bf16[64,512]{1,0:T(8,128)(2,1)S(1)}, u32[]{:S(2)}, u32[]{:S(2)}) collective-permute-start(bf16[64,512]{1,0:T(8,128)(2,1)S(1)} %get-tuple-element.60), channel_id=1, source_target_pairs={{0,8},{2,10},{4,12},{6,14},{8,0},{10,2},{12,4},{14,6},{1,9},{3,11}... | collective-permute-start | bytes 196616 | tf_op jit(solution)/shard_map/ppermute | solution.py:412
  41.3 6.5 %collective-permute-start.17 = (bf16[64,512]{1,0:T(8,128)(2,1)S(1)}, bf16[64,512]{1,0:T(8,128)(2,1)S(1)}, u32[]{:S(2)}, u32[]{:S(2)}) collective-permute-start(bf16[64,512]{1,0:T(8,128)(2,1)S(1)} %get-tuple-element.61), channel_id=1, source_target_pairs={{0,12},{2,14},{4,8},{6,10},{8,4},{10,6},{12,0},{14,2},{1,13},{3,15... | collective-permute-start | bytes 196616 | tf_op jit(solution)/shard_map/ppermute | solution.py:412
  41.9 6.7 %collective-permute-start.18 = (bf16[64,512]{1,0:T(8,128)(2,1)S(1)}, bf16[64,512]{1,0:T(8,128)(2,1)S(1)}, u32[]{:S(2)}, u32[]{:S(2)}) collective-permute-start(bf16[64,512]{1,0:T(8,128)(2,1)S(1)} %get-tuple-element.62), channel_id=1, source_target_pairs={{0,4},{2,6},{4,0},{6,2},{8,12},{10,14},{12,8},{14,10},{1,5},{3,7},... | collective-permute-start | bytes 196616 | tf_op jit(solution)/shard_map/ppermute | solution.py:412
  42.4 8.9 %collective-permute-start.19 = (bf16[64,512]{1,0:T(8,128)(2,1)S(1)}, bf16[64,512]{1,0:T(8,128)(2,1)S(1)}, u32[]{:S(2)}, u32[]{:S(2)}) collective-permute-start(bf16[64,512]{1,0:T(8,128)(2,1)S(1)} %get-tuple-element.59.refs_0_), channel_id=1, source_target_pairs={{0,2},{2,0},{4,6},{6,4},{8,10},{10,8},{12,14},{14,12},{1,3},{3,1},... | collective-permute-start | bytes 196616 | tf_op jit(solution)/shard_map/ppermute | solution.py:412
  46.6 4.7 %collective-permute-start.20 = (bf16[64,512]{1,0:T(8,128)(2,1)S(1)}, bf16[64,512]{1,0:T(8,128)(2,1)S(1)}, u32[]{:S(2)}, u32[]{:S(2)}) collective-permute-start(bf16[64,512]{1,0:T(8,128)(2,1)S(1)} %collective-permute-done.16.refs_2_.refs_1_), channel_id=1, source_target_pairs={{0,2},{2,0},{4,6},{6,4},{8,10},{10,8},{12,14},{14,12},{1,3},{3,1},... | collective-permute-start | bytes 196616 | tf_op jit(solution)/shard_map/ppermute | solution.py:412
  56.1 6.8 %collective-permute-start.23 = (bf16[64,512]{1,0:T(8,128)(2,1)S(1)}, bf16[64,512]{1,0:T(8,128)(2,1)S(1)}, u32[]{:S(2)}, u32[]{:S(2)}) collective-permute-start(bf16[64,512]{1,0:T(8,128)(2,1)S(1)} %get-tuple-element.65), channel_id=1, source_target_pairs={{0,24},{2,26},{4,28},{6,30},{8,16},{10,18},{12,20},{14,22},{16,8},... | collective-permute-start | bytes 196616 | tf_op jit(solution)/shard_map/ppermute | solution.py:422
  60.4 5.2 %collective-permute-start.26 = (bf16[64,512]{1,0:T(8,128)(2,1)S(1)}, bf16[64,512]{1,0:T(8,128)(2,1)S(1)}, u32[]{:S(2)}, u32[]{:S(2)}) collective-permute-start(bf16[64,512]{1,0:T(8,128)(2,1)S(1)} %get-tuple-element.68), channel_id=1, source_target_pairs={{0,20},{2,22},{4,16},{6,18},{8,28},{10,30},{12,24},{14,26},{16,4},... | collective-permute-start | bytes 196616 | tf_op jit(solution)/shard_map/ppermute | solution.py:422
  62.1 7.0 %collective-permute-start.24 = (bf16[64,512]{1,0:T(8,128)(2,1)S(1)}, bf16[64,512]{1,0:T(8,128)(2,1)S(1)}, u32[]{:S(2)}, u32[]{:S(2)}) collective-permute-start(bf16[64,512]{1,0:T(8,128)(2,1)S(1)} %get-tuple-element.66), channel_id=1, source_target_pairs={{0,28},{2,30},{4,24},{6,26},{8,20},{10,22},{12,16},{14,18},{16,12}... | collective-permute-start | bytes 196616 | tf_op jit(solution)/shard_map/ppermute | solution.py:422
  62.9 6.2 %collective-permute-start.27 = (bf16[64,512]{1,0:T(8,128)(2,1)S(1)}, bf16[64,512]{1,0:T(8,128)(2,1)S(1)}, u32[]{:S(2)}, u32[]{:S(2)}) collective-permute-start(bf16[64,512]{1,0:T(8,128)(2,1)S(1)} %collective-permute-done.23.refs_0_), channel_id=1, source_target_pairs={{0,1},{1,0},{2,3},{3,2},{4,5},{5,4},{6,7},{7,6},{8,9},{9,8},{10,11... | collective-permute-start | bytes 196616 | tf_op jit(solution)/shard_map/ppermute | solution.py:412
  63.8 6.6 %collective-permute-start.29 = (bf16[64,512]{1,0:T(8,128)(2,1)S(1)}, bf16[64,512]{1,0:T(8,128)(2,1)S(1)}, u32[]{:S(2)}, u32[]{:S(2)}) collective-permute-start(bf16[64,512]{1,0:T(8,128)(2,1)S(1)} %collective-permute-done.25.refs_2_), channel_id=1, source_target_pairs={{0,1},{1,0},{2,3},{3,2},{4,5},{5,4},{6,7},{7,6},{8,9},{9,8},{10,11... | collective-permute-start | bytes 196616 | tf_op jit(solution)/shard_map/ppermute | solution.py:412
  65.6 4.8 %collective-permute-start.30 = (bf16[64,512]{1,0:T(8,128)(2,1)S(1)}, bf16[64,512]{1,0:T(8,128)(2,1)S(1)}, u32[]{:S(2)}, u32[]{:S(2)}) collective-permute-start(bf16[64,512]{1,0:T(8,128)(2,1)S(1)} %collective-permute-done.26.refs_3_), channel_id=1, source_target_pairs={{0,1},{1,0},{2,3},{3,2},{4,5},{5,4},{6,7},{7,6},{8,9},{9,8},{10,11... | collective-permute-start | bytes 196616 | tf_op jit(solution)/shard_map/ppermute | solution.py:412
  70.4 8.0 %collective-permute-start.31 = (bf16[64,512]{1,0:T(8,128)(2,1)S(1)}, bf16[64,512]{1,0:T(8,128)(2,1)S(1)}, u32[]{:S(2)}, u32[]{:S(2)}) collective-permute-start(bf16[64,512]{1,0:T(8,128)(2,1)S(1)} %get-tuple-element.70), channel_id=1, source_target_pairs={{0,8},{2,10},{4,12},{6,14},{8,0},{10,2},{12,4},{14,6},{1,9},{3,11}... | collective-permute-start | bytes 196616 | tf_op jit(solution)/shard_map/ppermute | solution.py:412
  70.4 9.0 %collective-permute-start.32 = (bf16[64,512]{1,0:T(8,128)(2,1)S(1)}, bf16[64,512]{1,0:T(8,128)(2,1)S(1)}, u32[]{:S(2)}, u32[]{:S(2)}) collective-permute-start(bf16[64,512]{1,0:T(8,128)(2,1)S(1)} %get-tuple-element.71), channel_id=1, source_target_pairs={{0,12},{2,14},{4,8},{6,10},{8,4},{10,6},{12,0},{14,2},{1,13},{3,15... | collective-permute-start | bytes 196616 | tf_op jit(solution)/shard_map/ppermute | solution.py:412
  71.5 8.8 %collective-permute-start.33 = (bf16[64,512]{1,0:T(8,128)(2,1)S(1)}, bf16[64,512]{1,0:T(8,128)(2,1)S(1)}, u32[]{:S(2)}, u32[]{:S(2)}) collective-permute-start(bf16[64,512]{1,0:T(8,128)(2,1)S(1)} %get-tuple-element.72), channel_id=1, source_target_pairs={{0,4},{2,6},{4,0},{6,2},{8,12},{10,14},{12,8},{14,10},{1,5},{3,7},... | collective-permute-start | bytes 196616 | tf_op jit(solution)/shard_map/ppermute | solution.py:412
  73.9 10.8 %collective-permute-start.38 = (bf16[256,512]{1,0:T(8,128)(2,1)S(1)}, bf16[256,512]{1,0:T(8,128)(2,1)S(1)}, u32[]{:S(2)}, u32[]{:S(2)}) collective-permute-start(bf16[256,512]{1,0:T(8,128)(2,1)S(1)} %constant_dynamic-update-slice_fusion.refs_0_), channel_id=1, source_target_pairs={{0,16},{16,0},{1,17},{17,1},{2,18},{18,2},{3,19},{19,3},{4,20},{20... | collective-permute-start | bytes 786440 | tf_op jit(solution)/shard_map/ppermute | solution.py:454
  77.4 4.9 %collective-permute-start.34 = (bf16[64,512]{1,0:T(8,128)(2,1)S(1)}, bf16[64,512]{1,0:T(8,128)(2,1)S(1)}, u32[]{:S(2)}, u32[]{:S(2)}) collective-permute-start(bf16[64,512]{1,0:T(8,128)(2,1)S(1)} %get-tuple-element.73.refs_0_), channel_id=1, source_target_pairs={{0,2},{2,0},{4,6},{6,4},{8,10},{10,8},{12,14},{14,12},{1,3},{3,1},... | collective-permute-start | bytes 196616 | tf_op jit(solution)/shard_map/ppermute | solution.py:412
  78.4 4.9 %collective-permute-start.35 = (bf16[64,512]{1,0:T(8,128)(2,1)S(1)}, bf16[64,512]{1,0:T(8,128)(2,1)S(1)}, u32[]{:S(2)}, u32[]{:S(2)}) collective-permute-start(bf16[64,512]{1,0:T(8,128)(2,1)S(1)} %collective-permute-done.31.refs_2_.refs_1_), channel_id=1, source_target_pairs={{0,2},{2,0},{4,6},{6,4},{8,10},{10,8},{12,14},{14,12},{1,3},{3,1},... | collective-permute-start | bytes 196616 | tf_op jit(solution)/shard_map/ppermute | solution.py:412
  84.7 8.4 %collective-permute-start.39 = (bf16[64,512]{1,0:T(8,128)(2,1)S(1)}, bf16[64,512]{1,0:T(8,128)(2,1)S(1)}, u32[]{:S(2)}, u32[]{:S(2)}) collective-permute-start(bf16[64,512]{1,0:T(8,128)(2,1)S(1)} %get-tuple-element.84), channel_id=1, source_target_pairs={{0,16},{16,0},{1,17},{17,1},{2,18},{18,2},{3,19},{19,3},{4,20},{20... | collective-permute-start | bytes 196616 | tf_op jit(solution)/shard_map/ppermute | solution.py:454
  90.6 4.8 %collective-permute-start.44 = (bf16[64,512]{1,0:T(8,128)(2,1)S(1)}, bf16[64,512]{1,0:T(8,128)(2,1)S(1)}, u32[]{:S(2)}, u32[]{:S(2)}) collective-permute-start(bf16[64,512]{1,0:T(8,128)(2,1)S(1)} %get-tuple-element.90), channel_id=1, source_target_pairs={{0,16},{16,0},{1,17},{17,1},{2,18},{18,2},{3,19},{19,3},{4,20},{20... | collective-permute-start | bytes 196616 | tf_op jit(solution)/shard_map/ppermute | solution.py:454
  93.1 5.0 %collective-permute-start.41 = (bf16[64,512]{1,0:T(8,128)(2,1)S(1)}, bf16[64,512]{1,0:T(8,128)(2,1)S(1)}, u32[]{:S(2)}, u32[]{:S(2)}) collective-permute-start(bf16[64,512]{1,0:T(8,128)(2,1)S(1)} %get-tuple-element.88), channel_id=1, source_target_pairs={{0,16},{16,0},{1,17},{17,1},{2,18},{18,2},{3,19},{19,3},{4,20},{20... | collective-permute-start | bytes 196616 | tf_op jit(solution)/shard_map/ppermute | solution.py:454
  95.4 6.2 %collective-permute-start.45 = (bf16[64,512]{1,0:T(8,128)(2,1)S(1)}, bf16[64,512]{1,0:T(8,128)(2,1)S(1)}, u32[]{:S(2)}, u32[]{:S(2)}) collective-permute-start(bf16[64,512]{1,0:T(8,128)(2,1)S(1)} %broadcast_select_fusion), channel_id=1, source_target_pairs={{0,12},{2,14},{4,8},{6,10},{8,4},{10,6},{12,0},{14,2},{1,13},{3,15... | collective-permute-start | bytes 196616 | tf_op jit(solution)/shard_map/ppermute | solution.py:412
  96.8 6.2 %collective-permute-start.43 = (bf16[64,512]{1,0:T(8,128)(2,1)S(1)}, bf16[64,512]{1,0:T(8,128)(2,1)S(1)}, u32[]{:S(2)}, u32[]{:S(2)}) collective-permute-start(bf16[64,512]{1,0:T(8,128)(2,1)S(1)} %broadcast_select_fusion.3), channel_id=1, source_target_pairs={{0,8},{2,10},{4,12},{6,14},{8,0},{10,2},{12,4},{14,6},{1,9},{3,11}... | collective-permute-start | bytes 196616 | tf_op jit(solution)/shard_map/ppermute | solution.py:412
  98.1 5.6 %collective-permute-start.42 = (bf16[64,512]{1,0:T(8,128)(2,1)S(1)}, bf16[64,512]{1,0:T(8,128)(2,1)S(1)}, u32[]{:S(2)}, u32[]{:S(2)}) collective-permute-start(bf16[64,512]{1,0:T(8,128)(2,1)S(1)} %broadcast_select_fusion.1), channel_id=1, source_target_pairs={{0,4},{2,6},{4,0},{6,2},{8,12},{10,14},{12,8},{14,10},{1,5},{3,7},... | collective-permute-start | bytes 196616 | tf_op jit(solution)/shard_map/ppermute | solution.py:412
  (22 other events, 94.5 us)
